TPU v7x, 128 devices: a whole 4x4x4 slice. The times are simulated.
128 devices in a mesh: dp: 16 (over x, z_lo, core), tensor: 8 (over y, z_hi).
Axes of the slice: x: 4, y: 4, z: 4 (z_hi: 2, z_lo: 2; z = z_hi * 2 + z_lo), core: 2. Of those that a mesh axis runs over, the one named last changes fastest.
Arguments:
- tokens: bfloat16 [8192, 1024], P('dp'), may hold values from -6 to 6
- cotangent: bfloat16 [8192, 1024], P('dp'), may hold values from -6 to 6
- ln_gain: float32 [2, 2, 1024], replicated, may hold values from 0.5 to 1.5
- ln_bias: float32 [2, 2, 1024], replicated, may hold values from -2 to 2
- w_qkv: bfloat16 [2, 1024, 3, 1024], P(None, None, None, 'tensor'), may hold values from -0.1875 to 0.1875
- b_qkv: float32 [2, 3, 1024], P(None, None, 'tensor'), may hold values from -3 to 3
- w_out: bfloat16 [2, 1024, 1024], P(None, 'tensor'), may hold values from -1.5 to 1.5
- b_out: float32 [2, 1024], replicated, may hold values from -3 to 3
- w_in: bfloat16 [2, 1024, 4096], P(None, None, 'tensor'), may hold values from -0.1875 to 0.1875
- b_in: float32 [2, 4096], P(None, 'tensor'), may hold values from -3 to 3
- w_down: bfloat16 [2, 4096, 1024], P(None, 'tensor'), may hold values from -0.09375 to 0.09375
- b_down: float32 [2, 1024], replicated, may hold values from -3 to 3
Outputs:
- output: float32 [8192, 1024], P('dp')
- input_grad: float32 [8192, 1024], P('dp')
- grad_ln_gain: float32 [2, 2, 1024], replicated
- grad_ln_bias: float32 [2, 2, 1024], replicated
- grad_w_qkv: float32 [2, 1024, 3, 1024], P(None, 'dp', None, 'tensor')
- grad_b_qkv: float32 [2, 3, 1024], P(None, None, 'tensor')
- grad_w_out: float32 [2, 1024, 1024], P(None, 'tensor', 'dp')
- grad_b_out: float32 [2, 1024], replicated
- grad_w_in: float32 [2, 1024, 4096], P(None, 'dp', 'tensor')
- grad_b_in: float32 [2, 4096], P(None, 'tensor')
- grad_w_down: float32 [2, 4096, 1024], P(None, 'tensor', 'dp')
- grad_b_down: float32 [2, 1024], replicated
All inputs are finite; a program needn't handle non-finite values.
Results may differ from a plain program's by a relative error of at most 0.015.
The roundings to bfloat16 on the way count: a program that leaves them out, or rounds other values in their place, can miss the bound.
Values may be sent and summed in bfloat16 or wider, within the bound.
A program may use at most 128 MiB of HBM per device.

v0:
```python
import jax
import jax.numpy as jnp
from jax import lax
from jax.sharding import PartitionSpec as P

HEAD_DIM = 64
ROT = 16
SEQ = 2048
LAYERS = 2


def passed_along(block, axis, distance):
    devices = range(lax.axis_size(axis))
    route = [(i - distance, i) for i in devices if i - distance in devices]
    return lax.ppermute(block, axis, route)


def layer_norms(stream, gains, biases):
    center = stream - jnp.mean(stream, axis=-1, keepdims=True)
    spread = jnp.mean(center * center, axis=-1, keepdims=True)
    normed = center * lax.rsqrt(spread + 1e-05)
    return normed[None] * gains[:, None, :] + biases[:, None, :]


def rope_tables(positions):
    exponent = jnp.arange(0, ROT, 2).astype(jnp.float32) / ROT
    inverse = 1.0 / 10000.0**exponent
    angles = positions[:, None] * inverse[None, :]
    return (jnp.cos(angles), jnp.sin(angles))


def rotate(values, cosine, sine):
    halfway = cosine.shape[-1]
    leading = values[..., :halfway]
    trailing = values[..., halfway : 2 * halfway]
    cos_part = cosine[:, None, :]
    sin_part = sine[:, None, :]
    return jnp.concatenate(
        [
            leading * cos_part - trailing * sin_part,
            trailing * cos_part + leading * sin_part,
            values[..., 2 * halfway :],
        ],
        axis=-1,
    )


def scores_for(queries, keys, query_pos, key_pos):
    raw = jnp.einsum("thd,shd->hts", queries, keys, preferred_element_type=jnp.float32) * 0.125
    allowed = jnp.logical_and(key_pos[None, :] <= query_pos[:, None], key_pos[None, :] >= 0)
    return jnp.where(allowed[None], raw, -1e30)


def gelu_exact(values):
    return jax.nn.gelu(values, approximate=False)


def on_device(
    tokens, cotangent, ln_gain, ln_bias, w_qkv, b_qkv, w_out, b_out, w_in, b_in, w_down, b_down
):
    row_count = tokens.shape[0]
    width = w_qkv.shape[-1]
    heads_here = width // HEAD_DIM
    group = SEQ // row_count
    local_rank = lax.axis_index("dp") % group
    row_ids = jnp.arange(row_count)
    query_pos = local_rank * row_count + row_ids
    cosine, sine = rope_tables(query_pos.astype(jnp.float32))
    stream = tokens.astype(jnp.float32)
    saved = []
    for layer_index in range(LAYERS):
        normed_r = layer_norms(stream, ln_gain[layer_index], ln_bias[layer_index]).astype(
            jnp.bfloat16
        )
        mixed = (
            jnp.einsum(
                "td,dcf->tcf", normed_r[0], w_qkv[layer_index], preferred_element_type=jnp.float32
            )
            + b_qkv[layer_index][None]
        )
        query_r = rotate(mixed[:, 0].reshape(row_count, heads_here, HEAD_DIM), cosine, sine).astype(
            jnp.bfloat16
        )
        key_r = rotate(mixed[:, 1].reshape(row_count, heads_here, HEAD_DIM), cosine, sine).astype(
            jnp.bfloat16
        )
        value_r = mixed[:, 2].reshape(row_count, heads_here, HEAD_DIM).astype(jnp.bfloat16)
        key_pieces = [key_r]
        value_pieces = [value_r]
        pos_pieces = [query_pos]
        for shift_by in range(1, group):
            key_in, value_in = passed_along((key_r, value_r), "dp", shift_by)
            key_pieces.append(key_in)
            value_pieces.append(value_in)
            pos_pieces.append((local_rank - shift_by) * row_count + row_ids)
        key_all = jnp.concatenate(key_pieces, axis=0)
        value_all = jnp.concatenate(value_pieces, axis=0)
        key_pos = jnp.concatenate(pos_pieces, axis=0)
        scores = scores_for(query_r, key_all, query_pos, key_pos)
        top = jnp.max(scores, axis=-1, keepdims=True)
        expo = jnp.exp(scores - top)
        total = jnp.sum(expo, axis=-1, keepdims=True)
        probs_r = (expo / total).astype(jnp.bfloat16)
        attended = jnp.einsum(
            "hts,shd->thd", probs_r, value_all, preferred_element_type=jnp.float32
        )
        attended_r = attended.reshape(row_count, width).astype(jnp.bfloat16)
        hidden = (
            jnp.dot(normed_r[1], w_in[layer_index], preferred_element_type=jnp.float32)
            + b_in[layer_index]
        )
        active_r = gelu_exact(hidden).astype(jnp.bfloat16)
        branch = jnp.dot(attended_r, w_out[layer_index], preferred_element_type=jnp.float32)
        branch = branch + jnp.dot(active_r, w_down[layer_index], preferred_element_type=jnp.float32)
        summed = lax.psum(branch, "tensor")
        saved.append(
            (
                stream,
                normed_r,
                query_r,
                key_r,
                value_r,
                key_all,
                value_all,
                key_pos,
                top,
                total,
                attended_r,
                hidden,
                active_r,
            )
        )
        stream = stream + (summed + b_out[layer_index] + b_down[layer_index])
    gradient = cotangent.astype(jnp.float32)
    results = [None] * LAYERS
    for layer_index in reversed(range(LAYERS)):
        (
            stream_in,
            normed_r,
            query_r,
            key_r,
            value_r,
            key_all,
            value_all,
            key_pos,
            top,
            total,
            attended_r,
            hidden,
            active_r,
        ) = saved[layer_index]
        branch_grad = gradient.astype(jnp.bfloat16)
        grad_bias_res = jnp.sum(branch_grad, axis=0, dtype=jnp.float32)
        grad_wout = jnp.einsum(
            "tf,td->fd", attended_r, branch_grad, preferred_element_type=jnp.float32
        )
        grad_wdown = jnp.einsum(
            "tf,td->fd", active_r, branch_grad, preferred_element_type=jnp.float32
        )
        grad_active = jnp.einsum(
            "td,fd->tf", branch_grad, w_down[layer_index], preferred_element_type=jnp.float32
        )
        gelu_value, gelu_pull = jax.vjp(gelu_exact, hidden)
        grad_hidden_r = gelu_pull(grad_active)[0].astype(jnp.bfloat16)
        grad_win = jnp.einsum(
            "td,tf->df", normed_r[1], grad_hidden_r, preferred_element_type=jnp.float32
        )
        grad_bin = jnp.sum(grad_hidden_r, axis=0, dtype=jnp.float32)
        grad_norm_ff = jnp.einsum(
            "tf,df->td", grad_hidden_r, w_in[layer_index], preferred_element_type=jnp.float32
        )
        grad_attn_r = jnp.einsum(
            "td,fd->tf", branch_grad, w_out[layer_index], preferred_element_type=jnp.float32
        )
        grad_attn_r = grad_attn_r.astype(jnp.bfloat16).reshape(row_count, heads_here, HEAD_DIM)
        scores = scores_for(query_r, key_all, query_pos, key_pos)
        probs = jnp.exp(scores - top) / total
        probs_r = probs.astype(jnp.bfloat16)
        grad_probs = jnp.einsum(
            "thd,shd->hts", grad_attn_r, value_all, preferred_element_type=jnp.float32
        )
        delta = jnp.sum(probs * grad_probs, axis=-1, keepdims=True)
        grad_scores_r = (probs * (grad_probs - delta)).astype(jnp.bfloat16)
        grad_query = (
            jnp.einsum("hts,shd->thd", grad_scores_r, key_all, preferred_element_type=jnp.float32)
            * 0.125
        )
        key_terms = (
            jnp.einsum("hts,thd->shd", grad_scores_r, query_r, preferred_element_type=jnp.float32)
            * 0.125
        )
        value_terms = jnp.einsum(
            "hts,thd->shd", probs_r, grad_attn_r, preferred_element_type=jnp.float32
        )
        grad_key = key_terms[:row_count]
        grad_value = value_terms[:row_count]
        for shift_by in range(1, group):
            lower = shift_by * row_count
            key_back, value_back = passed_along(
                (key_terms[lower : lower + row_count], value_terms[lower : lower + row_count]),
                "dp",
                -shift_by,
            )
            grad_key = grad_key + key_back
            grad_value = grad_value + value_back
        grad_query_lin = rotate(grad_query, cosine, -sine).reshape(row_count, width)
        grad_key_lin = rotate(grad_key, cosine, -sine).reshape(row_count, width)
        grad_mixed_r = jnp.stack(
            [grad_query_lin, grad_key_lin, grad_value.reshape(row_count, width)], axis=1
        ).astype(jnp.bfloat16)
        grad_wqkv = jnp.einsum(
            "td,tcf->dcf", normed_r[0], grad_mixed_r, preferred_element_type=jnp.float32
        )
        grad_bqkv = jnp.sum(grad_mixed_r, axis=0, dtype=jnp.float32)
        grad_norm_attn = jnp.einsum(
            "tcf,dcf->td", grad_mixed_r, w_qkv[layer_index], preferred_element_type=jnp.float32
        )
        norm_value, norm_pull = jax.vjp(
            layer_norms, stream_in, ln_gain[layer_index], ln_bias[layer_index]
        )
        stream_part, gain_part, bias_part = norm_pull(jnp.stack([grad_norm_attn, grad_norm_ff]))
        stream_sum, gain_sum, bias_sum = lax.psum((stream_part, gain_part, bias_part), "tensor")
        gradient = gradient + stream_sum
        shard_wqkv, shard_wout, shard_win, shard_wdown = (
            lax.psum_scatter(grad_wqkv, "dp", scatter_dimension=0, tiled=True),
            lax.psum_scatter(grad_wout, "dp", scatter_dimension=1, tiled=True),
            lax.psum_scatter(grad_win, "dp", scatter_dimension=0, tiled=True),
            lax.psum_scatter(grad_wdown, "dp", scatter_dimension=1, tiled=True),
        )
        results[layer_index] = (
            gain_sum,
            bias_sum,
            shard_wqkv,
            grad_bqkv,
            shard_wout,
            grad_bias_res,
            shard_win,
            grad_bin,
            shard_wdown,
        )
    gain_stack = jnp.stack([entry[0] for entry in results])
    bias_stack = jnp.stack([entry[1] for entry in results])
    bqkv_stack = jnp.stack([entry[3] for entry in results])
    resid_stack = jnp.stack([entry[5] for entry in results])
    bin_stack = jnp.stack([entry[7] for entry in results])
    gain_stack, bias_stack, bqkv_stack, resid_stack, bin_stack = lax.psum(
        (gain_stack, bias_stack, bqkv_stack, resid_stack, bin_stack), "dp"
    )
    wqkv_stack = jnp.stack([entry[2] for entry in results])
    wout_stack = jnp.stack([entry[4] for entry in results])
    win_stack = jnp.stack([entry[6] for entry in results])
    wdown_stack = jnp.stack([entry[8] for entry in results])
    return (
        stream,
        gradient,
        gain_stack,
        bias_stack,
        wqkv_stack,
        bqkv_stack,
        wout_stack,
        resid_stack,
        win_stack,
        bin_stack,
        wdown_stack,
        resid_stack,
    )


def solution(mesh):
    return jax.shard_map(
        on_device,
        mesh=mesh,
        in_specs=(
            P("dp", None),
            P("dp", None),
            P(),
            P(),
            P(None, None, None, "tensor"),
            P(None, None, "tensor"),
            P(None, "tensor", None),
            P(),
            P(None, None, "tensor"),
            P(None, "tensor"),
            P(None, "tensor", None),
            P(),
        ),
        out_specs=(
            P("dp", None),
            P("dp", None),
            P(),
            P(),
            P(None, "dp", None, "tensor"),
            P(None, None, "tensor"),
            P(None, "tensor", "dp"),
            P(),
            P(None, "dp", "tensor"),
            P(None, "tensor"),
            P(None, "tensor", "dp"),
            P(),
        ),
        check_vma=False,
    )
```

profile of v0, /device:TPU:1, one launch (start us, length us, event | category | flops | bytes accessed | tf_op | source)
XLA Modules:
  0.0 1151.5 jit_solution(15973166297064990449)
XLA Ops:
  18.5 4.9 collective-permute-start.3
  23.4 2.7 collective-permute-start.4
  26.1 2.7 collective-permute-start.5
  28.8 3.8 collective-permute-start
  32.7 4.2 collective-permute-start.1
  37.5 5.9 multiply_convert_fusion.3
  45.6 5.1 fusion.143
  50.8 5.1 fusion.30
  64.6 104.1 %all-reduce.7.cloned.1.call-done = f32[512,1024]{1,0:T(8,128)} async-done(((f32[512,1024]{1,0:T(8,128)}), f32[512,1024]{1,0:T(8,128)}) %all-reduce.7.cloned.1.call-update) | async-done | bytes 2097168 | tf_op jit(solution)/shard_map/psum | solution.py:115
  176.5 7.0 collective-permute-start.11
  183.5 2.7 collective-permute-start.9
  186.3 4.1 collective-permute-start.6
  190.4 2.3 collective-permute-start.7
  192.7 3.6 multiply_convert_fusion.2
  200.1 3.6 collective-permute-start.8
  204.4 8.4 fusion.144
  212.7 4.4 convolution_bitcast_fusion.1
  218.9 2.7 multiply_reduce_fusion.1
  224.1 3.2 collective-permute-start.12
  237.5 6.8 collective-permute-done.14
  248.9 8.5 collective-permute-done.17
  262.4 3.4 fusion.15
  268.9 5.2 fusion.33
  276.2 98.0 %all-reduce.9.cloned.1.call-done = f32[512,1024]{1,0:T(8,128)} async-done(((f32[512,1024]{1,0:T(8,128)}), f32[512,1024]{1,0:T(8,128)}) %all-reduce.9.cloned.1.call-update) | async-done | bytes 2097168 | tf_op jit(solution)/shard_map/psum | solution.py:222
  374.3 2.9 convert_reduce_fusion.2
  379.6 3.1 fusion.38
  384.5 4.7 multiply_reduce_fusion
  393.0 4.6 collective-permute-start.18
  408.5 8.1 collective-permute-done.20
  423.6 6.2 collective-permute-done.23
  433.5 3.2 fusion.40
  436.8 3.5 fusion.148
  440.3 3.5 fusion.147
  443.9 3.5 fusion.75
  447.7 3.9 convert_reduce_fusion.4
  456.2 3.5 convolution_add_fusion
  468.9 31.5 %all-reduce.1 = (f32[1,2,1024]{2,1,0:T(2,128)S(1)}, f32[1,2,1024]{2,1,0:T(2,128)S(1)}, f32[1,2,1024]{2,1,0:T(2,128)S(1)}, f32[1,2,1024]{2,1,0:T(2,128)S(1)}) all-reduce(f32[1,2,1024]{2,1,0:T(2,128)S(1)} %bitcast.231, f32[1,2,1024]{2,1,0:T(2,128)} %bitcast.233, ...), channel_id=1, replica_groups=mesh['dp'=16,'tensor'=8] {'tensor'}, use_global_device_ids=true, to_apply=%region_23.24 | all-reduce | flops 8192 | bytes 65536 | tf_op jit(solution)/shard_map/psum | solution.py:222
  502.3 3.4 reduce-scatter.13.cloned.1.call-done
  507.1 61.6 %reduce-scatter.11.cloned.1.call-done = f32[64,3,128]{2,0,1:T(8,128)} async-done(((f32[1024,3,128]{2,0,1:T(8,128)}), f32[64,3,128]{2,0,1:T(8,128)}) %reduce-scatter.11.cloned.1.call-update) | async-done | bytes 98320 | tf_op jit(solution)/shard_map/reduce_scatter | solution.py:225
  568.7 63.6 %reduce-scatter.9.cloned.1.call-done = f32[64,3,128]{2,0,1:T(8,128)} async-done(((f32[1024,3,128]{2,0,1:T(8,128)}), f32[64,3,128]{2,0,1:T(8,128)}) %reduce-scatter.9.cloned.1.call-update) | async-done | bytes 98320 | tf_op jit(solution)/shard_map/reduce_scatter | solution.py:225
  633.9 63.1 %reduce-scatter.23.cloned.1.call-done = f32[512,64]{0,1:T(8,128)} async-done(((f32[512,1024]{0,1:T(8,128)}), f32[512,64]{0,1:T(8,128)}) %reduce-scatter.23.cloned.1.call-update) | async-done | bytes 131088 | tf_op jit(solution)/shard_map/reduce_scatter | solution.py:228
  697.0 64.8 %reduce-scatter.21.cloned.1.call-done = f32[512,64]{0,1:T(8,128)} async-done(((f32[512,1024]{0,1:T(8,128)}), f32[512,64]{0,1:T(8,128)}) %reduce-scatter.21.cloned.1.call-update) | async-done | bytes 131088 | tf_op jit(solution)/shard_map/reduce_scatter | solution.py:228
  763.5 63.2 %reduce-scatter.19.cloned.1.call-done = f32[64,512]{1,0:T(8,128)} async-done(((f32[1024,512]{1,0:T(8,128)}), f32[64,512]{1,0:T(8,128)}) %reduce-scatter.19.cloned.1.call-update) | async-done | bytes 131088 | tf_op jit(solution)/shard_map/reduce_scatter | solution.py:227
  826.7 64.7 %reduce-scatter.17.cloned.1.call-done = f32[64,512]{1,0:T(8,128)} async-done(((f32[1024,512]{1,0:T(8,128)}), f32[64,512]{1,0:T(8,128)}) %reduce-scatter.17.cloned.1.call-update) | async-done | bytes 131088 | tf_op jit(solution)/shard_map/reduce_scatter | solution.py:227
  893.2 190.0 %all-reduce.11.cloned.1.call-done = (f32[512,1024]{1,0:T(8,128)}, f32[512,1024]{1,0:T(8,128)}) async-done(((f32[512,1024]{1,0:T(8,128)}, f32[512,1024]{1,0:T(8,128)}), (f32[512,1024]{1,0:T(8,128)}, f32[512,1024]{1,0:T(8,128)})) %all-reduce.11.cloned.1.call-update) | async-done | bytes 4194320 | tf_op jit(solution)/shard_map/psum | solution.py:115
  1083.2 4.3 convert_reduce_fusion.1
  1087.5 52.2 %all-reduce = (f32[2,2,1024]{2,1,0:T(2,128)}, f32[2,2,1024]{2,1,0:T(2,128)}, f32[2,3,128]{2,1,0:T(4,128)S(1)}, f32[2,1024]{1,0:T(2,128)S(1)}, f32[2,512]{1,0:T(2,128)}) all-reduce(f32[2,2,1024]{2,1,0:T(2,128)S(1)} %pad_maximum_fusion.24, f32[2,2,1024]{2,1,0:T(2,128)S(1)} %pad_maximum_fusion.25, ...), channel_id=1, replica_groups=mesh['dp'=16,'tensor'=8] {'dp'}, use_global_device_ids=true, to_apply=%region_24.25 | all-reduce | flops 12032 | bytes 96256 | tf_op jit(solution)/shard_map/psum | solution.py:246
  1140.3 3.6 add_add_fusion.2
  (388 shorter events, 116.3 us)
Async XLA Ops:
  7.2 161.6 %all-reduce.7.cloned.1.call-start = ((), (), s32[]{:S(2)}) async-start(), calls=%async_computation.8 | async-start | bytes 4194304 | tf_op jit(solution)/shard_map/psum | solution.py:115
  15.7 156.6 %copy-start.50 = (f32[2,1024]{1,0:T(2,128)}, f32[2,1024]{1,0:T(2,128)S(1)}, u32[]{:S(2)}) copy-start(f32[2,1024]{1,0:T(2,128)S(1)} %get-tuple-element.125) | copy-start | bytes 24580
  17.5 19.5 %copy-start.89 = (f32[2,512]{1,0:T(2,128)S(1)}, f32[2,512]{1,0:T(2,128)}, u32[]{:S(2)}) copy-start(f32[2,512]{1,0:T(2,128)} %param.21) | copy-start | bytes 12292
  18.2 27.3 %copy-start.38 = (bf16[512,2,48]{0,2,1:T(8,128)(2,1)}, bf16[512,2,48]{0,2,1:T(8,128)(2,1)S(1)}, u32[]{:S(2)}) copy-start(bf16[512,2,48]{0,2,1:T(8,128)(2,1)S(1)} %slice.510) | copy-start | bytes 294916
  18.4 226.0 %copy-start.42 = (f32[512,8]{0,1:T(8,128)}, f32[512,8]{0,1:T(8,128)S(1)}, u32[]{:S(2)}) copy-start(f32[512,8]{0,1:T(8,128)S(1)} %get-tuple-element.107) | copy-start | bytes 49156
  18.4 27.1 %copy-start.52 = (bf16[512,2,8]{0,2,1:T(8,128)(2,1)}, bf16[512,2,8]{0,2,1:T(8,128)(2,1)S(1)}, u32[]{:S(2)}) copy-start(bf16[512,2,8]{0,2,1:T(8,128)(2,1)S(1)} %get-tuple-element.93) | copy-start | bytes 49156
  18.5 27.1 %copy-start.54 = (bf16[512,2,8]{0,2,1:T(8,128)(2,1)}, bf16[512,2,8]{0,2,1:T(8,128)(2,1)S(1)}, u32[]{:S(2)}) copy-start(bf16[512,2,8]{0,2,1:T(8,128)(2,1)S(1)} %get-tuple-element.94) | copy-start | bytes 49156
  18.5 27.1 %copy-start.56 = (bf16[512,2,8]{0,2,1:T(8,128)(2,1)}, bf16[512,2,8]{0,2,1:T(8,128)(2,1)S(1)}, u32[]{:S(2)}) copy-start(bf16[512,2,8]{0,2,1:T(8,128)(2,1)S(1)} %get-tuple-element.83) | copy-start | bytes 49156
  18.5 27.1 %copy-start.58 = (bf16[512,2,8]{0,2,1:T(8,128)(2,1)}, bf16[512,2,8]{0,2,1:T(8,128)(2,1)S(1)}, u32[]{:S(2)}) copy-start(bf16[512,2,8]{0,2,1:T(8,128)(2,1)S(1)} %get-tuple-element.84) | copy-start | bytes 49156
  18.5 25.6 %collective-permute-start.3 = (bf16[512,2,64]{0,2,1:T(8,128)(2,1)S(1)}, bf16[512,2,64]{0,2,1:T(8,128)(2,1)S(1)}, u32[]{:S(2)}, u32[]{:S(2)}) collective-permute-start(bf16[512,2,64]{0,2,1:T(8,128)(2,1)S(1)} %pad_maximum_fusion.12), channel_id=1, source_target_pairs={{0,8},{8,16},{16,24},{24,32},{32,40},{40,48},{48,56},{56,64},{64,7... | collective-permute-start | bytes 393224 | tf_op jit(solution)/shard_map/ppermute | solution.py:15
  23.4 22.0 %collective-permute-start.4 = (bf16[512,2,64]{0,2,1:T(8,128)(2,1)S(1)}, bf16[512,2,64]{0,2,1:T(8,128)(2,1)S(1)}, u32[]{:S(2)}, u32[]{:S(2)}) collective-permute-start(bf16[512,2,64]{0,2,1:T(8,128)(2,1)S(1)} %pad_maximum_fusion.12), channel_id=1, source_target_pairs={{0,16},{8,24},{16,32},{24,40},{32,48},{40,56},{48,64},{56,72},{64,... | collective-permute-start | bytes 393224 | tf_op jit(solution)/shard_map/ppermute | solution.py:15
  26.1 19.4 %collective-permute-start.5 = (bf16[512,2,64]{0,2,1:T(8,128)(2,1)S(1)}, bf16[512,2,64]{0,2,1:T(8,128)(2,1)S(1)}, u32[]{:S(2)}, u32[]{:S(2)}) collective-permute-start(bf16[512,2,64]{0,2,1:T(8,128)(2,1)S(1)} %pad_maximum_fusion.12), channel_id=1, source_target_pairs={{0,24},{8,32},{16,40},{24,48},{32,56},{40,64},{48,72},{56,80},{64,... | collective-permute-start | bytes 393224 | tf_op jit(solution)/shard_map/ppermute | solution.py:15
  28.8 21.9 %copy-start.44 = (bf16[512,1,128]{0,2,1:T(8,128)(2,1)}, bf16[512,1,128]{0,2,1:T(8,128)(2,1)S(1)}, u32[]{:S(2)}) copy-start(bf16[512,1,128]{0,2,1:T(8,128)(2,1)S(1)} %slice.503) | copy-start | bytes 393220
  28.8 21.9 %collective-permute-start = (bf16[512,2,64]{0,2,1:T(8,128)(2,1)S(1)}, bf16[512,2,64]{0,2,1:T(8,128)(2,1)S(1)}, u32[]{:S(2)}, u32[]{:S(2)}) collective-permute-start(bf16[512,2,64]{0,2,1:T(8,128)(2,1)S(1)} %bitcast.214), channel_id=1, source_target_pairs={{0,8},{8,16},{16,24},{24,32},{32,40},{40,48},{48,56},{56,64},{64,7... | collective-permute-start | bytes 393224 | tf_op jit(solution)/shard_map/ppermute | solution.py:15
  32.7 18.1 %collective-permute-start.1 = (bf16[512,2,64]{0,2,1:T(8,128)(2,1)S(1)}, bf16[512,2,64]{0,2,1:T(8,128)(2,1)}, u32[]{:S(2)}, u32[]{:S(2)}) collective-permute-start(bf16[512,2,64]{0,2,1:T(8,128)(2,1)S(1)} %bitcast.215), channel_id=1, source_target_pairs={{0,16},{8,24},{16,32},{24,40},{32,48},{40,56},{48,64},{56,72},{64,... | collective-permute-start | bytes 393224 | tf_op jit(solution)/shard_map/ppermute | solution.py:15
  44.2 6.6 collective-permute-start.2
  59.1 315.2 %all-reduce.9.cloned.1.call-start = ((), (), s32[]{:S(2)}) async-start(), calls=%async_computation.9 | async-start | bytes 4194304 | tf_op jit(solution)/shard_map/psum | solution.py:222
  175.0 25.0 %collective-permute-start.10 = (bf16[512,2,64]{0,2,1:T(8,128)(2,1)S(1)}, bf16[512,2,64]{0,2,1:T(8,128)(2,1)S(1)}, u32[]{:S(2)}, u32[]{:S(2)}) collective-permute-start(bf16[512,2,64]{0,2,1:T(8,128)(2,1)S(1)} %pad_maximum_fusion.14), channel_id=1, source_target_pairs={{0,16},{8,24},{16,32},{24,40},{32,48},{40,56},{48,64},{56,72},{64,... | collective-permute-start | bytes 393224 | tf_op jit(solution)/shard_map/ppermute | solution.py:15
  176.5 27.2 %collective-permute-start.11 = (bf16[512,2,64]{0,2,1:T(8,128)(2,1)S(1)}, bf16[512,2,64]{0,2,1:T(8,128)(2,1)S(1)}, u32[]{:S(2)}, u32[]{:S(2)}) collective-permute-start(bf16[512,2,64]{0,2,1:T(8,128)(2,1)S(1)} %pad_maximum_fusion.14), channel_id=1, source_target_pairs={{0,24},{8,32},{16,40},{24,48},{32,56},{40,64},{48,72},{56,80},{64,... | collective-permute-start | bytes 393224 | tf_op jit(solution)/shard_map/ppermute | solution.py:15
  183.5 20.2 %collective-permute-start.9 = (bf16[512,2,64]{0,2,1:T(8,128)(2,1)S(1)}, bf16[512,2,64]{0,2,1:T(8,128)(2,1)S(1)}, u32[]{:S(2)}, u32[]{:S(2)}) collective-permute-start(bf16[512,2,64]{0,2,1:T(8,128)(2,1)S(1)} %pad_maximum_fusion.14), channel_id=1, source_target_pairs={{0,8},{8,16},{16,24},{24,32},{32,40},{40,48},{48,56},{56,64},{64,7... | collective-permute-start | bytes 393224 | tf_op jit(solution)/shard_map/ppermute | solution.py:15
  186.3 30.9 %copy-start.45 = (bf16[512,1,128]{0,2,1:T(8,128)(2,1)}, bf16[512,1,128]{0,2,1:T(8,128)(2,1)S(1)}, u32[]{:S(2)}) copy-start(bf16[512,1,128]{0,2,1:T(8,128)(2,1)S(1)} %slice.502) | copy-start | bytes 393220
  186.3 30.9 %collective-permute-start.6 = (bf16[512,2,64]{0,2,1:T(8,128)(2,1)S(1)}, bf16[512,2,64]{0,2,1:T(8,128)(2,1)}, u32[]{:S(2)}, u32[]{:S(2)}) collective-permute-start(bf16[512,2,64]{0,2,1:T(8,128)(2,1)S(1)} %bitcast.219), channel_id=1, source_target_pairs={{0,8},{8,16},{16,24},{24,32},{32,40},{40,48},{48,56},{56,64},{64,7... | collective-permute-start | bytes 393224 | tf_op jit(solution)/shard_map/ppermute | solution.py:15
  190.4 26.8 %collective-permute-start.7 = (bf16[512,2,64]{0,2,1:T(8,128)(2,1)S(1)}, bf16[512,2,64]{0,2,1:T(8,128)(2,1)}, u32[]{:S(2)}, u32[]{:S(2)}) collective-permute-start(bf16[512,2,64]{0,2,1:T(8,128)(2,1)S(1)} %bitcast.220), channel_id=1, source_target_pairs={{0,16},{8,24},{16,32},{24,40},{32,48},{40,56},{48,64},{56,72},{64,... | collective-permute-start | bytes 393224 | tf_op jit(solution)/shard_map/ppermute | solution.py:15
  200.1 17.2 %collective-permute-start.8 = (bf16[512,2,64]{0,2,1:T(8,128)(2,1)S(1)}, bf16[512,2,64]{0,2,1:T(8,128)(2,1)}, u32[]{:S(2)}, u32[]{:S(2)}) collective-permute-start(bf16[512,2,64]{0,2,1:T(8,128)(2,1)S(1)} %bitcast.221), channel_id=1, source_target_pairs={{0,24},{8,32},{16,40},{24,48},{32,56},{40,64},{48,72},{56,80},{64,... | collective-permute-start | bytes 393224 | tf_op jit(solution)/shard_map/ppermute | solution.py:15
  224.1 11.4 collective-permute-start.12
  227.3 10.3 collective-permute-start.13
  228.6 15.7 %collective-permute-start.14 = (f32[512,2,64]{0,2,1:T(8,128)S(1)}, f32[512,2,64]{0,2,1:T(8,128)S(1)}, u32[]{:S(2)}, u32[]{:S(2)}) collective-permute-start(f32[512,2,64]{0,2,1:T(8,128)S(1)} %get-tuple-element.62), channel_id=1, source_target_pairs={{24,0},{32,8},{40,16},{48,24},{56,32},{64,40},{72,48},{80,56},{88,... | collective-permute-start | bytes 786440 | tf_op jit(solution)/shard_map/ppermute | solution.py:15
  232.2 14.6 %collective-permute-start.15 = (f32[512,2,64]{0,2,1:T(8,128)}, f32[512,2,64]{0,2,1:T(8,128)}, u32[]{:S(2)}, u32[]{:S(2)}) collective-permute-start(f32[512,2,64]{0,2,1:T(8,128)} %get-tuple-element.64), channel_id=1, source_target_pairs={{8,0},{16,8},{24,16},{32,24},{40,32},{48,40},{56,48},{64,56},{72,6... | collective-permute-start | bytes 786440 | tf_op jit(solution)/shard_map/ppermute | solution.py:15
  234.1 14.7 %collective-permute-start.16 = (f32[512,2,64]{0,2,1:T(8,128)}, f32[512,2,64]{0,2,1:T(8,128)}, u32[]{:S(2)}, u32[]{:S(2)}) collective-permute-start(f32[512,2,64]{0,2,1:T(8,128)} %get-tuple-element.66), channel_id=1, source_target_pairs={{16,0},{24,8},{32,16},{40,24},{48,32},{56,40},{64,48},{72,56},{80,... | collective-permute-start | bytes 786440 | tf_op jit(solution)/shard_map/ppermute | solution.py:15
  235.5 21.9 %collective-permute-start.17 = (f32[512,2,64]{0,2,1:T(8,128)}, f32[512,2,64]{0,2,1:T(8,128)}, u32[]{:S(2)}, u32[]{:S(2)}) collective-permute-start(f32[512,2,64]{0,2,1:T(8,128)} %get-tuple-element.65), channel_id=1, source_target_pairs={{24,0},{32,8},{40,16},{48,24},{56,32},{64,40},{72,48},{80,56},{88,... | collective-permute-start | bytes 786440 | tf_op jit(solution)/shard_map/ppermute | solution.py:15
  268.7 233.6 %reduce-scatter.15.cloned.1.call-start = ((), (), s32[]{:S(2)}) async-start(), calls=%async_computation.13 | async-start | bytes 557056 | tf_op jit(solution)/shard_map/reduce_scatter | solution.py:226
  276.2 229.5 %reduce-scatter.13.cloned.1.call-start = ((), (), s32[]{:S(2)}) async-start(), calls=%async_computation.12 | async-start | bytes 557056 | tf_op jit(solution)/shard_map/reduce_scatter | solution.py:226
  379.5 189.2 %reduce-scatter.11.cloned.1.call-start = ((), (), s32[]{:S(2)}) async-start(), calls=%async_computation.11 | async-start | bytes 1671168 | tf_op jit(solution)/shard_map/reduce_scatter | solution.py:225
  382.7 249.6 %reduce-scatter.9.cloned.1.call-start = ((), (), s32[]{:S(2)}) async-start(), calls=%async_computation.10 | async-start | bytes 1671168 | tf_op jit(solution)/shard_map/reduce_scatter | solution.py:225
  393.0 14.2 %collective-permute-start.18 = (f32[512,2,64]{0,2,1:T(8,128)S(1)}, f32[512,2,64]{0,2,1:T(8,128)S(1)}, u32[]{:S(2)}, u32[]{:S(2)}) collective-permute-start(f32[512,2,64]{0,2,1:T(8,128)S(1)} %get-tuple-element.55), channel_id=1, source_target_pairs={{8,0},{16,8},{24,16},{32,24},{40,32},{48,40},{56,48},{64,56},{72,6... | collective-permute-start | bytes 786440 | tf_op jit(solution)/shard_map/ppermute | solution.py:15
  397.6 10.9 collective-permute-start.19
  399.0 17.7 %collective-permute-start.20 = (f32[512,2,64]{0,2,1:T(8,128)S(1)}, f32[512,2,64]{0,2,1:T(8,128)S(1)}, u32[]{:S(2)}, u32[]{:S(2)}) collective-permute-start(f32[512,2,64]{0,2,1:T(8,128)S(1)} %get-tuple-element.56), channel_id=1, source_target_pairs={{24,0},{32,8},{40,16},{48,24},{56,32},{64,40},{72,48},{80,56},{88,... | collective-permute-start | bytes 786440 | tf_op jit(solution)/shard_map/ppermute | solution.py:15
  404.0 19.6 %collective-permute-start.21 = (f32[512,2,64]{0,2,1:T(8,128)}, f32[512,2,64]{0,2,1:T(8,128)}, u32[]{:S(2)}, u32[]{:S(2)}) collective-permute-start(f32[512,2,64]{0,2,1:T(8,128)} %get-tuple-element.58), channel_id=1, source_target_pairs={{8,0},{16,8},{24,16},{32,24},{40,32},{48,40},{56,48},{64,56},{72,6... | collective-permute-start | bytes 786440 | tf_op jit(solution)/shard_map/ppermute | solution.py:15
  405.9 17.7 %collective-permute-start.22 = (f32[512,2,64]{0,2,1:T(8,128)}, f32[512,2,64]{0,2,1:T(8,128)}, u32[]{:S(2)}, u32[]{:S(2)}) collective-permute-start(f32[512,2,64]{0,2,1:T(8,128)} %get-tuple-element.60), channel_id=1, source_target_pairs={{16,0},{24,8},{32,16},{40,24},{48,32},{56,40},{64,48},{72,56},{80,... | collective-permute-start | bytes 786440 | tf_op jit(solution)/shard_map/ppermute | solution.py:15
  407.2 22.7 %collective-permute-start.23 = (f32[512,2,64]{0,2,1:T(8,128)}, f32[512,2,64]{0,2,1:T(8,128)}, u32[]{:S(2)}, u32[]{:S(2)}) collective-permute-start(f32[512,2,64]{0,2,1:T(8,128)} %get-tuple-element.59), channel_id=1, source_target_pairs={{24,0},{32,8},{40,16},{48,24},{56,32},{64,40},{72,48},{80,56},{88,... | collective-permute-start | bytes 786440 | tf_op jit(solution)/shard_map/ppermute | solution.py:15
  436.7 260.3 %reduce-scatter.23.cloned.1.call-start = ((), (), s32[]{:S(2)}) async-start(), calls=%async_computation.17 | async-start | bytes 2228224 | tf_op jit(solution)/shard_map/reduce_scatter | solution.py:228
  440.2 321.6 %reduce-scatter.21.cloned.1.call-start = ((), (), s32[]{:S(2)}) async-start(), calls=%async_computation.16 | async-start | bytes 2228224 | tf_op jit(solution)/shard_map/reduce_scatter | solution.py:228
  443.8 382.9 %reduce-scatter.19.cloned.1.call-start = ((), (), s32[]{:S(2)}) async-start(), calls=%async_computation.15 | async-start | bytes 2228224 | tf_op jit(solution)/shard_map/reduce_scatter | solution.py:227
  447.4 444.1 %reduce-scatter.17.cloned.1.call-start = ((), (), s32[]{:S(2)}) async-start(), calls=%async_computation.14 | async-start | bytes 2228224 | tf_op jit(solution)/shard_map/reduce_scatter | solution.py:227
  454.6 628.6 %all-reduce.11.cloned.1.call-start = ((), (), s32[]{:S(2)}) async-start(), calls=%async_computation.18 | async-start | bytes 8388608 | tf_op jit(solution)/shard_map/psum | solution.py:115
  467.5 615.6 %copy-start.8 = (bf16[512,1024]{1,0:T(8,128)(2,1)S(1)}, bf16[512,1024]{1,0:T(8,128)(2,1)}, u32[]{:S(2)}) copy-start(bf16[512,1024]{1,0:T(8,128)(2,1)} %param.13) | copy-start | bytes 3145732
  1083.2 57.2 %copy-start.77 = (f32[1,1024]{1,0:T(1,128)S(1)}, f32[1,1024]{1,0:T(1,128)}, u32[]{:S(2)}) copy-start(f32[1,1024]{1,0:T(1,128)} %get-tuple-element.99) | copy-start | bytes 12292
  1083.2 57.2 %copy-start.78 = (f32[1,1024]{1,0:T(1,128)S(1)}, f32[1,1024]{1,0:T(1,128)}, u32[]{:S(2)}) copy-start(f32[1,1024]{1,0:T(1,128)} %get-tuple-element.101) | copy-start | bytes 12292
  (96 other events, 367.4 us)
Sparse Core Ops, SparseCore 0:
  59.2 109.5 all-reduce.6
  268.8 105.4 all-reduce.8
  376.6 69.4 reduce-scatter.14
  448.5 57.1 reduce-scatter.12
  507.9 60.7 reduce-scatter.10
  571.1 61.1 reduce-scatter.8
  634.7 62.2 reduce-scatter.22
  699.4 62.4 reduce-scatter.20
  764.3 62.4 reduce-scatter.18
  829.0 62.4 reduce-scatter.16
  894.6 188.5 all-reduce.10
where the time goes:
time: 1170 us; the launch traced here: 1150 us
  waiting for transfers between devices  809 us (69%)
  matrix products  96.1 us (8%)
  blocking collectives  83.7 us (7%)
  starting transfers between devices  64.2 us (5%)
  other arithmetic  50.5 us (4%)
  local copies, waits for them, and re-layouts  31.6 us (3%)
  between operations  16 us (1%)
    psum x2, waiting for transfers between devices, on_device(): summed = lax.psum(branch, 'tensor')  294 us
    reduce_scatter x2, waiting for transfers between devices, on_device(): lax.psum_scatter(grad_wdown, 'dp', scatter_dimension=1, tiled=True)  128 us
    reduce_scatter x2, waiting for transfers between devices, on_device(): lax.psum_scatter(grad_win, 'dp', scatter_dimension=0, tiled=True)  128 us
    reduce_scatter x2, waiting for transfers between devices, on_device(): lax.psum_scatter(grad_wqkv, 'dp', scatter_dimension=0, tiled=True)  125 us
    psum x1, waiting for transfers between devices, on_device(): lax.psum((stream_part, gain_part, bias_part), 'tensor')  98 us
    ppermute x24, starting transfers between devices, passed_along(): return lax.ppermute(block, axis, route)  62.8 us
    psum x1, blocking collectives, on_device(): lax.psum((gain_stack, bias_stack, bqkv_stack, resid_stack, bin_stack), 'dp')  52.2 us
    ppermute x24, waiting for transfers between devices, passed_along(): return lax.ppermute(block, axis, route)  32.5 us
  transfers between devices with their start and end apart: 35, of which 16 were waited for; matrix products, arithmetic and copies ran while one was open for 10% of the time, Pallas kernels for 0%

commit v1 on v0

v1 whole, which is shorter than its diff:
```python
import functools

import jax
import jax.numpy as jnp
import numpy as np
from jax import lax
from jax.experimental import pallas as pl
from jax.experimental.pallas import tpu as pltpu
from jax.sharding import PartitionSpec as P

HEAD_DIM = 64
ROT = 16
SEQ = 2048
LAYERS = 2
EPS = 1e-05
F32 = jnp.float32
BF16 = jnp.bfloat16
MESH = pl.DeviceIdType.MESH
LANES = 128
QT = 256
KT = 256
MT = 256
ST = 32


def nn(a, b):
    return jnp.dot(a, b, preferred_element_type=F32)


def nt(a, b):
    return lax.dot_general(a, b, (((1,), (1,)), ((), ())), preferred_element_type=F32)


def rope_constants():
    half = ROT // 2
    exponent = np.arange(0, ROT, 2).astype(np.float32) / np.float32(ROT)
    inverse = (np.float32(1.0) / np.float32(10000.0) ** exponent).astype(np.float32)
    angles = np.arange(SEQ).astype(np.float32)[:, None] * inverse[None, :]
    cosine = np.ones((SEQ, LANES), np.float32)
    sine = np.zeros((SEQ, LANES), np.float32)
    for start in range(0, LANES, HEAD_DIM):
        cosine[:, start : start + half] = np.cos(angles)
        cosine[:, start + half : start + ROT] = np.cos(angles)
        sine[:, start : start + half] = -np.sin(angles)
        sine[:, start + half : start + ROT] = np.sin(angles)
    return cosine, sine


def rotate(values, cosine, sine):
    half = ROT // 2
    lane = lax.broadcasted_iota(jnp.int32, values.shape, 1)
    partner = jnp.where(
        lane % HEAD_DIM < half,
        pltpu.roll(values, LANES - half, 1),
        pltpu.roll(values, half, 1),
    )
    return values * cosine + partner * sine


def head_only(values, head):
    lane = lax.broadcasted_iota(jnp.int32, values.shape, 1)
    return jnp.where(lane // HEAD_DIM == head, values, jnp.zeros_like(values))


def rows_at(step, size):
    return pl.ds(pl.multiple_of(step * size, size), size)


def remote(src, dst, send_sem, recv_sem, **device):
    return pltpu.make_async_remote_copy(
        src_ref=src,
        dst_ref=dst,
        send_sem=send_sem,
        recv_sem=recv_sem,
        device_id=device,
        device_id_type=MESH,
    )


class Refs:
    pass


def step_kernel(nt_dev, nd, *refs):
    names = (
        "tok", "cot", "gain", "bias", "wqkv_h", "bqkv", "wout_h", "bout", "win_h", "bin",
        "wdown_h", "bdown", "cos_h", "sin_h", "x", "g", "ogain", "obias", "obqkv", "obout",
        "obin", "obdown", "oq", "oo", "oi", "od", "wqkv", "wout", "win", "wdown", "cosine",
        "sine", "xt", "ct", "h0", "h1", "qm", "kv", "kt", "vt", "ob", "ot", "lse", "u", "act",
        "mu", "rs", "part", "psend", "rsbuf", "agbuf", "dz", "do", "dom", "delta", "dqt",
        "dkvo", "dkvi", "own", "dqkv", "du", "dh0", "ge", "gl", "r1e", "r1l", "r2e", "r2l",
        "s3e", "s3l", "r3e", "r3l", "k3e", "k3l", "sm", "sr1", "sr2", "sr3", "lnacc", "lsem",
        "kvs", "kvr", "dks", "dkr", "ars", "arr", "g1s", "g1r", "g2s", "g2r", "g3s", "g3r",
        "s1s", "s1r", "s2s", "s2r", "s3s", "s3r",
    )
    assert len(names) == len(refs)
    v = Refs()
    v.__dict__.update(zip(names, refs))
    rows, depth = v.x.shape
    group = SEQ // rows
    nx = nd // group
    chunk = rows // nt_dev
    grow = depth // nd
    width = v.wout.shape[1]
    ff = v.win.shape[2]

    me_t = lax.axis_index("tensor")
    me_d = lax.axis_index("dp")
    rank = lax.rem(me_d, group)
    core = lax.rem(me_d, 2)
    zlo = lax.rem(me_d // 2, 2)
    xc = me_d // group
    other_core = me_d + 1 - 2 * core
    other_z = me_d + 2 - 4 * zlo

    barrier = pltpu.get_barrier_semaphore()
    for k in range(1, nt_dev):
        pl.semaphore_signal(
            barrier, inc=1, device_id={"tensor": lax.rem(me_t + k, nt_dev)}, device_id_type=MESH
        )
    for k in range(1, nd):
        pl.semaphore_signal(
            barrier, inc=1, device_id={"dp": lax.rem(me_d + k, nd)}, device_id_type=MESH
        )

    def load(src, dst, index):
        copy = pltpu.make_async_copy(src, dst, v.lsem.at[index])
        copy.start()
        return copy

    load_tok = load(v.tok, v.xt, 0)
    load_cos = load(v.cos_h.at[rows_at(rank, rows)], v.cosine, 1)
    load_sin = load(v.sin_h.at[rows_at(rank, rows)], v.sine, 2)
    load_qkv = []
    load_rest = []
    for l in range(LAYERS):
        load_qkv.append(
            [
                load(
                    v.wqkv_h.at[l, c],
                    v.wqkv.at[l, :, pl.ds(c * width, width)],
                    4 + 6 * l + c,
                )
                for c in range(3)
            ]
        )
        load_rest.append(
            [
                load(v.win_h.at[l], v.win.at[l], 4 + 6 * l + 3),
                load(v.wdown_h.at[l], v.wdown.at[l], 4 + 6 * l + 4),
                load(v.wout_h.at[l], v.wout.at[l], 4 + 6 * l + 5),
            ]
        )
    load_cot = load(v.cot, v.ct, 3)

    def norm_rows(l, at, x):
        mean = jnp.mean(x, axis=-1, keepdims=True)
        center = x - mean
        spread = jnp.mean(center * center, axis=-1, keepdims=True)
        r = lax.rsqrt(spread + EPS)
        xhat = center * r
        v.mu[l, at, :] = mean
        v.rs[l, at, :] = r
        v.h0[l, at, :] = (xhat * v.gain[l, 0:1, :] + v.bias[l, 0:1, :]).astype(BF16)
        v.h1[l, at, :] = (xhat * v.gain[l, 1:2, :] + v.bias[l, 1:2, :]).astype(BF16)

    def stream_rows(l, at):
        if l == 0:
            return v.xt[at, :].astype(F32)
        return v.x[at, :]

    def rs_copy(s, j):
        return remote(
            v.psend.at[s, j],
            v.rsbuf.at[s, me_t],
            v.ars.at[s, 0, j],
            v.arr.at[s, 0, me_t],
            tensor=j,
        )

    def rs_start(s, j):
        @pl.when(j != me_t)
        def _():
            rs_copy(s, j).start()

    def rs_finish(s):
        v.rsbuf[s, me_t] = v.psend[s, me_t]

        def one(k, carry):
            src = lax.rem(me_t + k, nt_dev)
            remote(
                v.psend.at[s, src],
                v.rsbuf.at[s, src],
                v.ars.at[s, 0, src],
                v.arr.at[s, 0, src],
                tensor=src,
            ).wait()
            return carry

        lax.fori_loop(1, nt_dev, one, 0)

    def rs_sum(s, at):
        total = v.rsbuf[s, 0, at, :].astype(F32)
        for k in range(1, nt_dev):
            total = total + v.rsbuf[s, k, at, :].astype(F32)
        return total

    def ag_copy(s, k):
        return remote(
            v.agbuf.at[s, me_t],
            v.agbuf.at[s, me_t],
            v.ars.at[s, 1, k],
            v.arr.at[s, 1, me_t],
            tensor=lax.rem(me_t + k, nt_dev),
        )

    def ag_start(s):
        for k in range(1, nt_dev):
            ag_copy(s, k).start()

    def ag_each(s, use):
        def one(k, carry):
            src = lax.rem(me_t + k, nt_dev)

            @pl.when(k > 0)
            def _():
                remote(
                    v.agbuf.at[s, src],
                    v.agbuf.at[s, src],
                    v.ars.at[s, 1, k],
                    v.arr.at[s, 1, src],
                    tensor=src,
                ).wait_recv()

            for i in range(chunk // ST):
                use(
                    pl.ds(pl.multiple_of(src * chunk + i * ST, ST), ST),
                    v.agbuf[s, src, i * ST : (i + 1) * ST, :].astype(F32),
                )
            return carry

        lax.fori_loop(0, nt_dev, one, 0)
        for k in range(1, nt_dev):
            ag_copy(s, k).wait_send()

    def kv_copy(l, s):
        return remote(
            v.kv.at[l, rank], v.kv.at[l, rank], v.kvs.at[l, s - 1], v.kvr.at[l, s - 1], dp=me_d + s
        )

    def kv_in(l, s):
        return remote(
            v.kv.at[l, rank - s],
            v.kv.at[l, rank - s],
            v.kvs.at[l, s - 1],
            v.kvr.at[l, s - 1],
            dp=me_d - s,
        )

    def dkv_copy(l, s):
        return remote(
            v.dkvo.at[l, rank - s],
            v.dkvi.at[l, s - 1],
            v.dks.at[l, s - 1],
            v.dkr.at[l, s - 1],
            dp=me_d - s,
        )

    def dkv_in(l, s):
        return remote(
            v.dkvo.at[l, rank],
            v.dkvi.at[l, s - 1],
            v.dks.at[l, s - 1],
            v.dkr.at[l, s - 1],
            dp=me_d + s,
        )

    def transpose_block(l, b):
        block = v.kv[l, b].astype(F32)
        v.kt[l, b] = block[:, :width].T.astype(BF16)
        v.vt[l, b] = block[:, width:].T.astype(BF16)

    def qkv_and_send(l, barrier_wait):
        for c in load_qkv[l]:
            c.wait()
        if l == 0:
            load_cos.wait()
            load_sin.wait()

        def one(i, carry):
            at = rows_at(i, MT)
            mixed = nn(v.h0[l, at, :], v.wqkv[l])
            cosine, sine = v.cosine[at, :], v.sine[at, :]
            q = rotate(mixed[:, :width] + v.bqkv[0, l : l + 1, :], cosine, sine).astype(BF16)
            k = rotate(mixed[:, width : 2 * width] + v.bqkv[1, l : l + 1, :], cosine, sine)
            val = mixed[:, 2 * width :] + v.bqkv[2, l : l + 1, :]
            scaled = (q.astype(F32) * 0.125).astype(BF16)
            v.qm[l, 0, at, :] = head_only(scaled, 0)
            v.qm[l, 1, at, :] = head_only(scaled, 1)
            v.kv[l, rank, at, :width] = k.astype(BF16)
            v.kv[l, rank, at, width:] = val.astype(BF16)
            return carry

        lax.fori_loop(0, rows // MT, one, 0)
        if barrier_wait:
            with jax.named_scope("barrier"):
                pl.semaphore_wait(barrier, nt_dev - 1 + nd - 1)
        for s in range(1, group):

            @pl.when(rank + s < group)
            def _():
                kv_copy(l, s).start()

    def feed_forward(l):
        for c in load_rest[l]:
            c.wait()

        def up(i, carry):
            at = rows_at(i, MT)
            v.u[l, at, :] = nn(v.h1[l, at, :], v.win[l]) + v.bin[l : l + 1, :]
            return carry

        lax.fori_loop(0, rows // MT, up, 0)

        def activate(i, carry):
            at = rows_at(i, ST)
            u = v.u[l, at, :]
            v.act[l, at, :] = (0.5 * u * (1.0 + lax.erf(u * np.float32(0.5**0.5)))).astype(BF16)
            return carry

        lax.fori_loop(0, rows // ST, activate, 0)

        def down(i, carry):
            at = rows_at(i, MT)
            v.part[at, :] = nn(v.act[l, at, :], v.wdown[l])
            return carry

        lax.fori_loop(0, rows // MT, down, 0)

    def attention(l, s):
        transpose_block(l, rank)
        for k in range(1, group):

            @pl.when(rank >= k)
            def _():
                kv_in(l, k).wait_recv()
                transpose_block(l, rank - k)

        for qt in range(rows // QT):
            q_at = slice(qt * QT, (qt + 1) * QT)
            for h in range(2):
                qh = v.qm[l, h, q_at, :]
                head_rows = slice(h * HEAD_DIM, (h + 1) * HEAD_DIM)

                def block(b, carry, masked):
                    top, total, out = carry
                    sc = nt(v.kv[l, b, :, :width], qh)
                    if masked:
                        key = lax.broadcasted_iota(jnp.int32, sc.shape, 0)
                        query = lax.broadcasted_iota(jnp.int32, sc.shape, 1) + qt * QT
                        sc = jnp.where(key <= query, sc, -1e30)
                    new = jnp.maximum(top, jnp.max(sc, axis=0, keepdims=True))
                    p = jnp.exp(sc - new)
                    fade = jnp.exp(top - new)
                    total = total * fade + jnp.sum(p, axis=0, keepdims=True)
                    out = out * fade + nn(v.vt[l, b, head_rows, :], p.astype(BF16))
                    return new, total, out

                carry = (
                    jnp.full((1, QT), -1e30, F32),
                    jnp.zeros((1, QT), F32),
                    jnp.zeros((HEAD_DIM, QT), F32),
                )
                carry = lax.fori_loop(0, rank, functools.partial(block, masked=False), carry)
                top, total, out = block(rank, carry, True)
                v.ot[l, head_rows, q_at] = out / total
                v.lse[l, h : h + 1, q_at] = top + jnp.log(total)
            v.ob[l, q_at, :] = v.ot[l, :, q_at].T.astype(BF16)
            both = nn(v.ob[l, q_at, :], v.wout[l]) + v.part[q_at, :]
            first = qt * QT // chunk
            v.psend[s, first : first + QT // chunk] = both.astype(BF16).reshape(
                QT // chunk, chunk, depth
            )
            for j in range(first, first + QT // chunk):
                rs_start(s, j)

    def branch_reduce(s):
        rs_finish(s)
        for i in range(chunk // 16):
            at = slice(i * 16, (i + 1) * 16)
            v.agbuf[s, me_t, at, :] = rs_sum(s, at).astype(BF16)
        ag_start(s)

    grads = {0: (v.ge, v.r1e, v.r2e, v.s3e, v.r3e, v.k3e), 1: (v.gl, v.r1l, v.r2l, v.s3l, v.r3l, v.k3l)}

    def core_copy(l, p):
        g, r1 = grads[p][:2]
        return remote(
            g.at[l, 1 - core], r1.at[l], v.g1s.at[l, p], v.g1r.at[l, p], dp=other_core
        )

    def x_copy(l, p, k):
        r1, r2 = grads[p][1:3]
        to = lax.rem(xc + k, nx)
        return remote(
            r1.at[l, pl.ds(2 * to, 2)],
            r2.at[l, k - 1],
            v.g2s.at[l, p, k - 1],
            v.g2r.at[l, p, k - 1],
            dp=to * group + zlo * 2 + core,
        )

    def z_copy(l, p):
        return remote(
            grads[p][3].at[l], grads[p][4].at[l], v.g3s.at[l, p], v.g3r.at[l, p], dp=other_z
        )

    def grad_core(l, p):
        core_copy(l, p).start()

    def grad_x(l, p):
        core_copy(l, p).wait()
        g, r1 = grads[p][:2]

        def one(i, carry):
            for j in range(grow // 16):
                at = slice(j * 16, (j + 1) * 16)
                r1[l, i, at, :] = (
                    r1[l, i, at, :].astype(F32) + g[l, core, i, at, :].astype(F32)
                ).astype(BF16)
            return carry

        lax.fori_loop(0, nd // 2, one, 0)
        for k in range(1, nx):
            x_copy(l, p, k).start()

    def grad_z(l, p):
        _, r1, r2, s3, r3, k3 = grads[p]
        for k in range(1, nx):
            x_copy(l, p, k).wait()

        def total(z, at):
            value = r1[l, 2 * xc + z, at, :].astype(F32)
            for k in range(1, nx):
                value = value + r2[l, k - 1, z, at, :].astype(F32)
            return value

        for j in range(grow // 16):
            at = slice(j * 16, (j + 1) * 16)
            s3[l, at, :] = total(1 - zlo, at).astype(BF16)
        z_copy(l, p).start()
        for j in range(grow // 16):
            at = slice(j * 16, (j + 1) * 16)
            k3[l, at, :] = total(zlo, at)

    def grad_end(l, p):
        z_copy(l, p).wait()
        _, _, _, _, r3, k3 = grads[p]
        for j in range(grow // 16):
            at = slice(j * 16, (j + 1) * 16)
            total = k3[l, at, :] + r3[l, at, :].astype(F32)
            if p == 0:
                v.oo[l, at, :] = total[:, :width]
                v.od[l, at, :] = total[:, width : width + ff]
                v.oi[l, at, :] = total[:, width + ff :]
            else:
                for c in range(3):
                    v.oq[l, c, at, :] = total[:, c * width : (c + 1) * width]

    def start_gradient(l, at, gradient):
        v.dz[at, :] = gradient.astype(BF16)

    def attention_back(l):
        v.do[...] = nt(v.dz[...], v.wout[l]).astype(BF16)
        do = v.do[...]
        v.dom[0] = head_only(do, 0)
        v.dom[1] = head_only(do, 1)
        product = do.astype(F32).T * v.ot[l]
        v.delta[0:1, :] = jnp.sum(product[:HEAD_DIM], axis=0, keepdims=True)
        v.delta[1:2, :] = jnp.sum(product[HEAD_DIM:], axis=0, keepdims=True)
        v.dqt[...] = jnp.zeros_like(v.dqt)

        def piece(b, i, masked):
            at = rows_at(i, KT)
            keys = v.kv[l, b, at, :width]
            values = v.kv[l, b, at, width:]
            dk = jnp.zeros((KT, width), F32)
            dv = jnp.zeros((KT, width), F32)
            for h in range(2):
                head_rows = slice(h * HEAD_DIM, (h + 1) * HEAD_DIM)
                sc = nt(keys, v.qm[l, h])
                if masked:
                    key = lax.broadcasted_iota(jnp.int32, sc.shape, 0) + i * KT
                    query = lax.broadcasted_iota(jnp.int32, sc.shape, 1)
                    sc = jnp.where(key <= query, sc, -1e30)
                p = jnp.exp(sc - v.lse[l, h : h + 1, :])
                dp = nt(values, v.dom[h])
                ds = (p * (dp - v.delta[h : h + 1, :])).astype(BF16)
                dv = dv + nn(p.astype(BF16), v.dom[h])
                dk = dk + nn(ds, v.qm[l, h])
                v.dqt[head_rows, :] += nn(v.kt[l, b, head_rows, at], ds)
            return dk, dv

        def far(b, carry):
            def inner(i, c):
                dk, dv = piece(b, i, False)
                at = rows_at(i, KT)
                v.dkvo[l, b, at, :width] = dk.astype(BF16)
                v.dkvo[l, b, at, width:] = dv.astype(BF16)
                return c

            lax.fori_loop(0, rows // KT, inner, 0)
            for s in range(1, group):

                @pl.when(rank - b == s)
                def _():
                    dkv_copy(l, s).start()

            return carry

        lax.fori_loop(0, rank, far, 0)

        def near(i, c):
            dk, dv = piece(rank, i, True)
            at = rows_at(i, KT)
            v.own[at, :width] = dk
            v.own[at, width:] = dv
            return c

        lax.fori_loop(0, rows // KT, near, 0)

    def feed_forward_back(l):
        def up(i, carry):
            at = rows_at(i, MT)
            v.part[at, :ff] = nt(v.dz[at, :], v.wdown[l])
            return carry

        lax.fori_loop(0, rows // MT, up, 0)

        def slope(i, acc):
            at = rows_at(i, ST)
            u = v.u[l, at, :]
            inner = 0.5 * (1.0 + lax.erf(u * np.float32(0.5**0.5)))
            inner = inner + u * jnp.exp(-0.5 * u * u) * np.float32((2.0 * np.pi) ** -0.5)
            du = (v.part[at, :ff] * inner).astype(BF16)
            v.du[at, :] = du
            return acc + jnp.sum(du.astype(F32).reshape(ST // 8, 8, ff), axis=0)

        acc = lax.fori_loop(0, rows // ST, slope, jnp.zeros((8, ff), F32))
        v.sm[l, 5:6, :ff] = jnp.sum(acc, axis=0, keepdims=True)

        def down(i, carry):
            at = rows_at(i, MT)
            v.part[at, :] = nt(v.du[at, :], v.win[l])
            return carry

        lax.fori_loop(0, rows // MT, down, 0)

    def early_grads(l):
        def one(i, carry):
            at = rows_at(i, 2 * grow)
            dzt = v.dz[:, at].astype(F32).T.astype(BF16)
            ht = v.h1[l, :, at].astype(F32).T.astype(BF16)
            wo = nn(dzt, v.ob[l]).astype(BF16)
            wd = nn(dzt, v.act[l]).astype(BF16)
            wi = nn(ht, v.du[...]).astype(BF16)
            for c in range(2):
                part = slice(c * grow, (c + 1) * grow)
                v.ge[l, c, i, :, :width] = wo[part]
                v.ge[l, c, i, :, width : width + ff] = wd[part]
                v.ge[l, c, i, :, width + ff :] = wi[part]
            return carry

        lax.fori_loop(0, depth // (2 * grow), one, 0)

    def late_grads(l):
        def one(i, carry):
            at = rows_at(i, 2 * grow)
            ht = v.h0[l, :, at].astype(F32).T.astype(BF16)
            wq = nn(ht, v.dqkv[...]).astype(BF16)
            for c in range(2):
                v.gl[l, c, i] = wq[c * grow : (c + 1) * grow]
            return carry

        lax.fori_loop(0, depth // (2 * grow), one, 0)

    def qkv_back(l):
        for s in range(1, group):

            @pl.when(rank + s < group)
            def _():
                dkv_in(l, s).wait_recv()
                v.own[...] += v.dkvi[l, s - 1].astype(F32)

        cosine, sine = v.cosine[...], -v.sine[...]
        v.dqkv[:, :width] = rotate(v.dqt[...].T * 0.125, cosine, sine).astype(BF16)
        v.dqkv[:, width : 2 * width] = rotate(v.own[:, :width], cosine, sine).astype(BF16)
        v.dqkv[:, 2 * width : 3 * width] = v.own[:, width:].astype(BF16)
        v.sm[l, 5:6, ff : ff + 3 * width] = jnp.sum(
            v.dqkv[...].astype(F32), axis=0, keepdims=True
        )

        def one(i, carry):
            at = rows_at(i, MT)
            v.dh0[at, :] = nt(v.dqkv[at, :], v.wqkv[l])
            return carry

        lax.fori_loop(0, rows // MT, one, 0)

        def send(k, carry):
            j = lax.rem(me_t + k, nt_dev)
            for i in range(chunk // ST):
                at = pl.ds(pl.multiple_of(j * chunk + i * ST, ST), ST)
                both = v.dh0[at, :] * v.gain[l, 0:1, :] + v.part[at, :] * v.gain[l, 1:2, :]
                v.psend[0, j, i * ST : (i + 1) * ST, :] = both.astype(BF16)
            rs_start(0, j)
            return carry

        lax.fori_loop(1, nt_dev + 1, send, 0)

    def norm_grads(l):
        v.lnacc[...] = jnp.zeros_like(v.lnacc)

        def fold(value):
            return jnp.sum(value.reshape(2, 8, depth), axis=0)

        def one(i, carry):
            at = rows_at(i, 16)
            xhat = (stream_rows(l, at) - v.mu[l, at, :]) * v.rs[l, at, :]
            first, second = v.dh0[at, :], v.part[at, :]
            v.lnacc[0] += fold(first * xhat)
            v.lnacc[1] += fold(second * xhat)
            v.lnacc[2] += fold(first)
            v.lnacc[3] += fold(second)
            v.lnacc[4] += fold(v.dz[at, :].astype(F32))
            return carry

        lax.fori_loop(0, rows // 16, one, 0)
        for i in range(5):
            v.sm[l, i : i + 1, :] = jnp.sum(v.lnacc[i], axis=0, keepdims=True)

    def stream_reduce(l):
        rs_finish(0)
        for i in range(chunk // 16):
            at = pl.ds(pl.multiple_of(me_t * chunk + i * 16, 16), 16)
            gd = rs_sum(0, slice(i * 16, (i + 1) * 16))
            r = v.rs[l, at, :]
            xhat = (stream_rows(l, at) - v.mu[l, at, :]) * r
            mean = jnp.mean(gd, axis=-1, keepdims=True)
            along = jnp.mean(gd * xhat, axis=-1, keepdims=True)
            dx = r * (gd - mean - xhat * along)
            v.agbuf[0, me_t, i * 16 : (i + 1) * 16, :] = dx.astype(BF16)
        ag_start(0)

    def small_core():
        return remote(v.sm, v.sr1, v.s1s, v.s1r, dp=other_core)

    def small_dp(k):
        to = lax.rem(me_d + 2 * k, nd)
        return remote(v.sm, v.sr2.at[k - 1], v.s2s.at[k - 1], v.s2r.at[k - 1], dp=to)

    def small_tensor(k):
        to = lax.rem(me_t + k, nt_dev)
        return remote(
            v.sm,
            v.sr3.at[k - 1],
            v.s3s.at[k - 1],
            v.s3r.at[k - 1],
            tensor=to,
        )

    with jax.named_scope("tok"):
        load_tok.wait()

    def first_norm(i, carry):
        at = rows_at(i, ST)
        norm_rows(0, at, v.xt[at, :].astype(F32))
        return carry

    with jax.named_scope("norm0"):
        lax.fori_loop(0, rows // ST, first_norm, 0)
    v.sm[...] = jnp.zeros_like(v.sm)
    with jax.named_scope("qkv0"):
        qkv_and_send(0, True)
    with jax.named_scope("ffn0"):
        feed_forward(0)
    with jax.named_scope("attn0"):
        attention(0, 0)
    with jax.named_scope("reduce0"):
        branch_reduce(0)

    def next_stream(at, z):
        x = v.xt[at, :].astype(F32) + (z + (v.bout[0:1, :] + v.bdown[0:1, :]))
        v.x[at, :] = x
        norm_rows(1, at, x)

    with jax.named_scope("gather0"):
        ag_each(0, next_stream)
    with jax.named_scope("qkv1"):
        qkv_and_send(1, False)
    with jax.named_scope("ffn1"):
        feed_forward(1)
    with jax.named_scope("attn1"):
        attention(1, 1)

    with jax.named_scope("cot"):
        load_cot.wait()

    def first_gradient(i, carry):
        at = rows_at(i, ST)
        v.dz[at, :] = v.ct[at, :]
        v.g[at, :] = v.ct[at, :].astype(F32)
        return carry

    with jax.named_scope("dz1"):
        lax.fori_loop(0, rows // ST, first_gradient, 0)
    with jax.named_scope("attn_grad1"):
        attention_back(1)
    with jax.named_scope("ffn_grad1"):
        feed_forward_back(1)
    with jax.named_scope("reduce1"):
        branch_reduce(1)
    with jax.named_scope("early1"):
        early_grads(1)
    grad_core(1, 0)
    with jax.named_scope("qkv_grad1"):
        qkv_back(1)
    with jax.named_scope("late1"):
        late_grads(1)
    grad_core(1, 1)
    with jax.named_scope("gx10"):
        grad_x(1, 0)
    with jax.named_scope("norm_grad1"):
        norm_grads(1)
    with jax.named_scope("stream_reduce1"):
        stream_reduce(1)
    with jax.named_scope("gx11"):
        grad_x(1, 1)

    def last_stream(at, z):
        v.x[at, :] = v.x[at, :] + (z + (v.bout[1:2, :] + v.bdown[1:2, :]))

    with jax.named_scope("gather1"):
        ag_each(1, last_stream)

    def next_gradient(at, dx):
        gradient = v.g[at, :] + dx
        v.g[at, :] = gradient
        v.dz[at, :] = gradient.astype(BF16)

    with jax.named_scope("gather2"):
        ag_each(0, next_gradient)
    with jax.named_scope("attn_grad0"):
        attention_back(0)
    with jax.named_scope("gz10"):
        grad_z(1, 0)
    with jax.named_scope("gz11"):
        grad_z(1, 1)
    with jax.named_scope("ffn_grad0"):
        feed_forward_back(0)
    with jax.named_scope("early0"):
        early_grads(0)
    grad_core(0, 0)
    with jax.named_scope("gend10"):
        grad_end(1, 0)
    with jax.named_scope("gend11"):
        grad_end(1, 1)
    with jax.named_scope("qkv_grad0"):
        qkv_back(0)
    with jax.named_scope("gx00"):
        grad_x(0, 0)
    with jax.named_scope("late0"):
        late_grads(0)
    grad_core(0, 1)
    with jax.named_scope("norm_grad0"):
        norm_grads(0)
    small_core().start()
    with jax.named_scope("stream_reduce0"):
        stream_reduce(0)
    with jax.named_scope("gx01"):
        grad_x(0, 1)
    small_core().wait()
    v.sm[...] += v.sr1[...]
    for k in range(1, nd // 2):
        small_dp(k).start()

    def last_gradient(at, dx):
        v.g[at, :] = v.g[at, :] + dx

    with jax.named_scope("gather3"):
        ag_each(0, last_gradient)
    for k in range(1, nd // 2):
        small_dp(k).wait()
    total = v.sm[...]
    for k in range(1, nd // 2):
        total = total + v.sr2[k - 1]
    v.sm[...] = total
    for k in range(1, nt_dev):
        small_tensor(k).start()
    with jax.named_scope("gz00"):
        grad_z(0, 0)
    with jax.named_scope("gz01"):
        grad_z(0, 1)
    for l in range(LAYERS):
        v.obout[l : l + 1, :] = v.sm[l, 4:5, :]
        v.obdown[l : l + 1, :] = v.sm[l, 4:5, :]
        v.obin[l : l + 1, :] = v.sm[l, 5:6, :ff]
        for c in range(3):
            v.obqkv[c, l : l + 1, :] = v.sm[l, 5:6, ff + c * width : ff + (c + 1) * width]
    for k in range(1, nt_dev):
        small_tensor(k).wait()
    total = v.sm[...]
    for k in range(1, nt_dev):
        total = total + v.sr3[k - 1]
    v.ogain[...] = total[:, 0:2, :]
    v.obias[...] = total[:, 2:4, :]
    with jax.named_scope("gend00"):
        grad_end(0, 0)
    with jax.named_scope("gend01"):
        grad_end(0, 1)
    for l in range(LAYERS):
        for s in range(1, group):

            @pl.when(rank + s < group)
            def _():
                kv_copy(l, s).wait_send()

            @pl.when(rank >= s)
            def _():
                dkv_copy(l, s).wait_send()


def on_device(nt_dev, nd, *args):
    tokens, cotangent, ln_gain, ln_bias, w_qkv, b_qkv, w_out, b_out, w_in, b_in, w_down, b_down = args
    rows, depth = tokens.shape
    width = w_out.shape[1]
    ff = w_in.shape[2]
    group = SEQ // rows
    chunk = rows // nt_dev
    grow = depth // nd
    half = nd // 2
    nx = nd // group
    early = width + 2 * ff
    late = 3 * width
    cosine, sine = rope_constants()
    vm = pltpu.VMEM
    dma = pltpu.SemaphoreType.DMA
    two = LAYERS
    scratch = [
        vm((two, depth, 3 * width), BF16),
        vm((two, width, depth), BF16),
        vm((two, depth, ff), BF16),
        vm((two, ff, depth), BF16),
        vm((rows, LANES), F32),
        vm((rows, LANES), F32),
        vm((rows, depth), BF16),
        vm((rows, depth), BF16),
        vm((two, rows, depth), BF16),
        vm((two, rows, depth), BF16),
        vm((two, 2, rows, width), BF16),
        vm((two, group, rows, 2 * width), BF16),
        vm((two, group, width, rows), BF16),
        vm((two, group, width, rows), BF16),
        vm((two, rows, width), BF16),
        vm((two, width, rows), F32),
        vm((two, 8, rows), F32),
        vm((two, rows, ff), F32),
        vm((two, rows, ff), BF16),
        vm((two, rows, 1), F32),
        vm((two, rows, 1), F32),
        vm((rows, depth), F32),
        vm((2, nt_dev, chunk, depth), BF16),
        vm((2, nt_dev, chunk, depth), BF16),
        vm((2, nt_dev, chunk, depth), BF16),
        vm((rows, depth), BF16),
        vm((rows, width), BF16),
        vm((2, rows, width), BF16),
        vm((8, rows), F32),
        vm((width, rows), F32),
        vm((two, group, rows, 2 * width), BF16),
        vm((two, group - 1, rows, 2 * width), BF16),
        vm((rows, 2 * width), F32),
        vm((rows, 3 * width), BF16),
        vm((rows, ff), BF16),
        vm((rows, depth), F32),
        vm((two, 2, half, grow, early), BF16),
        vm((two, 2, half, grow, late), BF16),
        vm((two, half, grow, early), BF16),
        vm((two, half, grow, late), BF16),
        vm((two, nx - 1, 2, grow, early), BF16),
        vm((two, nx - 1, 2, grow, late), BF16),
        vm((two, grow, early), BF16),
        vm((two, grow, late), BF16),
        vm((two, grow, early), BF16),
        vm((two, grow, late), BF16),
        vm((two, grow, early), F32),
        vm((two, grow, late), F32),
        vm((two, 8, depth), F32),
        vm((two, 8, depth), F32),
        vm((half - 1, two, 8, depth), F32),
        vm((nt_dev - 1, two, 8, depth), F32),
        vm((5, 8, depth), F32),
        dma((16,)),
        dma((two, group - 1)),
        dma((two, group - 1)),
        dma((two, group - 1)),
        dma((two, group - 1)),
        dma((2, 2, nt_dev)),
        dma((2, 2, nt_dev)),
        dma((two, 2)),
        dma((two, 2)),
        dma((two, 2, nx - 1)),
        dma((two, 2, nx - 1)),
        dma((two, 2)),
        dma((two, 2)),
        dma(()),
        dma(()),
        dma((half - 1,)),
        dma((half - 1,)),
        dma((nt_dev - 1,)),
        dma((nt_dev - 1,)),
    ]
    here = pl.BlockSpec(memory_space=pltpu.VMEM)
    away = pl.BlockSpec(memory_space=pl.ANY)
    shapes = [
        (rows, depth),
        (rows, depth),
        (two, 2, depth),
        (two, 2, depth),
        (3, two, width),
        (two, depth),
        (two, ff),
        (two, depth),
        (two, 3, grow, width),
        (two, grow, width),
        (two, grow, ff),
        (two, grow, ff),
    ]
    out = pl.pallas_call(
        functools.partial(step_kernel, nt_dev, nd),
        out_shape=[jax.ShapeDtypeStruct(s, F32) for s in shapes],
        in_specs=[away, away, here, here, away, here, away, here, away, here, away, here, away, away],
        out_specs=[here] * len(shapes),
        scratch_shapes=scratch,
        compiler_params=pltpu.CompilerParams(
            collective_id=0, has_side_effects=True, vmem_limit_bytes=64 * 1024 * 1024 - 65536
        ),
    )(
        tokens,
        cotangent,
        ln_gain,
        ln_bias,
        w_qkv.transpose(0, 2, 1, 3),
        b_qkv.transpose(1, 0, 2),
        w_out,
        b_out,
        w_in,
        b_in,
        w_down,
        b_down,
        jnp.asarray(cosine),
        jnp.asarray(sine),
    )
    x, g, gain, bias, bqkv, bout, b_in_g, bdown, wq, wo, wi, wd = out
    return (
        x,
        g,
        gain,
        bias,
        wq.transpose(0, 2, 1, 3),
        bqkv.transpose(1, 0, 2),
        wo.transpose(0, 2, 1),
        bout,
        wi,
        b_in_g,
        wd.transpose(0, 2, 1),
        bdown,
    )


def solution(mesh):
    return jax.shard_map(
        functools.partial(on_device, mesh.shape["tensor"], mesh.shape["dp"]),
        mesh=mesh,
        in_specs=(
            P("dp", None),
            P("dp", None),
            P(),
            P(),
            P(None, None, None, "tensor"),
            P(None, None, "tensor"),
            P(None, "tensor", None),
            P(),
            P(None, None, "tensor"),
            P(None, "tensor"),
            P(None, "tensor", None),
            P(),
        ),
        out_specs=(
            P("dp", None),
            P("dp", None),
            P(),
            P(),
            P(None, "dp", None, "tensor"),
            P(None, None, "tensor"),
            P(None, "tensor", "dp"),
            P(),
            P(None, "dp", "tensor"),
            P(None, "tensor"),
            P(None, "tensor", "dp"),
            P(),
        ),
        check_vma=False,
    )
```

time: 1170 us -> 212 us (0.18); the launches traced: 1150 us -> 212 us
  waiting for transfers between devices: 809 us -> 0 us
  Pallas kernels: 0 us -> 200 us
  matrix products: 96.1 us -> 0 us
  blocking collectives: 83.7 us -> 0 us
  starting transfers between devices: 64.2 us -> 0 us
  other arithmetic: 50.5 us -> 0 us
  local copies, waits for them, and re-layouts: 31.6 us -> 11 us
  between operations: 16 us -> 0.74 us
    psum x3 -> x0, waiting for transfers between devices: 392 us -> none  [the longest x2 294 us: on_device(): summed = lax.psum(branch, 'tensor')]
    reduce_scatter x8 -> x0, waiting for transfers between devices: 384 us -> none  [the longest x2 128 us: on_device(): lax.psum_scatter(grad_wdown, 'dp', scatter_dimension=1, tiled=True)]
    pallas_call x0 -> x1, Pallas kernels: none -> 200 us  [on_device(): pl.pallas_call(functools.partial(step_kernel, nt_dev, nd), out_shape=[jax...]
    psum x2 -> x0, blocking collectives: 83.7 us -> none  [the longest x1 52.2 us: on_device(): lax.psum((gain_stack, bias_stack, bqkv_stack, resid_stack, bin_stack), 'dp')]
    dot_general x32 -> x0, matrix products: 81.4 us -> none  [the longest x2 10.3 us: on_device(): jnp.einsum('hts,shd->thd', probs_r, value_all, preferred_element_type=jnp...]
    ppermute x24 -> x0, starting transfers between devices: 62.8 us -> none  [passed_along(): return lax.ppermute(block, axis, route)]
    ppermute x24 -> x0, waiting for transfers between devices: 32.5 us -> none  [passed_along(): return lax.ppermute(block, axis, route)]
    reduce_sum x14 -> x0, other arithmetic: 21.6 us -> none  [the longest x2 7.19 us: on_device(): grad_bias_res = jnp.sum(branch_grad, axis=0, dtype=jnp.float32)]
  transfers between devices with their start and end apart: 35 -> 0, of which waited for: 16 -> 0; matrix products, arithmetic and copies ran while one was open for 10% -> 0% of each run, Pallas kernels for 0% -> 0%
where the time goes in v1:
time: 212 us
  Pallas kernels  200 us (94%)
  local copies, waits for them, and re-layouts  11 us (5%)
    pallas_call x1, Pallas kernels, on_device(): pl.pallas_call(functools.partial(step_kernel, nt_dev, nd), out_shape=[jax...  200 us
    unnamed x34, local copies, waits for them, and re-layouts  11 us

profile of v1, /device:TPU:1, one launch (start us, length us, event | category | flops | bytes accessed | tf_op | source)
XLA Modules:
  0.0 212.0 jit_solution(18231214486395959023)
XLA Ops:
  0.6 200.3 %shard_map.229 = (f32[512,1024]{1,0:T(8,128)}, f32[512,1024]{1,0:T(8,128)}, f32[2,2,1024]{2,1,0:T(2,128)}, f32[2,2,1024]{2,1,0:T(2,128)}, f32[3,2,128]{2,1,0:T(2...) custom-call(bf16[512,1024]{1,0:T(8,128)(2,1)} %refs_0_.1, ...), custom_call_target="tpu_custom_call" | custom-call | tf_op jit(solution)/shard_map/pallas_call | solution.py:939
  200.9 0.0 copy-start
  200.9 3.3 %copy.38 = f32[512,1024]{1,0:T(8,128)} copy(f32[512,1024]{1,0:T(8,128)} %get-tuple-element.48) | data formatting | bytes 4194304
  204.2 0.0 copy-done
  204.2 0.0 copy-start.6
  204.2 0.0 copy-start.5
  204.2 0.0 copy-start.3
  204.3 0.0 copy-start.10
  204.3 0.0 copy-start.4
  204.3 0.0 copy-start.8
  204.3 0.0 copy-start.2
  204.3 0.0 copy-start.9
  204.3 0.0 copy-start.1
  204.3 0.0 copy-start.7
  204.3 1.3 copy.39
  205.6 0.0 copy-done.6
  205.6 0.6 copy.40
  206.3 0.0 copy-done.5
  206.3 0.6 copy.41
  206.9 0.0 copy-done.3
  206.9 0.7 copy.42
  207.5 0.0 copy-done.10
  207.5 0.6 copy.43
  208.1 0.0 copy-done.4
  208.1 0.6 copy.44
  208.8 0.0 copy-done.8
  208.8 0.6 copy.45
  209.4 0.0 copy-done.2
  209.4 0.7 copy.46
  210.1 0.0 copy-done.9
  210.1 0.6 copy.47
  210.7 0.0 copy-done.1
  210.7 0.7 copy.48
  211.4 0.0 copy-done.7
  211.4 0.6 copy.49
Async XLA Ops:
  200.9 3.3 %copy-start = (f32[512,1024]{1,0:T(8,128)S(1)}, f32[512,1024]{1,0:T(8,128)}, u32[]{:S(2)}) copy-start(f32[512,1024]{1,0:T(8,128)} %get-tuple-element.49) | copy-start | bytes 6291460
  204.2 1.4 copy-start.6
  204.2 2.0 copy-start.5
  204.2 2.6 %copy-start.3 = (f32[2,3,64,128]{3,2,1,0:T(8,128)S(1)}, f32[2,3,64,128]{3,2,1,0:T(8,128)}, u32[]{:S(2)}) copy-start(f32[2,3,64,128]{3,2,1,0:T(8,128)} %get-tuple-element.28) | copy-start | bytes 589828
  204.3 3.3 %copy-start.10 = (f32[3,2,128]{2,1,0:T(2,128)S(1)}, f32[3,2,128]{2,1,0:T(2,128)}, u32[]{:S(2)}) copy-start(f32[3,2,128]{2,1,0:T(2,128)} %get-tuple-element.29) | copy-start | bytes 9220
  204.3 3.9 %copy-start.4 = (f32[2,64,128]{2,1,0:T(8,128)S(1)}, f32[2,64,128]{2,1,0:T(8,128)}, u32[]{:S(2)}) copy-start(f32[2,64,128]{2,1,0:T(8,128)} %get-tuple-element.30) | copy-start | bytes 196612
  204.3 4.5 %copy-start.8 = (f32[2,1024]{1,0:T(2,128)S(1)}, f32[2,1024]{1,0:T(2,128)}, u32[]{:S(2)}) copy-start(f32[2,1024]{1,0:T(2,128)} %get-tuple-element.55) | copy-start | bytes 24580
  204.3 5.1 %copy-start.2 = (f32[2,64,512]{2,1,0:T(8,128)S(1)}, f32[2,64,512]{2,1,0:T(8,128)}, u32[]{:S(2)}) copy-start(f32[2,64,512]{2,1,0:T(8,128)} %get-tuple-element.56) | copy-start | bytes 786436
  204.3 5.8 %copy-start.9 = (f32[2,512]{1,0:T(2,128)S(1)}, f32[2,512]{1,0:T(2,128)}, u32[]{:S(2)}) copy-start(f32[2,512]{1,0:T(2,128)} %get-tuple-element.57) | copy-start | bytes 12292
  204.3 6.4 %copy-start.1 = (f32[2,64,512]{2,1,0:T(8,128)S(1)}, f32[2,64,512]{2,1,0:T(8,128)}, u32[]{:S(2)}) copy-start(f32[2,64,512]{2,1,0:T(8,128)} %get-tuple-element.34) | copy-start | bytes 786436
  204.3 7.1 %copy-start.7 = (f32[2,1024]{1,0:T(2,128)S(1)}, f32[2,1024]{1,0:T(2,128)}, u32[]{:S(2)}) copy-start(f32[2,1024]{1,0:T(2,128)} %get-tuple-element.59) | copy-start | bytes 24580

commit v2 on v1

--- a/solution.py
+++ b/solution.py
@@ -21,6 +21,7 @@
 KT = 256
 MT = 256
 ST = 32
+PARTS = 8
 
 
 def nn(a, b):
@@ -84,14 +85,15 @@
 def step_kernel(nt_dev, nd, *refs):
     names = (
         "tok", "cot", "gain", "bias", "wqkv_h", "bqkv", "wout_h", "bout", "win_h", "bin",
-        "wdown_h", "bdown", "cos_h", "sin_h", "x", "g", "ogain", "obias", "obqkv", "obout",
+        "wdown_h", "bdown", "cos_h", "sin_h", "ox", "og", "ogain", "obias", "obqkv", "obout",
         "obin", "obdown", "oq", "oo", "oi", "od", "wqkv", "wout", "win", "wdown", "cosine",
-        "sine", "xt", "ct", "h0", "h1", "qm", "kv", "kt", "vt", "ob", "ot", "lse", "u", "act",
-        "mu", "rs", "part", "psend", "rsbuf", "agbuf", "dz", "do", "dom", "delta", "dqt",
-        "dkvo", "dkvi", "own", "dqkv", "du", "dh0", "ge", "gl", "r1e", "r1l", "r2e", "r2l",
-        "s3e", "s3l", "r3e", "r3l", "k3e", "k3l", "sm", "sr1", "sr2", "sr3", "lnacc", "lsem",
-        "kvs", "kvr", "dks", "dkr", "ars", "arr", "g1s", "g1r", "g2s", "g2r", "g3s", "g3r",
-        "s1s", "s1r", "s2s", "s2r", "s3s", "s3r",
+        "sine", "x", "g", "xt", "ct", "h0", "h1", "qm", "kv", "kt", "vt", "ob", "ot", "lse",
+        "u", "act", "mu", "rs", "part", "psend", "rsbuf", "agbuf", "dz", "do", "dom", "delta",
+        "dqt", "dkvo", "dkvi", "own", "dqkv", "du", "dact", "binacc", "dh0", "ge", "gl", "r1e",
+        "r1l", "r2e", "r2l", "s3e", "s3l", "r3e", "r3l", "k3e", "k3l", "ln", "other", "ln1",
+        "other1", "ln2", "other2", "lnc", "ln3", "lnall", "lnacc", "lsem", "kvs", "kvr", "dks",
+        "dkr", "ars", "arr", "g1s", "g1r", "g2s", "g2r", "g3s", "g3r", "s1s", "s1r", "s2s",
+        "s2r", "s3s", "s3r", "s4s", "s4r",
     )
     assert len(names) == len(refs)
     v = Refs()
@@ -218,61 +220,53 @@
         for k in range(1, nt_dev):
             ag_copy(s, k).start()
 
-    def ag_each(s, use):
-        def one(k, carry):
-            src = lax.rem(me_t + k, nt_dev)
-
-            @pl.when(k > 0)
-            def _():
-                remote(
-                    v.agbuf.at[s, src],
-                    v.agbuf.at[s, src],
-                    v.ars.at[s, 1, k],
-                    v.arr.at[s, 1, src],
-                    tensor=src,
-                ).wait_recv()
-
-            for i in range(chunk // ST):
-                use(
-                    pl.ds(pl.multiple_of(src * chunk + i * ST, ST), ST),
-                    v.agbuf[s, src, i * ST : (i + 1) * ST, :].astype(F32),
-                )
-            return carry
-
-        lax.fori_loop(0, nt_dev, one, 0)
+    def ag_pairs(s, first, last, use, after):
+        def one(m, carry):
+            pair = lax.rem(me_t // 2 + m, nt_dev // 2)
+            for i in range(2):
+                src = 2 * pair + i
+
+                @pl.when(src != me_t)
+                def _():
+                    remote(
+                        v.agbuf.at[s, src],
+                        v.agbuf.at[s, src],
+                        v.ars.at[s, 1, 1],
+                        v.arr.at[s, 1, src],
+                        tensor=src,
+                    ).wait_recv()
+
+                for j in range(chunk // ST):
+                    use(
+                        pl.ds(pl.multiple_of(src * chunk + j * ST, ST), ST),
+                        v.agbuf[s, src, j * ST : (j + 1) * ST, :].astype(F32),
+                    )
+            after(rows_at(pair, 2 * chunk))
+            return carry
+
+        lax.fori_loop(first, last, one, 0)
+
+    def ag_sent(s):
         for k in range(1, nt_dev):
             ag_copy(s, k).wait_send()
 
-    def kv_copy(l, s):
+    def kv_copy(l, step):
+        slot, to = [(rank, other_core), (rank, other_z), (rank - 2, other_core)][step]
+        block = v.kv.at[l, slot]
+        return remote(block, block, v.kvs.at[l, step], v.kvr.at[l, step], dp=to)
+
+    def kv_in(l, step):
+        slot = [rank - 1, rank - 2, rank - 1 - 2 * core][step]
+        block = v.kv.at[l, slot]
+        return remote(block, block, v.kvs.at[l, step], v.kvr.at[l, step], dp=other_core)
+
+    def dkv_copy(l, step):
         return remote(
-            v.kv.at[l, rank], v.kv.at[l, rank], v.kvs.at[l, s - 1], v.kvr.at[l, s - 1], dp=me_d + s
-        )
-
-    def kv_in(l, s):
-        return remote(
-            v.kv.at[l, rank - s],
-            v.kv.at[l, rank - s],
-            v.kvs.at[l, s - 1],
-            v.kvr.at[l, s - 1],
-            dp=me_d - s,
-        )
-
-    def dkv_copy(l, s):
-        return remote(
-            v.dkvo.at[l, rank - s],
-            v.dkvi.at[l, s - 1],
-            v.dks.at[l, s - 1],
-            v.dkr.at[l, s - 1],
-            dp=me_d - s,
-        )
-
-    def dkv_in(l, s):
-        return remote(
-            v.dkvo.at[l, rank],
-            v.dkvi.at[l, s - 1],
-            v.dks.at[l, s - 1],
-            v.dkr.at[l, s - 1],
-            dp=me_d + s,
+            v.dkvo.at[l, step],
+            v.dkvi.at[l, step],
+            v.dks.at[l, step],
+            v.dkr.at[l, step],
+            dp=other_z if step == 1 else other_core,
         )
 
     def transpose_block(l, b):
@@ -280,36 +274,46 @@
         v.kt[l, b] = block[:, :width].T.astype(BF16)
         v.vt[l, b] = block[:, width:].T.astype(BF16)
 
-    def qkv_and_send(l, barrier_wait):
-        for c in load_qkv[l]:
-            c.wait()
-        if l == 0:
-            load_cos.wait()
-            load_sin.wait()
-
-        def one(i, carry):
-            at = rows_at(i, MT)
-            mixed = nn(v.h0[l, at, :], v.wqkv[l])
-            cosine, sine = v.cosine[at, :], v.sine[at, :]
-            q = rotate(mixed[:, :width] + v.bqkv[0, l : l + 1, :], cosine, sine).astype(BF16)
-            k = rotate(mixed[:, width : 2 * width] + v.bqkv[1, l : l + 1, :], cosine, sine)
-            val = mixed[:, 2 * width :] + v.bqkv[2, l : l + 1, :]
-            scaled = (q.astype(F32) * 0.125).astype(BF16)
-            v.qm[l, 0, at, :] = head_only(scaled, 0)
-            v.qm[l, 1, at, :] = head_only(scaled, 1)
-            v.kv[l, rank, at, :width] = k.astype(BF16)
-            v.kv[l, rank, at, width:] = val.astype(BF16)
-            return carry
-
-        lax.fori_loop(0, rows // MT, one, 0)
-        if barrier_wait:
-            with jax.named_scope("barrier"):
-                pl.semaphore_wait(barrier, nt_dev - 1 + nd - 1)
-        for s in range(1, group):
-
-            @pl.when(rank + s < group)
-            def _():
-                kv_copy(l, s).start()
+    def qkv_rows(l, at, size):
+        mixed = nn(v.h0[l, at, :], v.wqkv[l])
+        cosine, sine = v.cosine[at, :], v.sine[at, :]
+        q = rotate(mixed[:, :width] + v.bqkv[0, l : l + 1, :], cosine, sine).astype(BF16)
+        k = rotate(mixed[:, width : 2 * width] + v.bqkv[1, l : l + 1, :], cosine, sine)
+        val = mixed[:, 2 * width :] + v.bqkv[2, l : l + 1, :]
+        scaled = (q.astype(F32) * 0.125).astype(BF16)
+        v.qm[l, 0, at, :] = head_only(scaled, 0)
+        v.qm[l, 1, at, :] = head_only(scaled, 1)
+        v.kv[l, rank, at, :width] = k.astype(BF16)
+        v.kv[l, rank, at, width:] = val.astype(BF16)
+
+    def kv_send(l):
+        @pl.when(zlo == 0)
+        def _():
+            kv_copy(l, 1).start()
+
+        @pl.when(core == 0)
+        def _():
+            kv_copy(l, 0).start()
+
+    def kv_relay(l):
+        @pl.when(zlo == 1)
+        def _():
+            kv_in(l, 1).wait_recv()
+            kv_copy(l, 2).start()
+
+    def kv_finish(l):
+        transpose_block(l, rank)
+
+        @pl.when(core == 1)
+        def _():
+            kv_in(l, 0).wait_recv()
+            transpose_block(l, rank - 1)
+
+        @pl.when(zlo == 1)
+        def _():
+            transpose_block(l, rank - 2)
+            kv_in(l, 2).wait_recv()
+            transpose_block(l, rank - 1 - 2 * core)
 
     def feed_forward(l):
         for c in load_rest[l]:
@@ -338,23 +342,17 @@
         lax.fori_loop(0, rows // MT, down, 0)
 
     def attention(l, s):
-        transpose_block(l, rank)
-        for k in range(1, group):
-
-            @pl.when(rank >= k)
-            def _():
-                kv_in(l, k).wait_recv()
-                transpose_block(l, rank - k)
-
         for qt in range(rows // QT):
             q_at = slice(qt * QT, (qt + 1) * QT)
-            for h in range(2):
-                qh = v.qm[l, h, q_at, :]
-                head_rows = slice(h * HEAD_DIM, (h + 1) * HEAD_DIM)
-
-                def block(b, carry, masked):
-                    top, total, out = carry
-                    sc = nt(v.kv[l, b, :, :width], qh)
+            head_rows = [slice(h * HEAD_DIM, (h + 1) * HEAD_DIM) for h in range(2)]
+
+            def block(b, carry, masked):
+                keys = v.kv[l, b, :, :width]
+                scores = [nt(keys, v.qm[l, h, q_at, :]) for h in range(2)]
+                result = []
+                for h in range(2):
+                    top, total, out = carry[h]
+                    sc = scores[h]
                     if masked:
                         key = lax.broadcasted_iota(jnp.int32, sc.shape, 0)
                         query = lax.broadcasted_iota(jnp.int32, sc.shape, 1) + qt * QT
@@ -363,17 +361,20 @@
                     p = jnp.exp(sc - new)
                     fade = jnp.exp(top - new)
                     total = total * fade + jnp.sum(p, axis=0, keepdims=True)
-                    out = out * fade + nn(v.vt[l, b, head_rows, :], p.astype(BF16))
-                    return new, total, out
-
-                carry = (
-                    jnp.full((1, QT), -1e30, F32),
-                    jnp.zeros((1, QT), F32),
-                    jnp.zeros((HEAD_DIM, QT), F32),
-                )
-                carry = lax.fori_loop(0, rank, functools.partial(block, masked=False), carry)
-                top, total, out = block(rank, carry, True)
-                v.ot[l, head_rows, q_at] = out / total
+                    out = out * fade + nn(v.vt[l, b, head_rows[h], :], p.astype(BF16))
+                    result.append((new, total, out))
+                return tuple(result)
+
+            start = (
+                jnp.full((1, QT), -1e30, F32),
+                jnp.zeros((1, QT), F32),
+                jnp.zeros((HEAD_DIM, QT), F32),
+            )
+            carry = lax.fori_loop(0, rank, functools.partial(block, masked=False), (start, start))
+            carry = block(rank, carry, True)
+            for h in range(2):
+                top, total, out = carry[h]
+                v.ot[l, head_rows[h], q_at] = out / total
                 v.lse[l, h : h + 1, q_at] = top + jnp.log(total)
             v.ob[l, q_at, :] = v.ot[l, :, q_at].T.astype(BF16)
             both = nn(v.ob[l, q_at, :], v.wout[l]) + v.part[q_at, :]
@@ -471,10 +472,7 @@
         v.dz[at, :] = gradient.astype(BF16)
 
     def attention_back(l):
-        v.do[...] = nt(v.dz[...], v.wout[l]).astype(BF16)
         do = v.do[...]
-        v.dom[0] = head_only(do, 0)
-        v.dom[1] = head_only(do, 1)
         product = do.astype(F32).T * v.ot[l]
         v.delta[0:1, :] = jnp.sum(product[:HEAD_DIM], axis=0, keepdims=True)
         v.delta[1:2, :] = jnp.sum(product[HEAD_DIM:], axis=0, keepdims=True)
@@ -501,24 +499,29 @@
                 v.dqt[head_rows, :] += nn(v.kt[l, b, head_rows, at], ds)
             return dk, dv
 
-        def far(b, carry):
+        def far(b, slot, received):
             def inner(i, c):
                 dk, dv = piece(b, i, False)
                 at = rows_at(i, KT)
-                v.dkvo[l, b, at, :width] = dk.astype(BF16)
-                v.dkvo[l, b, at, width:] = dv.astype(BF16)
+                if received:
+                    dk = dk + v.dkvi[l, 0, at, :width].astype(F32)
+                    dv = dv + v.dkvi[l, 0, at, width:].astype(F32)
+                v.dkvo[l, slot, at, :width] = dk.astype(BF16)
+                v.dkvo[l, slot, at, width:] = dv.astype(BF16)
                 return c
 
             lax.fori_loop(0, rows // KT, inner, 0)
-            for s in range(1, group):
-
-                @pl.when(rank - b == s)
-                def _():
-                    dkv_copy(l, s).start()
-
-            return carry
-
-        lax.fori_loop(0, rank, far, 0)
+            dkv_copy(l, slot).start()
+
+        @pl.when(zlo == 1)
+        def _():
+            far(1 - core, 0, False)
+            dkv_copy(l, 0).wait_recv()
+            far(core, 1, True)
+
+        @pl.when(core == 1)
+        def _():
+            far(rank - 1, 2, False)
 
         def near(i, c):
             dk, dv = piece(rank, i, True)
@@ -529,32 +532,25 @@
 
         lax.fori_loop(0, rows // KT, near, 0)
 
-    def feed_forward_back(l):
-        def up(i, carry):
-            at = rows_at(i, MT)
-            v.part[at, :ff] = nt(v.dz[at, :], v.wdown[l])
-            return carry
-
-        lax.fori_loop(0, rows // MT, up, 0)
+    def back_rows(l, at, size):
+        do = nt(v.dz[at, :], v.wout[l]).astype(BF16)
+        v.do[at, :] = do
+        v.dom[0, at, :] = head_only(do, 0)
+        v.dom[1, at, :] = head_only(do, 1)
+        v.dact[at, :] = nt(v.dz[at, :], v.wdown[l])
+        start = at.start if isinstance(at, pl.Slice) else at
 
         def slope(i, acc):
-            at = rows_at(i, ST)
-            u = v.u[l, at, :]
+            rows_now = pl.ds(pl.multiple_of(start + i * ST, ST), ST)
+            u = v.u[l, rows_now, :]
             inner = 0.5 * (1.0 + lax.erf(u * np.float32(0.5**0.5)))
             inner = inner + u * jnp.exp(-0.5 * u * u) * np.float32((2.0 * np.pi) ** -0.5)
-            du = (v.part[at, :ff] * inner).astype(BF16)
-            v.du[at, :] = du
+            du = (v.dact[rows_now, :] * inner).astype(BF16)
+            v.du[rows_now, :] = du
             return acc + jnp.sum(du.astype(F32).reshape(ST // 8, 8, ff), axis=0)
 
-        acc = lax.fori_loop(0, rows // ST, slope, jnp.zeros((8, ff), F32))
-        v.sm[l, 5:6, :ff] = jnp.sum(acc, axis=0, keepdims=True)
-
-        def down(i, carry):
-            at = rows_at(i, MT)
-            v.part[at, :] = nt(v.du[at, :], v.win[l])
-            return carry
-
-        lax.fori_loop(0, rows // MT, down, 0)
+        v.binacc[l] += lax.fori_loop(0, size // ST, slope, jnp.zeros((8, ff), F32))
+        v.part[at, :] = nt(v.du[at, :], v.win[l])
 
     def early_grads(l):
         def one(i, carry):
@@ -585,18 +581,18 @@
         lax.fori_loop(0, depth // (2 * grow), one, 0)
 
     def qkv_back(l):
-        for s in range(1, group):
-
-            @pl.when(rank + s < group)
+        for step, here in ((2, core == 0), (1, zlo == 0)):
+
+            @pl.when(here)
             def _():
-                dkv_in(l, s).wait_recv()
-                v.own[...] += v.dkvi[l, s - 1].astype(F32)
+                dkv_copy(l, step).wait_recv()
+                v.own[...] += v.dkvi[l, step].astype(F32)
 
         cosine, sine = v.cosine[...], -v.sine[...]
         v.dqkv[:, :width] = rotate(v.dqt[...].T * 0.125, cosine, sine).astype(BF16)
         v.dqkv[:, width : 2 * width] = rotate(v.own[:, :width], cosine, sine).astype(BF16)
         v.dqkv[:, 2 * width : 3 * width] = v.own[:, width:].astype(BF16)
-        v.sm[l, 5:6, ff : ff + 3 * width] = jnp.sum(
+        v.other[4 * l + 3 : 4 * l + 4, : 3 * width] = jnp.sum(
             v.dqkv[...].astype(F32), axis=0, keepdims=True
         )
 
@@ -636,8 +632,12 @@
             return carry
 
         lax.fori_loop(0, rows // 16, one, 0)
-        for i in range(5):
-            v.sm[l, i : i + 1, :] = jnp.sum(v.lnacc[i], axis=0, keepdims=True)
+        for i in range(4):
+            v.ln[4 * l + i : 4 * l + i + 1, :] = jnp.sum(v.lnacc[i], axis=0, keepdims=True)
+        column = jnp.sum(v.lnacc[4], axis=0, keepdims=True)
+        v.other[4 * l : 4 * l + 1, :] = column[:, :ff]
+        v.other[4 * l + 1 : 4 * l + 2, :] = column[:, ff:]
+        v.other[4 * l + 2 : 4 * l + 3, :] = jnp.sum(v.binacc[l], axis=0, keepdims=True)
 
     def stream_reduce(l):
         rs_finish(0)
@@ -652,22 +652,88 @@
             v.agbuf[0, me_t, i * 16 : (i + 1) * 16, :] = dx.astype(BF16)
         ag_start(0)
 
-    def small_core():
-        return remote(v.sm, v.sr1, v.s1s, v.s1r, dp=other_core)
-
-    def small_dp(k):
+    def small_core(i):
+        mine, theirs = [(v.ln, v.ln1), (v.other, v.other1)][i]
+        return remote(mine, theirs, v.s1s.at[i], v.s1r.at[i], dp=other_core)
+
+    def small_scatter(k):
+        to = lax.rem(me_t + k, nt_dev)
+        columns = pl.ds(pl.multiple_of(to * LANES, LANES), LANES)
+        return remote(
+            v.ln.at[:, columns], v.ln2.at[k - 1], v.s2s.at[k - 1], v.s2r.at[k - 1], tensor=to
+        )
+
+    def small_dp(k, i):
         to = lax.rem(me_d + 2 * k, nd)
-        return remote(v.sm, v.sr2.at[k - 1], v.s2s.at[k - 1], v.s2r.at[k - 1], dp=to)
-
-    def small_tensor(k):
+        mine, theirs = [(v.lnc, v.ln3), (v.other, v.other2)][i]
+        return remote(mine, theirs.at[k - 1], v.s3s.at[i, k - 1], v.s3r.at[i, k - 1], dp=to)
+
+    def small_gather(k):
         to = lax.rem(me_t + k, nt_dev)
-        return remote(
-            v.sm,
-            v.sr3.at[k - 1],
-            v.s3s.at[k - 1],
-            v.s3r.at[k - 1],
-            tensor=to,
-        )
+        block = v.lnall.at[me_t]
+        return remote(block, block, v.s4s.at[k - 1], v.s4r.at[me_t], tensor=to)
+
+    def small_start():
+        for i in range(2):
+            small_core(i).start()
+
+    def small_second():
+        for i in range(2):
+            small_core(i).wait()
+        v.ln[...] += v.ln1[...]
+        v.other[...] += v.other1[...]
+        for k in range(1, nt_dev):
+            small_scatter(k).start()
+        for k in range(1, nd // 2):
+            small_dp(k, 1).start()
+
+    def small_third():
+        mine = pl.ds(pl.multiple_of(me_t * LANES, LANES), LANES)
+        total = v.ln[:, mine]
+        for k in range(1, nt_dev):
+            small_scatter(k).wait()
+            total = total + v.ln2[k - 1]
+        v.lnc[...] = total
+        for k in range(1, nd // 2):
+            small_dp(k, 0).start()
+
+    def small_fourth():
+        total = v.lnc[...]
+        for k in range(1, nd // 2):
+            small_dp(k, 0).wait()
+            total = total + v.ln3[k - 1]
+        v.lnall[me_t] = total
+        for k in range(1, nt_dev):
+            small_gather(k).start()
+        total = v.other[...]
+        for k in range(1, nd // 2):
+            small_dp(k, 1).wait()
+            total = total + v.other2[k - 1]
+        for l in range(LAYERS):
+            for half in range(2):
+                at = slice(half * ff, (half + 1) * ff)
+                row = total[4 * l + half : 4 * l + half + 1, :]
+                v.obout[l : l + 1, at] = row
+                v.obdown[l : l + 1, at] = row
+            v.obin[l : l + 1, :] = total[4 * l + 2 : 4 * l + 3, :]
+            for c in range(3):
+                at = slice(c * width, (c + 1) * width)
+                v.obqkv[c, l : l + 1, :] = total[4 * l + 3 : 4 * l + 4, at]
+
+    def small_end():
+        for k in range(1, nt_dev):
+            src = lax.rem(me_t + k, nt_dev)
+            block = v.lnall.at[src]
+            remote(block, block, v.s4s.at[k - 1], v.s4r.at[src], tensor=src).wait()
+        for j in range(nt_dev):
+            at = slice(j * LANES, (j + 1) * LANES)
+            block = v.lnall[j]
+            for l in range(LAYERS):
+                v.ogain[l, :, at] = block[4 * l : 4 * l + 2, :]
+                v.obias[l, :, at] = block[4 * l + 2 : 4 * l + 4, :]
+
+    def nothing(at):
+        pass
 
     with jax.named_scope("tok"):
         load_tok.wait()
@@ -678,12 +744,29 @@
         return carry
 
     with jax.named_scope("norm0"):
-        lax.fori_loop(0, rows // ST, first_norm, 0)
-    v.sm[...] = jnp.zeros_like(v.sm)
+        lax.fori_loop(0, rows // ST, first_norm, 0, unroll=2)
     with jax.named_scope("qkv0"):
-        qkv_and_send(0, True)
+        for c in load_qkv[0]:
+            c.wait()
+        load_cos.wait()
+        load_sin.wait()
+
+        def first_qkv(i, carry):
+            qkv_rows(0, rows_at(i, MT), MT)
+            return carry
+
+        lax.fori_loop(0, rows // MT, first_qkv, 0)
+    with jax.named_scope("barrier"):
+        pl.semaphore_wait(barrier, nt_dev - 1 + nd - 1)
+    kv_send(0)
+    v.ln[...] = jnp.zeros_like(v.ln)
+    v.other[...] = jnp.zeros_like(v.other)
+    v.binacc[...] = jnp.zeros_like(v.binacc)
     with jax.named_scope("ffn0"):
         feed_forward(0)
+    with jax.named_scope("kv0"):
+        kv_relay(0)
+        kv_finish(0)
     with jax.named_scope("attn0"):
         attention(0, 0)
     with jax.named_scope("reduce0"):
@@ -694,140 +777,179 @@
         v.x[at, :] = x
         norm_rows(1, at, x)
 
+    def next_qkv(at):
+        qkv_rows(1, at, 2 * chunk)
+
     with jax.named_scope("gather0"):
-        ag_each(0, next_stream)
-    with jax.named_scope("qkv1"):
-        qkv_and_send(1, False)
+        for c in load_qkv[1]:
+            c.wait()
+        ag_pairs(0, 0, nt_dev // 2, next_stream, next_qkv)
+        kv_send(1)
+        ag_sent(0)
     with jax.named_scope("ffn1"):
         feed_forward(1)
+    with jax.named_scope("kv1"):
+        kv_relay(1)
+        kv_finish(1)
     with jax.named_scope("attn1"):
         attention(1, 1)
 
-    with jax.named_scope("cot"):
+    with jax.named_scope("dz1"):
         load_cot.wait()
 
-    def first_gradient(i, carry):
-        at = rows_at(i, ST)
-        v.dz[at, :] = v.ct[at, :]
-        v.g[at, :] = v.ct[at, :].astype(F32)
-        return carry
-
-    with jax.named_scope("dz1"):
+        def first_gradient(i, carry):
+            at = rows_at(i, ST)
+            v.dz[at, :] = v.ct[at, :]
+            v.g[at, :] = v.ct[at, :].astype(F32)
+            return carry
+
         lax.fori_loop(0, rows // ST, first_gradient, 0)
+
+    with jax.named_scope("back1"):
+
+        def first_back(i, carry):
+            back_rows(1, rows_at(i, MT), MT)
+            return carry
+
+        lax.fori_loop(0, rows // MT, first_back, 0)
     with jax.named_scope("attn_grad1"):
         attention_back(1)
-    with jax.named_scope("ffn_grad1"):
-        feed_forward_back(1)
-    with jax.named_scope("reduce1"):
-        branch_reduce(1)
+
+    def early(l, z):
+        @pl.when(zlo == z)
+        def _():
+            early_grads(l)
+            grad_core(l, 0)
+
     with jax.named_scope("early1"):
-        early_grads(1)
-    grad_core(1, 0)
+        early(1, 0)
     with jax.named_scope("qkv_grad1"):
         qkv_back(1)
+    with jax.named_scope("early1b"):
+        early(1, 1)
     with jax.named_scope("late1"):
         late_grads(1)
-    grad_core(1, 1)
+        grad_core(1, 1)
+    with jax.named_scope("norm_grad1"):
+        norm_grads(1)
     with jax.named_scope("gx10"):
         grad_x(1, 0)
-    with jax.named_scope("norm_grad1"):
-        norm_grads(1)
     with jax.named_scope("stream_reduce1"):
         stream_reduce(1)
     with jax.named_scope("gx11"):
         grad_x(1, 1)
 
-    def last_stream(at, z):
-        v.x[at, :] = v.x[at, :] + (z + (v.bout[1:2, :] + v.bdown[1:2, :]))
-
-    with jax.named_scope("gather1"):
-        ag_each(1, last_stream)
-
     def next_gradient(at, dx):
         gradient = v.g[at, :] + dx
         v.g[at, :] = gradient
         v.dz[at, :] = gradient.astype(BF16)
 
+    def next_back(at):
+        back_rows(0, at, 2 * chunk)
+
     with jax.named_scope("gather2"):
-        ag_each(0, next_gradient)
+        ag_pairs(0, 0, nt_dev // 2, next_gradient, next_back)
+        ag_sent(0)
+    with jax.named_scope("reduce1"):
+        branch_reduce(1)
     with jax.named_scope("attn_grad0"):
         attention_back(0)
-    with jax.named_scope("gz10"):
+    with jax.named_scope("gz1"):
         grad_z(1, 0)
-    with jax.named_scope("gz11"):
         grad_z(1, 1)
-    with jax.named_scope("ffn_grad0"):
-        feed_forward_back(0)
     with jax.named_scope("early0"):
-        early_grads(0)
-    grad_core(0, 0)
-    with jax.named_scope("gend10"):
-        grad_end(1, 0)
-    with jax.named_scope("gend11"):
-        grad_end(1, 1)
+        early(0, 0)
     with jax.named_scope("qkv_grad0"):
         qkv_back(0)
+    with jax.named_scope("early0b"):
+        early(0, 1)
+    with jax.named_scope("late0"):
+        late_grads(0)
+        grad_core(0, 1)
+    with jax.named_scope("norm_grad0"):
+        norm_grads(0)
+        small_start()
     with jax.named_scope("gx00"):
         grad_x(0, 0)
-    with jax.named_scope("late0"):
-        late_grads(0)
-    grad_core(0, 1)
-    with jax.named_scope("norm_grad0"):
-        norm_grads(0)
-    small_core().start()
+
+    def last_stream(at, z):
+        v.x[at, :] = v.x[at, :] + (z + (v.bout[1:2, :] + v.bdown[1:2, :]))
+
+    store_x = pltpu.make_async_copy(v.x, v.ox, v.lsem.at[0])
+    store_g = pltpu.make_async_copy(v.g, v.og, v.lsem.at[1])
+    with jax.named_scope("small_second"):
+        small_second()
     with jax.named_scope("stream_reduce0"):
         stream_reduce(0)
     with jax.named_scope("gx01"):
         grad_x(0, 1)
-    small_core().wait()
-    v.sm[...] += v.sr1[...]
-    for k in range(1, nd // 2):
-        small_dp(k).start()
+    with jax.named_scope("small_third"):
+        small_third()
+    with jax.named_scope("gather1"):
+        ag_pairs(1, 0, nt_dev // 2, last_stream, nothing)
+        ag_sent(1)
+        store_x.start()
+    with jax.named_scope("gend1"):
+        grad_end(1, 0)
+        grad_end(1, 1)
 
     def last_gradient(at, dx):
         v.g[at, :] = v.g[at, :] + dx
 
     with jax.named_scope("gather3"):
-        ag_each(0, last_gradient)
-    for k in range(1, nd // 2):
-        small_dp(k).wait()
-    total = v.sm[...]
-    for k in range(1, nd // 2):
-        total = total + v.sr2[k - 1]
-    v.sm[...] = total
-    for k in range(1, nt_dev):
-        small_tensor(k).start()
-    with jax.named_scope("gz00"):
+        ag_pairs(0, 0, nt_dev // 4, last_gradient, nothing)
+    with jax.named_scope("small_fourth"):
+        small_fourth()
+    with jax.named_scope("gather3b"):
+        ag_pairs(0, nt_dev // 4, nt_dev // 2, last_gradient, nothing)
+        store_g.start()
+        ag_sent(0)
+    with jax.named_scope("gz0"):
         grad_z(0, 0)
-    with jax.named_scope("gz01"):
         grad_z(0, 1)
+    with jax.named_scope("small_end"):
+        small_end()
+    with jax.named_scope("gend0"):
+        grad_end(0, 0)
+        grad_end(0, 1)
+        store_x.wait()
+        store_g.wait()
     for l in range(LAYERS):
-        v.obout[l : l + 1, :] = v.sm[l, 4:5, :]
-        v.obdown[l : l + 1, :] = v.sm[l, 4:5, :]
-        v.obin[l : l + 1, :] = v.sm[l, 5:6, :ff]
-        for c in range(3):
-            v.obqkv[c, l : l + 1, :] = v.sm[l, 5:6, ff + c * width : ff + (c + 1) * width]
-    for k in range(1, nt_dev):
-        small_tensor(k).wait()
-    total = v.sm[...]
-    for k in range(1, nt_dev):
-        total = total + v.sr3[k - 1]
-    v.ogain[...] = total[:, 0:2, :]
-    v.obias[...] = total[:, 2:4, :]
-    with jax.named_scope("gend00"):
-        grad_end(0, 0)
-    with jax.named_scope("gend01"):
-        grad_end(0, 1)
-    for l in range(LAYERS):
-        for s in range(1, group):
-
-            @pl.when(rank + s < group)
+        for step, here in ((0, core == 0), (1, zlo == 0), (2, zlo == 1)):
+
+            @pl.when(here)
             def _():
-                kv_copy(l, s).wait_send()
-
-            @pl.when(rank >= s)
+                kv_copy(l, step).wait_send()
+
+        for step, here in ((0, zlo == 1), (1, zlo == 1), (2, core == 1)):
+
+            @pl.when(here)
             def _():
-                dkv_copy(l, s).wait_send()
+                dkv_copy(l, step).wait_send()
+
+
+def store_kernel(count, *refs):
+    given, kept = refs[:count], refs[count : 2 * count]
+    held = refs[2 * count : 2 * count + 2]
+    sems = refs[2 * count + 2]
+    rows = held[0].shape[0] // PARTS
+    parts = [(i, slice(j * rows, (j + 1) * rows), i * PARTS + j) for j in range(PARTS) for i in range(2)]
+    loads = [
+        pltpu.make_async_copy(given[i].at[at], held[i].at[at], sems.at[0, n]) for i, at, n in parts
+    ]
+    stores = [
+        pltpu.make_async_copy(held[i].at[at], kept[i].at[at], sems.at[1, n]) for i, at, n in parts
+    ]
+    others = [
+        pltpu.make_async_copy(given[i], kept[i], sems.at[2, i]) for i in range(2, count)
+    ]
+    for copy in loads + others:
+        copy.start()
+    for load, store in zip(loads, stores):
+        load.wait()
+        store.start()
+    for copy in stores + others:
+        copy.wait()
 
 
 def on_device(nt_dev, nd, *args):
@@ -853,6 +975,8 @@
         vm((two, ff, depth), BF16),
         vm((rows, LANES), F32),
         vm((rows, LANES), F32),
+        vm((rows, depth), F32),
+        vm((rows, depth), F32),
         vm((rows, depth), BF16),
         vm((rows, depth), BF16),
         vm((two, rows, depth), BF16),
@@ -877,11 +1001,13 @@
         vm((2, rows, width), BF16),
         vm((8, rows), F32),
         vm((width, rows), F32),
-        vm((two, group, rows, 2 * width), BF16),
-        vm((two, group - 1, rows, 2 * width), BF16),
+        vm((two, 3, rows, 2 * width), BF16),
+        vm((two, 3, rows, 2 * width), BF16),
         vm((rows, 2 * width), F32),
         vm((rows, 3 * width), BF16),
         vm((rows, ff), BF16),
+        vm((rows, ff), F32),
+        vm((two, 8, ff), F32),
         vm((rows, depth), F32),
         vm((two, 2, half, grow, early), BF16),
         vm((two, 2, half, grow, late), BF16),
@@ -895,16 +1021,21 @@
         vm((two, grow, late), BF16),
         vm((two, grow, early), F32),
         vm((two, grow, late), F32),
-        vm((two, 8, depth), F32),
-        vm((two, 8, depth), F32),
-        vm((half - 1, two, 8, depth), F32),
-        vm((nt_dev - 1, two, 8, depth), F32),
+        vm((8, depth), F32),
+        vm((8, ff), F32),
+        vm((8, depth), F32),
+        vm((8, ff), F32),
+        vm((nt_dev - 1, 8, LANES), F32),
+        vm((half - 1, 8, ff), F32),
+        vm((8, LANES), F32),
+        vm((half - 1, 8, LANES), F32),
+        vm((nt_dev, 8, LANES), F32),
         vm((5, 8, depth), F32),
         dma((16,)),
-        dma((two, group - 1)),
-        dma((two, group - 1)),
-        dma((two, group - 1)),
-        dma((two, group - 1)),
+        dma((two, 3)),
+        dma((two, 3)),
+        dma((two, 3)),
+        dma((two, 3)),
         dma((2, 2, nt_dev)),
         dma((2, 2, nt_dev)),
         dma((two, 2)),
@@ -913,12 +1044,14 @@
         dma((two, 2, nx - 1)),
         dma((two, 2)),
         dma((two, 2)),
-        dma(()),
-        dma(()),
-        dma((half - 1,)),
-        dma((half - 1,)),
+        dma((2,)),
+        dma((2,)),
         dma((nt_dev - 1,)),
         dma((nt_dev - 1,)),
+        dma((2, half - 1)),
+        dma((2, half - 1)),
+        dma((nt_dev - 1,)),
+        dma((nt_dev,)),
     ]
     here = pl.BlockSpec(memory_space=pltpu.VMEM)
     away = pl.BlockSpec(memory_space=pl.ANY)
@@ -940,7 +1073,7 @@
         functools.partial(step_kernel, nt_dev, nd),
         out_shape=[jax.ShapeDtypeStruct(s, F32) for s in shapes],
         in_specs=[away, away, here, here, away, here, away, here, away, here, away, here, away, away],
-        out_specs=[here] * len(shapes),
+        out_specs=[away] * 2 + [here] * (len(shapes) - 2),
         scratch_shapes=scratch,
         compiler_params=pltpu.CompilerParams(
             collective_id=0, has_side_effects=True, vmem_limit_bytes=64 * 1024 * 1024 - 65536
@@ -961,6 +1094,13 @@
         jnp.asarray(cosine),
         jnp.asarray(sine),
     )
+    out = pl.pallas_call(
+        functools.partial(store_kernel, len(shapes)),
+        out_shape=[jax.ShapeDtypeStruct(s, F32) for s in shapes],
+        in_specs=[away] * 2 + [here] * (len(shapes) - 2),
+        out_specs=[away] * len(shapes),
+        scratch_shapes=[vm((rows, depth), F32), vm((rows, depth), F32), dma((3, 16))],
+    )(*out)
     x, g, gain, bias, bqkv, bout, b_in_g, bdown, wq, wo, wi, wd = out
     return (
         x,

time: 212 us -> 191 us (0.901); the launches traced: 212 us -> 189 us
  Pallas kernels: 200 us -> 188 us
  local copies, waits for them, and re-layouts: 11 us -> 0 us
    pallas_call x1, Pallas kernels: 200 us -> 182 us  [on_device(): pl.pallas_call(functools.partial(step_kernel, nt_dev, nd), out_shape=[jax...]
    unnamed x34 -> x0, local copies, waits for them, and re-layouts: 11 us -> none
    pallas_call x0 -> x1, Pallas kernels: none -> 5.68 us  [on_device(): pl.pallas_call(functools.partial(store_kernel, len(shapes)), out_shape=[j...]
where the time goes in v2:
time: 191 us; the launch traced here: 189 us
  Pallas kernels  188 us (98%)
    pallas_call x1, Pallas kernels, on_device(): pl.pallas_call(functools.partial(step_kernel, nt_dev, nd), out_shape=[jax...  182 us
    pallas_call x1, Pallas kernels, on_device(): pl.pallas_call(functools.partial(store_kernel, len(shapes)), out_shape=[j...  5.68 us

profile of v2, /device:TPU:1, one launch (start us, length us, event | category | flops | bytes accessed | tf_op | source)
XLA Modules:
  0.0 188.7 jit_solution(11505417264884524780)
XLA Ops:
  0.6 182.2 %shard_map.229 = (f32[512,1024]{1,0:T(8,128)}, f32[512,1024]{1,0:T(8,128)}, f32[2,2,1024]{2,1,0:T(2,128)}, f32[2,2,1024]{2,1,0:T(2,128)}, f32[3,2,128]{2,1,0:T(2...) custom-call(bf16[512,1024]{1,0:T(8,128)(2,1)} %refs_0_.1, ...), custom_call_target="tpu_custom_call" | custom-call | tf_op jit(solution)/shard_map/pallas_call | solution.py:1072
  182.9 5.7 %shard_map.230 = (f32[512,1024]{1,0:T(8,128)}, f32[512,1024]{1,0:T(8,128)}, f32[2,2,1024]{2,1,0:T(2,128)}, f32[2,2,1024]{2,1,0:T(2,128)}, f32[3,2,128]{2,1,0:T(2...) custom-call(f32[512,1024]{1,0:T(8,128)} %get-tuple-element.36.refs_0, ...), custom_call_target="tpu_custom_call" | custom-call | tf_op jit(solution)/shard_map/pallas_call | solution.py:1097

commit v3 on v2

--- a/solution.py
+++ b/solution.py
@@ -88,12 +88,12 @@
         "wdown_h", "bdown", "cos_h", "sin_h", "ox", "og", "ogain", "obias", "obqkv", "obout",
         "obin", "obdown", "oq", "oo", "oi", "od", "wqkv", "wout", "win", "wdown", "cosine",
         "sine", "x", "g", "xt", "ct", "h0", "h1", "qm", "kv", "kt", "vt", "ob", "ot", "lse",
-        "u", "act", "mu", "rs", "part", "psend", "rsbuf", "agbuf", "dz", "do", "dom", "delta",
-        "dqt", "dkvo", "dkvi", "own", "dqkv", "du", "dact", "binacc", "dh0", "ge", "gl", "r1e",
-        "r1l", "r2e", "r2l", "s3e", "s3l", "r3e", "r3l", "k3e", "k3l", "ln", "other", "ln1",
-        "other1", "ln2", "other2", "lnc", "ln3", "lnall", "lnacc", "lsem", "kvs", "kvr", "dks",
-        "dkr", "ars", "arr", "g1s", "g1r", "g2s", "g2r", "g3s", "g3r", "s1s", "s1r", "s2s",
-        "s2r", "s3s", "s3r", "s4s", "s4r",
+        "u", "act", "mu", "rs", "part", "psend", "ra", "rb", "sa", "sb", "r2a", "r2b", "agbuf",
+        "dz", "do", "dom", "delta", "dqt", "dkvo", "dkvi", "own", "dqkv", "du", "dact",
+        "binacc", "dh0", "ge", "gl", "r1e", "r1l", "r2e", "r2l", "s3e", "s3l", "r3e", "r3l",
+        "k3e", "k3l", "ln", "other", "ln1", "other1", "ln2", "other2", "lnc", "ln3", "lnall",
+        "lnacc", "lsem", "kvs", "kvr", "dks", "dkr", "ars", "arr", "g1s", "g1r", "g2s", "g2r",
+        "g3s", "g3r", "s1s", "s1r", "s2s", "s2r", "s3s", "s3r", "s4s", "s4r",
     )
     assert len(names) == len(refs)
     v = Refs()
@@ -112,6 +112,11 @@
     core = lax.rem(me_d, 2)
     zlo = lax.rem(me_d // 2, 2)
     xc = me_d // group
+    ny = nt_dev // 2
+    hd = depth // 2
+    yy = me_t // 2
+    zh = lax.rem(me_t, 2)
+    other_zh = me_t + 1 - 2 * zh
     other_core = me_d + 1 - 2 * core
     other_z = me_d + 2 - 4 * zlo
 
@@ -171,75 +176,135 @@
             return v.xt[at, :].astype(F32)
         return v.x[at, :]
 
-    def rs_copy(s, j):
-        return remote(
-            v.psend.at[s, j],
-            v.rsbuf.at[s, me_t],
-            v.ars.at[s, 0, j],
-            v.arr.at[s, 0, me_t],
-            tensor=j,
+    def at_y(k):
+        return lax.rem(yy + k, ny)
+
+    def copy_of(s, src, dst, sem, to):
+        return remote(src, dst, v.ars.at[s, sem], v.arr.at[s, sem], tensor=to)
+
+    def a1(s, k):
+        to = at_y(k)
+        return copy_of(
+            s, v.psend.at[s, 0, pl.ds(2 * to, 2)], v.ra.at[s, k - 1], k - 1, 2 * to + zh
         )
 
-    def rs_start(s, j):
-        @pl.when(j != me_t)
+    def b1(s, m):
+        to = at_y(m)
+        return copy_of(
+            s, v.psend.at[s, 1, 2 * to + 1 - zh], v.rb.at[s, to], ny - 2 + m, other_zh
+        )
+
+    def a2(s):
+        return copy_of(s, v.sa.at[s], v.r2a.at[s], 2 * ny - 1, other_zh)
+
+    def b2(s, k):
+        return copy_of(
+            s, v.sb.at[s, k - 1], v.r2b.at[s, k - 1], 2 * ny - 1 + k, 2 * at_y(k) + zh
+        )
+
+    def rs_pair(s, m):
+        b1(s, m).start()
+
+        @pl.when(m < ny)
         def _():
-            rs_copy(s, j).start()
+            a1(s, m).start()
+
+    def rs_forward(s):
+        for m in range(1, ny):
+            b1(s, m).wait_recv()
+            to = at_y(m)
+            v.sb[s, m - 1] = (
+                v.psend[s, 1, 2 * to + zh].astype(F32) + v.rb[s, to].astype(F32)
+            ).astype(BF16)
+            b2(s, m).start()
+        for k in range(1, ny):
+            a1(s, k).wait_recv()
+        total = v.psend[s, 0, other_zh].astype(F32)
+        for k in range(1, ny):
+            total = total + v.ra[s, k - 1, 1 - zh].astype(F32)
+        v.sa[s] = total.astype(BF16)
+        a2(s).start()
+        b1(s, ny).wait_recv()
 
     def rs_finish(s):
-        v.rsbuf[s, me_t] = v.psend[s, me_t]
-
-        def one(k, carry):
-            src = lax.rem(me_t + k, nt_dev)
-            remote(
-                v.psend.at[s, src],
-                v.rsbuf.at[s, src],
-                v.ars.at[s, 0, src],
-                v.arr.at[s, 0, src],
-                tensor=src,
-            ).wait()
-            return carry
-
-        lax.fori_loop(1, nt_dev, one, 0)
+        a2(s).wait()
+        for k in range(1, ny):
+            b2(s, k).wait()
+            a1(s, k).wait_send()
+        for m in range(1, ny + 1):
+            b1(s, m).wait_send()
 
     def rs_sum(s, at):
-        total = v.rsbuf[s, 0, at, :].astype(F32)
-        for k in range(1, nt_dev):
-            total = total + v.rsbuf[s, k, at, :].astype(F32)
-        return total
-
-    def ag_copy(s, k):
-        return remote(
-            v.agbuf.at[s, me_t],
-            v.agbuf.at[s, me_t],
-            v.ars.at[s, 1, k],
-            v.arr.at[s, 1, me_t],
-            tensor=lax.rem(me_t + k, nt_dev),
-        )
+        first = v.psend[s, 0, me_t, at, :].astype(F32) + v.r2a[s, at, :].astype(F32)
+        second = v.psend[s, 1, me_t, at, :].astype(F32) + v.rb[s, yy, at, :].astype(F32)
+        for k in range(1, ny):
+            first = first + v.ra[s, k - 1, zh, at, :].astype(F32)
+            second = second + v.r2b[s, k - 1, at, :].astype(F32)
+        return jnp.concatenate([first, second], axis=1)
+
+    def ag_copy(s, half, chunk_at, sem, to):
+        block = v.agbuf.at[s, half, chunk_at]
+        return copy_of(s, block, block, sem, to)
+
+    ag0 = 3 * ny - 1
+
+    def gz(s):
+        return ag_copy(s, 0, me_t, ag0, other_zh)
+
+    def gy(s, k):
+        return ag_copy(s, 0, me_t, ag0 + k, 2 * at_y(k) + zh)
+
+    def fy(s, k):
+        return ag_copy(s, 0, other_zh, ag0 + ny - 1 + k, 2 * at_y(k) + zh)
+
+    def by(s, k):
+        return ag_copy(s, 1, me_t, ag0 + 2 * ny - 2 + k, 2 * at_y(k) + zh)
+
+    def bz(s, m):
+        return ag_copy(s, 1, 2 * at_y(m) + zh, ag0 + 3 * ny - 2 + m, other_zh)
+
+    def arrived(s, half, chunk_at, sem):
+        ag_copy(s, half, chunk_at, sem, other_zh).wait_recv()
+
+    def ag_put(s, at, value):
+        v.agbuf[s, 0, me_t, at, :] = value[:, :hd].astype(BF16)
+        v.agbuf[s, 1, me_t, at, :] = value[:, hd:].astype(BF16)
 
     def ag_start(s):
-        for k in range(1, nt_dev):
-            ag_copy(s, k).start()
+        gz(s).start()
+        for k in range(1, ny):
+            by(s, k).start()
+        bz(s, 0).start()
+        for k in range(1, ny):
+            gy(s, k).start()
+
+    def ag_forward(s):
+        arrived(s, 0, other_zh, ag0)
+        for k in range(1, ny):
+            fy(s, k).start()
+        for k in range(1, ny):
+            arrived(s, 1, 2 * at_y(ny - k) + zh, ag0 + 2 * ny - 2 + k)
+            bz(s, ny - k).start()
 
     def ag_pairs(s, first, last, use, after):
         def one(m, carry):
-            pair = lax.rem(me_t // 2 + m, nt_dev // 2)
+            pair = at_y(m)
+
+            @pl.when(m > 0)
+            def _():
+                arrived(s, 0, 2 * pair + zh, ag0 + ny - m)
+                arrived(s, 0, 2 * pair + 1 - zh, ag0 + 2 * ny - 1 - m)
+
+            arrived(s, 1, 2 * pair + 1 - zh, ag0 + 3 * ny - 2 + m)
             for i in range(2):
                 src = 2 * pair + i
-
-                @pl.when(src != me_t)
-                def _():
-                    remote(
-                        v.agbuf.at[s, src],
-                        v.agbuf.at[s, src],
-                        v.ars.at[s, 1, 1],
-                        v.arr.at[s, 1, src],
-                        tensor=src,
-                    ).wait_recv()
-
                 for j in range(chunk // ST):
+                    at = slice(j * ST, (j + 1) * ST)
                     use(
                         pl.ds(pl.multiple_of(src * chunk + j * ST, ST), ST),
-                        v.agbuf[s, src, j * ST : (j + 1) * ST, :].astype(F32),
+                        jnp.concatenate(
+                            [v.agbuf[s, 0, src, at, :], v.agbuf[s, 1, src, at, :]], axis=1
+                        ).astype(F32),
                     )
             after(rows_at(pair, 2 * chunk))
             return carry
@@ -247,8 +312,13 @@
         lax.fori_loop(first, last, one, 0)
 
     def ag_sent(s):
-        for k in range(1, nt_dev):
-            ag_copy(s, k).wait_send()
+        gz(s).wait_send()
+        bz(s, 0).wait_send()
+        for k in range(1, ny):
+            gy(s, k).wait_send()
+            fy(s, k).wait_send()
+            by(s, k).wait_send()
+            bz(s, k).wait_send()
 
     def kv_copy(l, step):
         slot, to = [(rank, other_core), (rank, other_z), (rank - 2, other_core)][step]
@@ -378,18 +448,20 @@
                 v.lse[l, h : h + 1, q_at] = top + jnp.log(total)
             v.ob[l, q_at, :] = v.ot[l, :, q_at].T.astype(BF16)
             both = nn(v.ob[l, q_at, :], v.wout[l]) + v.part[q_at, :]
+            both = both.astype(BF16)
             first = qt * QT // chunk
-            v.psend[s, first : first + QT // chunk] = both.astype(BF16).reshape(
-                QT // chunk, chunk, depth
-            )
-            for j in range(first, first + QT // chunk):
-                rs_start(s, j)
+            for half in range(2):
+                v.psend[s, half, first : first + QT // chunk] = both[
+                    :, half * hd : (half + 1) * hd
+                ].reshape(QT // chunk, chunk, hd)
+            for pair in range(first // 2, (first + QT // chunk) // 2):
+                rs_pair(s, lax.rem(pair - yy - 1 + 2 * ny, ny) + 1)
 
     def branch_reduce(s):
         rs_finish(s)
         for i in range(chunk // 16):
             at = slice(i * 16, (i + 1) * 16)
-            v.agbuf[s, me_t, at, :] = rs_sum(s, at).astype(BF16)
+            ag_put(s, at, rs_sum(s, at))
         ag_start(s)
 
     grads = {0: (v.ge, v.r1e, v.r2e, v.s3e, v.r3e, v.k3e), 1: (v.gl, v.r1l, v.r2l, v.s3l, v.r3l, v.k3l)}
@@ -603,16 +675,21 @@
 
         lax.fori_loop(0, rows // MT, one, 0)
 
-        def send(k, carry):
-            j = lax.rem(me_t + k, nt_dev)
-            for i in range(chunk // ST):
-                at = pl.ds(pl.multiple_of(j * chunk + i * ST, ST), ST)
+        def send(m, carry):
+            pair = at_y(m)
+            for i in range(2 * chunk // ST):
+                at = pl.ds(pl.multiple_of(pair * 2 * chunk + i * ST, ST), ST)
                 both = v.dh0[at, :] * v.gain[l, 0:1, :] + v.part[at, :] * v.gain[l, 1:2, :]
-                v.psend[0, j, i * ST : (i + 1) * ST, :] = both.astype(BF16)
-            rs_start(0, j)
+                both = both.astype(BF16)
+                part = slice(i * ST % chunk, i * ST % chunk + ST)
+                for half in range(2):
+                    v.psend[0, half, 2 * pair + i * ST // chunk, part, :] = both[
+                        :, half * hd : (half + 1) * hd
+                    ]
+            rs_pair(0, m)
             return carry
 
-        lax.fori_loop(1, nt_dev + 1, send, 0)
+        lax.fori_loop(1, ny + 1, send, 0)
 
     def norm_grads(l):
         v.lnacc[...] = jnp.zeros_like(v.lnacc)
@@ -649,7 +726,7 @@
             mean = jnp.mean(gd, axis=-1, keepdims=True)
             along = jnp.mean(gd * xhat, axis=-1, keepdims=True)
             dx = r * (gd - mean - xhat * along)
-            v.agbuf[0, me_t, i * 16 : (i + 1) * 16, :] = dx.astype(BF16)
+            ag_put(0, slice(i * 16, (i + 1) * 16), dx)
         ag_start(0)
 
     def small_core(i):
@@ -769,6 +846,8 @@
         kv_finish(0)
     with jax.named_scope("attn0"):
         attention(0, 0)
+    with jax.named_scope("forward0"):
+        rs_forward(0)
     with jax.named_scope("reduce0"):
         branch_reduce(0)
 
@@ -783,7 +862,8 @@
     with jax.named_scope("gather0"):
         for c in load_qkv[1]:
             c.wait()
-        ag_pairs(0, 0, nt_dev // 2, next_stream, next_qkv)
+        ag_forward(0)
+        ag_pairs(0, 0, ny, next_stream, next_qkv)
         kv_send(1)
         ag_sent(0)
     with jax.named_scope("ffn1"):
@@ -821,6 +901,8 @@
             early_grads(l)
             grad_core(l, 0)
 
+    with jax.named_scope("forward1"):
+        rs_forward(1)
     with jax.named_scope("early1"):
         early(1, 0)
     with jax.named_scope("qkv_grad1"):
@@ -830,6 +912,8 @@
     with jax.named_scope("late1"):
         late_grads(1)
         grad_core(1, 1)
+    with jax.named_scope("forward"):
+        rs_forward(0)
     with jax.named_scope("norm_grad1"):
         norm_grads(1)
     with jax.named_scope("gx10"):
@@ -848,12 +932,15 @@
         back_rows(0, at, 2 * chunk)
 
     with jax.named_scope("gather2"):
-        ag_pairs(0, 0, nt_dev // 2, next_gradient, next_back)
+        ag_forward(0)
+        ag_pairs(0, 0, ny, next_gradient, next_back)
         ag_sent(0)
     with jax.named_scope("reduce1"):
         branch_reduce(1)
     with jax.named_scope("attn_grad0"):
         attention_back(0)
+    with jax.named_scope("forward1b"):
+        ag_forward(1)
     with jax.named_scope("gz1"):
         grad_z(1, 0)
         grad_z(1, 1)
@@ -866,6 +953,8 @@
     with jax.named_scope("late0"):
         late_grads(0)
         grad_core(0, 1)
+    with jax.named_scope("forward"):
+        rs_forward(0)
     with jax.named_scope("norm_grad0"):
         norm_grads(0)
         small_start()
@@ -886,7 +975,7 @@
     with jax.named_scope("small_third"):
         small_third()
     with jax.named_scope("gather1"):
-        ag_pairs(1, 0, nt_dev // 2, last_stream, nothing)
+        ag_pairs(1, 0, ny, last_stream, nothing)
         ag_sent(1)
         store_x.start()
     with jax.named_scope("gend1"):
@@ -897,11 +986,12 @@
         v.g[at, :] = v.g[at, :] + dx
 
     with jax.named_scope("gather3"):
-        ag_pairs(0, 0, nt_dev // 4, last_gradient, nothing)
+        ag_forward(0)
+        ag_pairs(0, 0, ny // 2, last_gradient, nothing)
     with jax.named_scope("small_fourth"):
         small_fourth()
     with jax.named_scope("gather3b"):
-        ag_pairs(0, nt_dev // 4, nt_dev // 2, last_gradient, nothing)
+        ag_pairs(0, ny // 2, ny, last_gradient, nothing)
         store_g.start()
         ag_sent(0)
     with jax.named_scope("gz0"):
@@ -993,9 +1083,14 @@
         vm((two, rows, 1), F32),
         vm((two, rows, 1), F32),
         vm((rows, depth), F32),
-        vm((2, nt_dev, chunk, depth), BF16),
-        vm((2, nt_dev, chunk, depth), BF16),
-        vm((2, nt_dev, chunk, depth), BF16),
+        vm((2, 2, nt_dev, chunk, depth // 2), BF16),
+        vm((2, nt_dev // 2 - 1, 2, chunk, depth // 2), BF16),
+        vm((2, nt_dev // 2, chunk, depth // 2), BF16),
+        vm((2, chunk, depth // 2), BF16),
+        vm((2, nt_dev // 2 - 1, chunk, depth // 2), BF16),
+        vm((2, chunk, depth // 2), BF16),
+        vm((2, nt_dev // 2 - 1, chunk, depth // 2), BF16),
+        vm((2, 2, nt_dev, chunk, depth // 2), BF16),
         vm((rows, depth), BF16),
         vm((rows, width), BF16),
         vm((2, rows, width), BF16),
@@ -1036,8 +1131,8 @@
         dma((two, 3)),
         dma((two, 3)),
         dma((two, 3)),
-        dma((2, 2, nt_dev)),
-        dma((2, 2, nt_dev)),
+        dma((2, 7 * (nt_dev // 2) - 3)),
+        dma((2, 7 * (nt_dev // 2) - 3)),
         dma((two, 2)),
         dma((two, 2)),
         dma((two, 2, nx - 1)),

time: 191 us -> 166 us (0.87); the launches traced: 189 us -> 166 us
  Pallas kernels: 188 us -> 165 us
    pallas_call x1, Pallas kernels: 182 us -> 159 us  [on_device(): pl.pallas_call(functools.partial(step_kernel, nt_dev, nd), out_shape=[jax...]
where the time goes in v3:
time: 166 us
  Pallas kernels  165 us (99%)
    pallas_call x1, Pallas kernels, on_device(): pl.pallas_call(functools.partial(step_kernel, nt_dev, nd), out_shape=[jax...  159 us
    pallas_call x1, Pallas kernels, on_device(): pl.pallas_call(functools.partial(store_kernel, len(shapes)), out_shape=[j...  5.68 us

profile of v3, /device:TPU:1, one launch (start us, length us, event | category | flops | bytes accessed | tf_op | source)
XLA Modules:
  0.0 165.7 jit_solution(17203533142450263495)
XLA Ops:
  0.6 159.2 %shard_map.229 = (f32[512,1024]{1,0:T(8,128)}, f32[512,1024]{1,0:T(8,128)}, f32[2,2,1024]{2,1,0:T(2,128)}, f32[2,2,1024]{2,1,0:T(2,128)}, f32[3,2,128]{2,1,0:T(2...) custom-call(bf16[512,1024]{1,0:T(8,128)(2,1)} %refs_0_.1, ...), custom_call_target="tpu_custom_call" | custom-call | tf_op jit(solution)/shard_map/pallas_call | solution.py:1167
  159.9 5.7 %shard_map.230 = (f32[512,1024]{1,0:T(8,128)}, f32[512,1024]{1,0:T(8,128)}, f32[2,2,1024]{2,1,0:T(2,128)}, f32[2,2,1024]{2,1,0:T(2,128)}, f32[3,2,128]{2,1,0:T(2...) custom-call(f32[512,1024]{1,0:T(8,128)} %get-tuple-element.36.refs_0, ...), custom_call_target="tpu_custom_call" | custom-call | tf_op jit(solution)/shard_map/pallas_call | solution.py:1192

commit v4 on v3

--- a/solution.py
+++ b/solution.py
@@ -21,7 +21,8 @@
 KT = 256
 MT = 256
 ST = 32
-PARTS = 8
+TP = 4
+PARTS = 4
 
 
 def nn(a, b):
@@ -87,13 +88,13 @@
         "tok", "cot", "gain", "bias", "wqkv_h", "bqkv", "wout_h", "bout", "win_h", "bin",
         "wdown_h", "bdown", "cos_h", "sin_h", "ox", "og", "ogain", "obias", "obqkv", "obout",
         "obin", "obdown", "oq", "oo", "oi", "od", "wqkv", "wout", "win", "wdown", "cosine",
-        "sine", "x", "g", "xt", "ct", "h0", "h1", "qm", "kv", "kt", "vt", "ob", "ot", "lse",
-        "u", "act", "mu", "rs", "part", "psend", "ra", "rb", "sa", "sb", "r2a", "r2b", "agbuf",
-        "dz", "do", "dom", "delta", "dqt", "dkvo", "dkvi", "own", "dqkv", "du", "dact",
-        "binacc", "dh0", "ge", "gl", "r1e", "r1l", "r2e", "r2l", "s3e", "s3l", "r3e", "r3l",
-        "k3e", "k3l", "ln", "other", "ln1", "other1", "ln2", "other2", "lnc", "ln3", "lnall",
-        "lnacc", "lsem", "kvs", "kvr", "dks", "dkr", "ars", "arr", "g1s", "g1r", "g2s", "g2r",
-        "g3s", "g3r", "s1s", "s1r", "s2s", "s2r", "s3s", "s3r", "s4s", "s4r",
+        "sine", "x", "g", "xt", "ct", "h0", "h1", "qm", "kv", "kt", "vt", "ob", "ot", "top",
+        "lse", "u", "act", "mu", "rs", "part", "psend", "ra", "rb", "sa", "sb", "r2a", "r2b",
+        "agbuf", "dz", "do", "dom", "delta", "dqt", "dkvo", "dkvi", "own", "dqkv", "du", "dact",
+        "binacc", "dh0", "dh1", "ge", "gl", "r1e", "r1l", "r2e", "r2l", "s3e", "s3l", "r3e",
+        "r3l", "k3e", "k3l", "ln", "other", "ln1", "other1", "ln2", "other2", "lnsum", "ln3",
+        "lnall", "lnacc", "lsem", "kvs", "kvr", "dks", "dkr", "ars", "arr", "g1s", "g1r", "g2s",
+        "g2r", "g3s", "g3r", "s1s", "s1r", "s2s", "s2r", "s3s", "s3r", "s4s", "s4r",
     )
     assert len(names) == len(refs)
     v = Refs()
@@ -130,12 +131,14 @@
             barrier, inc=1, device_id={"dp": lax.rem(me_d + k, nd)}, device_id_type=MESH
         )
 
+    parts = [slice(i * rows // TP, (i + 1) * rows // TP) for i in range(TP)]
+
     def load(src, dst, index):
         copy = pltpu.make_async_copy(src, dst, v.lsem.at[index])
         copy.start()
         return copy
 
-    load_tok = load(v.tok, v.xt, 0)
+    load_tok = [load(v.tok.at[at], v.xt.at[at], 16 + i) for i, at in enumerate(parts)]
     load_cos = load(v.cos_h.at[rows_at(rank, rows)], v.cosine, 1)
     load_sin = load(v.sin_h.at[rows_at(rank, rows)], v.sine, 2)
     load_qkv = []
@@ -247,6 +250,7 @@
         return copy_of(s, block, block, sem, to)
 
     ag0 = 3 * ny - 1
+    near_first = sorted(range(1, ny), key=lambda k: min(k, ny - k))
 
     def gz(s):
         return ag_copy(s, 0, me_t, ag0, other_zh)
@@ -262,6 +266,9 @@
 
     def bz(s, m):
         return ag_copy(s, 1, 2 * at_y(m) + zh, ag0 + 3 * ny - 2 + m, other_zh)
+
+    def place(step):
+        return lax.rem((step + 1) // 2 * (2 * lax.rem(step, 2) - 1) + ny, ny)
 
     def arrived(s, half, chunk_at, sem):
         ag_copy(s, half, chunk_at, sem, other_zh).wait_recv()
@@ -272,22 +279,23 @@
 
     def ag_start(s):
         gz(s).start()
-        for k in range(1, ny):
+        for k in near_first:
             by(s, k).start()
         bz(s, 0).start()
-        for k in range(1, ny):
+        for k in near_first:
             gy(s, k).start()
 
     def ag_forward(s):
         arrived(s, 0, other_zh, ag0)
-        for k in range(1, ny):
+        for k in near_first:
             fy(s, k).start()
-        for k in range(1, ny):
+        for k in near_first:
             arrived(s, 1, 2 * at_y(ny - k) + zh, ag0 + 2 * ny - 2 + k)
             bz(s, ny - k).start()
 
     def ag_pairs(s, first, last, use, after):
-        def one(m, carry):
+        def one(step, carry):
+            m = place(step)
             pair = at_y(m)
 
             @pl.when(m > 0)
@@ -365,53 +373,38 @@
         def _():
             kv_copy(l, 0).start()
 
-    def kv_relay(l):
+    def kv_near(l):
+        transpose_block(l, rank)
+
+        @pl.when(core == 1)
+        def _():
+            kv_in(l, 0).wait_recv()
+            transpose_block(l, rank - 1)
+
+    def kv_far(l):
         @pl.when(zlo == 1)
         def _():
             kv_in(l, 1).wait_recv()
             kv_copy(l, 2).start()
-
-    def kv_finish(l):
-        transpose_block(l, rank)
-
-        @pl.when(core == 1)
-        def _():
-            kv_in(l, 0).wait_recv()
-            transpose_block(l, rank - 1)
-
-        @pl.when(zlo == 1)
-        def _():
             transpose_block(l, rank - 2)
             kv_in(l, 2).wait_recv()
             transpose_block(l, rank - 1 - 2 * core)
 
-    def feed_forward(l):
-        for c in load_rest[l]:
-            c.wait()
-
-        def up(i, carry):
-            at = rows_at(i, MT)
-            v.u[l, at, :] = nn(v.h1[l, at, :], v.win[l]) + v.bin[l : l + 1, :]
+    def feed_forward(l, at, size):
+        v.u[l, at, :] = nn(v.h1[l, at, :], v.win[l]) + v.bin[l : l + 1, :]
+
+        def activate(i, carry):
+            now = pl.ds(pl.multiple_of(at.start + i * ST, ST), ST)
+            u = v.u[l, now, :]
+            inner = 0.5 * (1.0 + lax.erf(u * np.float32(0.5**0.5)))
+            v.act[l, now, :] = (u * inner).astype(BF16)
+            v.u[l, now, :] = inner + u * jnp.exp(-0.5 * u * u) * np.float32((2.0 * np.pi) ** -0.5)
             return carry
 
-        lax.fori_loop(0, rows // MT, up, 0)
-
-        def activate(i, carry):
-            at = rows_at(i, ST)
-            u = v.u[l, at, :]
-            v.act[l, at, :] = (0.5 * u * (1.0 + lax.erf(u * np.float32(0.5**0.5)))).astype(BF16)
-            return carry
-
-        lax.fori_loop(0, rows // ST, activate, 0)
-
-        def down(i, carry):
-            at = rows_at(i, MT)
-            v.part[at, :] = nn(v.act[l, at, :], v.wdown[l])
-            return carry
-
-        lax.fori_loop(0, rows // MT, down, 0)
-
-    def attention(l, s):
+        lax.fori_loop(0, size // ST, activate, 0)
+        v.part[at, :] = nn(v.act[l, at, :], v.wdown[l])
+
+    def attention(l, s, part):
         for qt in range(rows // QT):
             q_at = slice(qt * QT, (qt + 1) * QT)
             head_rows = [slice(h * HEAD_DIM, (h + 1) * HEAD_DIM) for h in range(2)]
@@ -440,8 +433,25 @@
                 jnp.zeros((1, QT), F32),
                 jnp.zeros((HEAD_DIM, QT), F32),
             )
-            carry = lax.fori_loop(0, rank, functools.partial(block, masked=False), (start, start))
-            carry = block(rank, carry, True)
+            if part == 0:
+                carry = block(rank, (start, start), True)
+                carry = lax.fori_loop(
+                    rank - core, rank, functools.partial(block, masked=False), carry
+                )
+                for h in range(2):
+                    v.top[h : h + 1, q_at] = carry[h][0]
+                    v.lse[l, h : h + 1, q_at] = carry[h][1]
+                    v.ot[l, head_rows[h], q_at] = carry[h][2]
+                continue
+            carry = tuple(
+                (
+                    v.top[h : h + 1, q_at],
+                    v.lse[l, h : h + 1, q_at],
+                    v.ot[l, head_rows[h], q_at],
+                )
+                for h in range(2)
+            )
+            carry = lax.fori_loop(0, 2 * zlo, functools.partial(block, masked=False), carry)
             for h in range(2):
                 top, total, out = carry[h]
                 v.ot[l, head_rows[h], q_at] = out / total
@@ -543,7 +553,7 @@
     def start_gradient(l, at, gradient):
         v.dz[at, :] = gradient.astype(BF16)
 
-    def attention_back(l):
+    def attention_back(l, first, second):
         do = v.do[...]
         product = do.astype(F32).T * v.ot[l]
         v.delta[0:1, :] = jnp.sum(product[:HEAD_DIM], axis=0, keepdims=True)
@@ -582,14 +592,16 @@
                 v.dkvo[l, slot, at, width:] = dv.astype(BF16)
                 return c
 
-            lax.fori_loop(0, rows // KT, inner, 0)
+            lax.fori_loop(0, rows // KT, inner, 0, unroll=True)
             dkv_copy(l, slot).start()
 
         @pl.when(zlo == 1)
         def _():
             far(1 - core, 0, False)
+            first()
             dkv_copy(l, 0).wait_recv()
             far(core, 1, True)
+            second()
 
         @pl.when(core == 1)
         def _():
@@ -602,27 +614,26 @@
             v.own[at, width:] = dv
             return c
 
-        lax.fori_loop(0, rows // KT, near, 0)
-
-    def back_rows(l, at, size):
+        lax.fori_loop(0, rows // KT, near, 0, unroll=True)
+
+    def do_rows(l, at):
         do = nt(v.dz[at, :], v.wout[l]).astype(BF16)
         v.do[at, :] = do
         v.dom[0, at, :] = head_only(do, 0)
         v.dom[1, at, :] = head_only(do, 1)
+
+    def dact_rows(l, at):
         v.dact[at, :] = nt(v.dz[at, :], v.wdown[l])
-        start = at.start if isinstance(at, pl.Slice) else at
-
+
+    def back_rows(l, at, size):
         def slope(i, acc):
-            rows_now = pl.ds(pl.multiple_of(start + i * ST, ST), ST)
-            u = v.u[l, rows_now, :]
-            inner = 0.5 * (1.0 + lax.erf(u * np.float32(0.5**0.5)))
-            inner = inner + u * jnp.exp(-0.5 * u * u) * np.float32((2.0 * np.pi) ** -0.5)
-            du = (v.dact[rows_now, :] * inner).astype(BF16)
-            v.du[rows_now, :] = du
+            now = pl.ds(pl.multiple_of(at.start + i * ST, ST), ST)
+            du = (v.dact[now, :] * v.u[l, now, :]).astype(BF16)
+            v.du[now, :] = du
             return acc + jnp.sum(du.astype(F32).reshape(ST // 8, 8, ff), axis=0)
 
         v.binacc[l] += lax.fori_loop(0, size // ST, slope, jnp.zeros((8, ff), F32))
-        v.part[at, :] = nt(v.du[at, :], v.win[l])
+        v.dh1[at, :] = nt(v.du[at, :], v.win[l])
 
     def early_grads(l):
         def one(i, carry):
@@ -679,7 +690,7 @@
             pair = at_y(m)
             for i in range(2 * chunk // ST):
                 at = pl.ds(pl.multiple_of(pair * 2 * chunk + i * ST, ST), ST)
-                both = v.dh0[at, :] * v.gain[l, 0:1, :] + v.part[at, :] * v.gain[l, 1:2, :]
+                both = v.dh0[at, :] * v.gain[l, 0:1, :] + v.dh1[at, :] * v.gain[l, 1:2, :]
                 both = both.astype(BF16)
                 part = slice(i * ST % chunk, i * ST % chunk + ST)
                 for half in range(2):
@@ -700,7 +711,7 @@
         def one(i, carry):
             at = rows_at(i, 16)
             xhat = (stream_rows(l, at) - v.mu[l, at, :]) * v.rs[l, at, :]
-            first, second = v.dh0[at, :], v.part[at, :]
+            first, second = v.dh0[at, :], v.dh1[at, :]
             v.lnacc[0] += fold(first * xhat)
             v.lnacc[1] += fold(second * xhat)
             v.lnacc[2] += fold(first)
@@ -733,17 +744,17 @@
         mine, theirs = [(v.ln, v.ln1), (v.other, v.other1)][i]
         return remote(mine, theirs, v.s1s.at[i], v.s1r.at[i], dp=other_core)
 
+    def small_dp(k, i):
+        to = lax.rem(me_d + 2 * k, nd)
+        mine, theirs = [(v.ln, v.ln3), (v.other, v.other2)][i]
+        return remote(mine, theirs.at[k - 1], v.s3s.at[i, k - 1], v.s3r.at[i, k - 1], dp=to)
+
     def small_scatter(k):
         to = lax.rem(me_t + k, nt_dev)
         columns = pl.ds(pl.multiple_of(to * LANES, LANES), LANES)
         return remote(
-            v.ln.at[:, columns], v.ln2.at[k - 1], v.s2s.at[k - 1], v.s2r.at[k - 1], tensor=to
+            v.lnsum.at[:, columns], v.ln2.at[k - 1], v.s2s.at[k - 1], v.s2r.at[k - 1], tensor=to
         )
-
-    def small_dp(k, i):
-        to = lax.rem(me_d + 2 * k, nd)
-        mine, theirs = [(v.lnc, v.ln3), (v.other, v.other2)][i]
-        return remote(mine, theirs.at[k - 1], v.s3s.at[i, k - 1], v.s3r.at[i, k - 1], dp=to)
 
     def small_gather(k):
         to = lax.rem(me_t + k, nt_dev)
@@ -759,29 +770,18 @@
             small_core(i).wait()
         v.ln[...] += v.ln1[...]
         v.other[...] += v.other1[...]
-        for k in range(1, nt_dev):
-            small_scatter(k).start()
         for k in range(1, nd // 2):
-            small_dp(k, 1).start()
+            for i in range(2):
+                small_dp(k, i).start()
 
     def small_third():
-        mine = pl.ds(pl.multiple_of(me_t * LANES, LANES), LANES)
-        total = v.ln[:, mine]
-        for k in range(1, nt_dev):
-            small_scatter(k).wait()
-            total = total + v.ln2[k - 1]
-        v.lnc[...] = total
-        for k in range(1, nd // 2):
-            small_dp(k, 0).start()
-
-    def small_fourth():
-        total = v.lnc[...]
+        total = v.ln[...]
         for k in range(1, nd // 2):
             small_dp(k, 0).wait()
             total = total + v.ln3[k - 1]
-        v.lnall[me_t] = total
+        v.lnsum[...] = total
         for k in range(1, nt_dev):
-            small_gather(k).start()
+            small_scatter(k).start()
         total = v.other[...]
         for k in range(1, nd // 2):
             small_dp(k, 1).wait()
@@ -797,6 +797,16 @@
                 at = slice(c * width, (c + 1) * width)
                 v.obqkv[c, l : l + 1, :] = total[4 * l + 3 : 4 * l + 4, at]
 
+    def small_fourth():
+        mine = pl.ds(pl.multiple_of(me_t * LANES, LANES), LANES)
+        total = v.lnsum[:, mine]
+        for k in range(1, nt_dev):
+            small_scatter(k).wait()
+            total = total + v.ln2[k - 1]
+        v.lnall[me_t] = total
+        for k in range(1, nt_dev):
+            small_gather(k).start()
+
     def small_end():
         for k in range(1, nt_dev):
             src = lax.rem(me_t + k, nt_dev)
@@ -812,16 +822,15 @@
     def nothing(at):
         pass
 
-    with jax.named_scope("tok"):
-        load_tok.wait()
-
     def first_norm(i, carry):
         at = rows_at(i, ST)
         norm_rows(0, at, v.xt[at, :].astype(F32))
         return carry
 
     with jax.named_scope("norm0"):
-        lax.fori_loop(0, rows // ST, first_norm, 0, unroll=2)
+        for i in range(TP):
+            load_tok[i].wait()
+            lax.fori_loop(i * rows // TP // ST, (i + 1) * rows // TP // ST, first_norm, 0, unroll=2)
     with jax.named_scope("qkv0"):
         for c in load_qkv[0]:
             c.wait()
@@ -840,12 +849,47 @@
     v.other[...] = jnp.zeros_like(v.other)
     v.binacc[...] = jnp.zeros_like(v.binacc)
     with jax.named_scope("ffn0"):
-        feed_forward(0)
+        for c in load_rest[0]:
+            c.wait()
+
+        def first_ffn(i, carry):
+            feed_forward(0, rows_at(i, MT), MT)
+            return carry
+
+        lax.fori_loop(0, rows // MT, first_ffn, 0)
+    with jax.named_scope("near0"):
+        kv_near(0)
+        attention(0, 0, 0)
+    def first_gradients(z):
+        @pl.when(zlo == z)
+        def _():
+            load_cot.wait()
+            for c in load_rest[1]:
+                c.wait()
+
+            def copy_rows(i, carry):
+                at = rows_at(i, ST)
+                v.dz[at, :] = v.ct[at, :]
+                v.g[at, :] = v.ct[at, :].astype(F32)
+                return carry
+
+            def rows_back(i, carry):
+                at = rows_at(i, MT)
+                do_rows(1, at)
+                dact_rows(1, at)
+                return carry
+
+            lax.fori_loop(0, rows // ST, copy_rows, 0)
+            lax.fori_loop(0, rows // MT, rows_back, 0)
+
+    with jax.named_scope("dz1"):
+        first_gradients(1)
     with jax.named_scope("kv0"):
-        kv_relay(0)
-        kv_finish(0)
+        kv_far(0)
     with jax.named_scope("attn0"):
-        attention(0, 0)
+        attention(0, 0, 1)
+    with jax.named_scope("dz1b"):
+        first_gradients(0)
     with jax.named_scope("forward0"):
         rs_forward(0)
     with jax.named_scope("reduce0"):
@@ -859,41 +903,34 @@
     def next_qkv(at):
         qkv_rows(1, at, 2 * chunk)
 
+    def next_ffn(at):
+        feed_forward(1, at, 2 * chunk)
+        back_rows(1, at, 2 * chunk)
+
+    def next_both(at):
+        next_qkv(at)
+        next_ffn(at)
+
     with jax.named_scope("gather0"):
         for c in load_qkv[1]:
             c.wait()
         ag_forward(0)
-        ag_pairs(0, 0, ny, next_stream, next_qkv)
+        ag_pairs(0, 0, ny - 1, next_stream, next_both)
+        ag_pairs(0, ny - 1, ny, next_stream, next_qkv)
         kv_send(1)
         ag_sent(0)
     with jax.named_scope("ffn1"):
-        feed_forward(1)
+        next_ffn(rows_at(at_y(place(jnp.int32(ny - 1))), 2 * chunk))
+    with jax.named_scope("near1"):
+        kv_near(1)
+        attention(1, 1, 0)
     with jax.named_scope("kv1"):
-        kv_relay(1)
-        kv_finish(1)
+        kv_far(1)
     with jax.named_scope("attn1"):
-        attention(1, 1)
-
-    with jax.named_scope("dz1"):
-        load_cot.wait()
-
-        def first_gradient(i, carry):
-            at = rows_at(i, ST)
-            v.dz[at, :] = v.ct[at, :]
-            v.g[at, :] = v.ct[at, :].astype(F32)
-            return carry
-
-        lax.fori_loop(0, rows // ST, first_gradient, 0)
-
-    with jax.named_scope("back1"):
-
-        def first_back(i, carry):
-            back_rows(1, rows_at(i, MT), MT)
-            return carry
-
-        lax.fori_loop(0, rows // MT, first_back, 0)
+        attention(1, 1, 1)
+
     with jax.named_scope("attn_grad1"):
-        attention_back(1)
+        attention_back(1, lambda: None, lambda: rs_forward(1))
 
     def early(l, z):
         @pl.when(zlo == z)
@@ -902,7 +939,11 @@
             grad_core(l, 0)
 
     with jax.named_scope("forward1"):
-        rs_forward(1)
+
+        @pl.when(zlo == 0)
+        def _():
+            rs_forward(1)
+
     with jax.named_scope("early1"):
         early(1, 0)
     with jax.named_scope("qkv_grad1"):
@@ -929,6 +970,8 @@
         v.dz[at, :] = gradient.astype(BF16)
 
     def next_back(at):
+        do_rows(0, at)
+        dact_rows(0, at)
         back_rows(0, at, 2 * chunk)
 
     with jax.named_scope("gather2"):
@@ -938,9 +981,13 @@
     with jax.named_scope("reduce1"):
         branch_reduce(1)
     with jax.named_scope("attn_grad0"):
-        attention_back(0)
+        attention_back(0, lambda: ag_forward(1), lambda: None)
     with jax.named_scope("forward1b"):
-        ag_forward(1)
+
+        @pl.when(zlo == 0)
+        def _():
+            ag_forward(1)
+
     with jax.named_scope("gz1"):
         grad_z(1, 0)
         grad_z(1, 1)
@@ -950,28 +997,30 @@
         qkv_back(0)
     with jax.named_scope("early0b"):
         early(0, 1)
+    with jax.named_scope("norm_grad0"):
+        norm_grads(0)
+        small_start()
     with jax.named_scope("late0"):
         late_grads(0)
         grad_core(0, 1)
+    with jax.named_scope("small_second"):
+        small_second()
+    with jax.named_scope("gx00"):
+        grad_x(0, 0)
     with jax.named_scope("forward"):
         rs_forward(0)
-    with jax.named_scope("norm_grad0"):
-        norm_grads(0)
-        small_start()
-    with jax.named_scope("gx00"):
-        grad_x(0, 0)
 
     def last_stream(at, z):
         v.x[at, :] = v.x[at, :] + (z + (v.bout[1:2, :] + v.bdown[1:2, :]))
 
     store_x = pltpu.make_async_copy(v.x, v.ox, v.lsem.at[0])
     store_g = pltpu.make_async_copy(v.g, v.og, v.lsem.at[1])
-    with jax.named_scope("small_second"):
-        small_second()
     with jax.named_scope("stream_reduce0"):
         stream_reduce(0)
     with jax.named_scope("gx01"):
         grad_x(0, 1)
+    with jax.named_scope("forward0c"):
+        ag_forward(0)
     with jax.named_scope("small_third"):
         small_third()
     with jax.named_scope("gather1"):
@@ -986,7 +1035,6 @@
         v.g[at, :] = v.g[at, :] + dx
 
     with jax.named_scope("gather3"):
-        ag_forward(0)
         ag_pairs(0, 0, ny // 2, last_gradient, nothing)
     with jax.named_scope("small_fourth"):
         small_fourth()
@@ -1019,26 +1067,27 @@
 
 
 def store_kernel(count, *refs):
-    given, kept = refs[:count], refs[count : 2 * count]
-    held = refs[2 * count : 2 * count + 2]
-    sems = refs[2 * count + 2]
-    rows = held[0].shape[0] // PARTS
-    parts = [(i, slice(j * rows, (j + 1) * rows), i * PARTS + j) for j in range(PARTS) for i in range(2)]
+    given, kept, held = refs[:count], refs[count : 2 * count], refs[2 * count : 3 * count]
+    sems = refs[3 * count]
+    parts = []
+    for i in range(count):
+        pieces = PARTS if i < 2 else 1
+        rows = held[i].shape[0] // pieces
+        parts += [(i, slice(j * rows, (j + 1) * rows)) for j in range(pieces)]
     loads = [
-        pltpu.make_async_copy(given[i].at[at], held[i].at[at], sems.at[0, n]) for i, at, n in parts
+        pltpu.make_async_copy(given[i].at[at], held[i].at[at], sems.at[0, n])
+        for n, (i, at) in enumerate(parts)
     ]
     stores = [
-        pltpu.make_async_copy(held[i].at[at], kept[i].at[at], sems.at[1, n]) for i, at, n in parts
+        pltpu.make_async_copy(held[i].at[at], kept[i].at[at], sems.at[1, n])
+        for n, (i, at) in enumerate(parts)
     ]
-    others = [
-        pltpu.make_async_copy(given[i], kept[i], sems.at[2, i]) for i in range(2, count)
-    ]
-    for copy in loads + others:
+    for copy in loads:
         copy.start()
     for load, store in zip(loads, stores):
         load.wait()
         store.start()
-    for copy in stores + others:
+    for copy in stores:
         copy.wait()
 
 
@@ -1077,6 +1126,7 @@
         vm((two, group, width, rows), BF16),
         vm((two, rows, width), BF16),
         vm((two, width, rows), F32),
+        vm((8, rows), F32),
         vm((two, 8, rows), F32),
         vm((two, rows, ff), F32),
         vm((two, rows, ff), BF16),
@@ -1104,6 +1154,7 @@
         vm((rows, ff), F32),
         vm((two, 8, ff), F32),
         vm((rows, depth), F32),
+        vm((rows, depth), F32),
         vm((two, 2, half, grow, early), BF16),
         vm((two, 2, half, grow, late), BF16),
         vm((two, half, grow, early), BF16),
@@ -1122,11 +1173,11 @@
         vm((8, ff), F32),
         vm((nt_dev - 1, 8, LANES), F32),
         vm((half - 1, 8, ff), F32),
-        vm((8, LANES), F32),
-        vm((half - 1, 8, LANES), F32),
+        vm((8, depth), F32),
+        vm((half - 1, 8, depth), F32),
         vm((nt_dev, 8, LANES), F32),
         vm((5, 8, depth), F32),
-        dma((16,)),
+        dma((16 + TP,)),
         dma((two, 3)),
         dma((two, 3)),
         dma((two, 3)),
@@ -1192,9 +1243,9 @@
     out = pl.pallas_call(
         functools.partial(store_kernel, len(shapes)),
         out_shape=[jax.ShapeDtypeStruct(s, F32) for s in shapes],
-        in_specs=[away] * 2 + [here] * (len(shapes) - 2),
+        in_specs=[away] * len(shapes),
         out_specs=[away] * len(shapes),
-        scratch_shapes=[vm((rows, depth), F32), vm((rows, depth), F32), dma((3, 16))],
+        scratch_shapes=[vm(s, F32) for s in shapes] + [dma((2, 2 * PARTS + len(shapes)))],
     )(*out)
     x, g, gain, bias, bqkv, bout, b_in_g, bdown, wq, wo, wi, wd = out
     return (

time: 166 us -> 152 us (0.916)
  the two profiles are of different devices: /device:TPU:1 before, /device:TPU:2 now
where the time goes in v4:
time: 152 us
  Pallas kernels  151 us (99%)
    pallas_call x1, Pallas kernels, on_device(): pl.pallas_call(functools.partial(step_kernel, nt_dev, nd), out_shape=[jax...  146 us
    pallas_call x1, Pallas kernels, on_device(): pl.pallas_call(functools.partial(store_kernel, len(shapes)), out_shape=[j...  4.63 us

profile of v4, /device:TPU:2, one launch (start us, length us, event | category | flops | bytes accessed | tf_op | source)
XLA Modules:
  0.0 151.6 jit_solution(5641415356539853176)
XLA Ops:
  0.6 146.1 %shard_map.229 = (f32[512,1024]{1,0:T(8,128)}, f32[512,1024]{1,0:T(8,128)}, f32[2,2,1024]{2,1,0:T(2,128)}, f32[2,2,1024]{2,1,0:T(2,128)}, f32[3,2,128]{2,1,0:T(2...) custom-call(bf16[512,1024]{1,0:T(8,128)(2,1)} %refs_0_.1, ...), custom_call_target="tpu_custom_call" | custom-call | tf_op jit(solution)/shard_map/pallas_call | solution.py:1218
  146.8 4.6 %shard_map.230 = (f32[512,1024]{1,0:T(8,128)}, f32[512,1024]{1,0:T(8,128)}, f32[2,2,1024]{2,1,0:T(2,128)}, f32[2,2,1024]{2,1,0:T(2,128)}, f32[3,2,128]{2,1,0:T(2...) custom-call(f32[512,1024]{1,0:T(8,128)} %get-tuple-element.36.refs_0, ...), custom_call_target="tpu_custom_call" | custom-call | tf_op jit(solution)/shard_map/pallas_call | solution.py:1243

commit v5 on v4

--- a/solution.py
+++ b/solution.py
@@ -246,7 +246,7 @@
         return jnp.concatenate([first, second], axis=1)
 
     def ag_copy(s, half, chunk_at, sem, to):
-        block = v.agbuf.at[s, half, chunk_at]
+        block = v.agbuf.at[s, :, chunk_at] if s == 1 else v.agbuf.at[s, half, chunk_at]
         return copy_of(s, block, block, sem, to)
 
     ag0 = 3 * ny - 1
@@ -268,7 +268,7 @@
         return ag_copy(s, 1, 2 * at_y(m) + zh, ag0 + 3 * ny - 2 + m, other_zh)
 
     def place(step):
-        return lax.rem((step + 1) // 2 * (2 * lax.rem(step, 2) - 1) + ny, ny)
+        return ((step + 1) // 2 * (2 * (step % 2) - 1) + ny) % ny
 
     def arrived(s, half, chunk_at, sem):
         ag_copy(s, half, chunk_at, sem, other_zh).wait_recv()
@@ -279,9 +279,10 @@
 
     def ag_start(s):
         gz(s).start()
-        for k in near_first:
-            by(s, k).start()
-        bz(s, 0).start()
+        if s == 0:
+            for k in near_first:
+                by(s, k).start()
+            bz(s, 0).start()
         for k in near_first:
             gy(s, k).start()
 
@@ -289,9 +290,10 @@
         arrived(s, 0, other_zh, ag0)
         for k in near_first:
             fy(s, k).start()
-        for k in near_first:
-            arrived(s, 1, 2 * at_y(ny - k) + zh, ag0 + 2 * ny - 2 + k)
-            bz(s, ny - k).start()
+        if s == 0:
+            for k in near_first:
+                arrived(s, 1, 2 * at_y(ny - k) + zh, ag0 + 2 * ny - 2 + k)
+                bz(s, ny - k).start()
 
     def ag_pairs(s, first, last, use, after):
         def one(step, carry):
@@ -303,7 +305,8 @@
                 arrived(s, 0, 2 * pair + zh, ag0 + ny - m)
                 arrived(s, 0, 2 * pair + 1 - zh, ag0 + 2 * ny - 1 - m)
 
-            arrived(s, 1, 2 * pair + 1 - zh, ag0 + 3 * ny - 2 + m)
+            if s == 0:
+                arrived(s, 1, 2 * pair + 1 - zh, ag0 + 3 * ny - 2 + m)
             for i in range(2):
                 src = 2 * pair + i
                 for j in range(chunk // ST):
@@ -321,12 +324,14 @@
 
     def ag_sent(s):
         gz(s).wait_send()
-        bz(s, 0).wait_send()
         for k in range(1, ny):
             gy(s, k).wait_send()
             fy(s, k).wait_send()
-            by(s, k).wait_send()
-            bz(s, k).wait_send()
+        if s == 0:
+            bz(s, 0).wait_send()
+            for k in range(1, ny):
+                by(s, k).wait_send()
+                bz(s, k).wait_send()
 
     def kv_copy(l, step):
         slot, to = [(rank, other_core), (rank, other_z), (rank - 2, other_core)][step]
@@ -338,12 +343,13 @@
         block = v.kv.at[l, slot]
         return remote(block, block, v.kvs.at[l, step], v.kvr.at[l, step], dp=other_core)
 
-    def dkv_copy(l, step):
+    def dkv_copy(l, step, i):
+        at = slice(i * KT, (i + 1) * KT)
         return remote(
-            v.dkvo.at[l, step],
-            v.dkvi.at[l, step],
-            v.dks.at[l, step],
-            v.dkr.at[l, step],
+            v.dkvo.at[l, step, at],
+            v.dkvi.at[l, step, at],
+            v.dks.at[l, step, i],
+            v.dkr.at[l, step, i],
             dp=other_z if step == 1 else other_core,
         )
 
@@ -561,7 +567,7 @@
         v.dqt[...] = jnp.zeros_like(v.dqt)
 
         def piece(b, i, masked):
-            at = rows_at(i, KT)
+            at = slice(i * KT, (i + 1) * KT)
             keys = v.kv[l, b, at, :width]
             values = v.kv[l, b, at, width:]
             dk = jnp.zeros((KT, width), F32)
@@ -582,39 +588,36 @@
             return dk, dv
 
         def far(b, slot, received):
-            def inner(i, c):
+            for i in range(rows // KT):
                 dk, dv = piece(b, i, False)
-                at = rows_at(i, KT)
+                at = slice(i * KT, (i + 1) * KT)
                 if received:
+                    dkv_copy(l, 0, i).wait_recv()
                     dk = dk + v.dkvi[l, 0, at, :width].astype(F32)
                     dv = dv + v.dkvi[l, 0, at, width:].astype(F32)
                 v.dkvo[l, slot, at, :width] = dk.astype(BF16)
                 v.dkvo[l, slot, at, width:] = dv.astype(BF16)
-                return c
-
-            lax.fori_loop(0, rows // KT, inner, 0, unroll=True)
-            dkv_copy(l, slot).start()
+                dkv_copy(l, slot, i).start()
 
         @pl.when(zlo == 1)
         def _():
             far(1 - core, 0, False)
             first()
-            dkv_copy(l, 0).wait_recv()
             far(core, 1, True)
+
+        @pl.when(core == 1)
+        def _():
+            far(rank - 1, 2, False)
+
+        @pl.when(rank == group - 1)
+        def _():
             second()
 
-        @pl.when(core == 1)
-        def _():
-            far(rank - 1, 2, False)
-
-        def near(i, c):
+        for i in range(rows // KT):
             dk, dv = piece(rank, i, True)
-            at = rows_at(i, KT)
+            at = slice(i * KT, (i + 1) * KT)
             v.own[at, :width] = dk
             v.own[at, width:] = dv
-            return c
-
-        lax.fori_loop(0, rows // KT, near, 0, unroll=True)
 
     def do_rows(l, at):
         do = nt(v.dz[at, :], v.wout[l]).astype(BF16)
@@ -664,11 +667,16 @@
         lax.fori_loop(0, depth // (2 * grow), one, 0)
 
     def qkv_back(l):
+        @pl.when(zlo == 0)
+        def _():
+            grad_x(l, 0)
+
         for step, here in ((2, core == 0), (1, zlo == 0)):
 
             @pl.when(here)
             def _():
-                dkv_copy(l, step).wait_recv()
+                for i in range(rows // KT):
+                    dkv_copy(l, step, i).wait_recv()
                 v.own[...] += v.dkvi[l, step].astype(F32)
 
         cosine, sine = v.cosine[...], -v.sine[...]
@@ -746,14 +754,14 @@
 
     def small_dp(k, i):
         to = lax.rem(me_d + 2 * k, nd)
-        mine, theirs = [(v.ln, v.ln3), (v.other, v.other2)][i]
+        mine, theirs = [(v.lnsum, v.ln3), (v.other, v.other2)][i]
         return remote(mine, theirs.at[k - 1], v.s3s.at[i, k - 1], v.s3r.at[i, k - 1], dp=to)
 
     def small_scatter(k):
         to = lax.rem(me_t + k, nt_dev)
         columns = pl.ds(pl.multiple_of(to * LANES, LANES), LANES)
         return remote(
-            v.lnsum.at[:, columns], v.ln2.at[k - 1], v.s2s.at[k - 1], v.s2r.at[k - 1], tensor=to
+            v.ln.at[:, columns], v.ln2.at[k - 1], v.s2s.at[k - 1], v.s2r.at[k - 1], tensor=to
         )
 
     def small_gather(k):
@@ -770,18 +778,29 @@
             small_core(i).wait()
         v.ln[...] += v.ln1[...]
         v.other[...] += v.other1[...]
+        for k in range(1, nt_dev):
+            small_scatter(k).start()
         for k in range(1, nd // 2):
-            for i in range(2):
-                small_dp(k, i).start()
+            small_dp(k, 1).start()
 
     def small_third():
-        total = v.ln[...]
+        mine = pl.ds(pl.multiple_of(me_t * LANES, LANES), LANES)
+        total = v.ln[:, mine]
+        for k in range(1, nt_dev):
+            small_scatter(k).wait()
+            total = total + v.ln2[k - 1]
+        v.lnsum[...] = total
+        for k in range(1, nd // 2):
+            small_dp(k, 0).start()
+
+    def small_fourth():
+        total = v.lnsum[...]
         for k in range(1, nd // 2):
             small_dp(k, 0).wait()
             total = total + v.ln3[k - 1]
-        v.lnsum[...] = total
+        v.lnall[me_t] = total
         for k in range(1, nt_dev):
-            small_scatter(k).start()
+            small_gather(k).start()
         total = v.other[...]
         for k in range(1, nd // 2):
             small_dp(k, 1).wait()
@@ -797,16 +816,6 @@
                 at = slice(c * width, (c + 1) * width)
                 v.obqkv[c, l : l + 1, :] = total[4 * l + 3 : 4 * l + 4, at]
 
-    def small_fourth():
-        mine = pl.ds(pl.multiple_of(me_t * LANES, LANES), LANES)
-        total = v.lnsum[:, mine]
-        for k in range(1, nt_dev):
-            small_scatter(k).wait()
-            total = total + v.ln2[k - 1]
-        v.lnall[me_t] = total
-        for k in range(1, nt_dev):
-            small_gather(k).start()
-
     def small_end():
         for k in range(1, nt_dev):
             src = lax.rem(me_t + k, nt_dev)
@@ -920,7 +929,7 @@
         kv_send(1)
         ag_sent(0)
     with jax.named_scope("ffn1"):
-        next_ffn(rows_at(at_y(place(jnp.int32(ny - 1))), 2 * chunk))
+        next_ffn(rows_at(at_y(place(ny - 1)), 2 * chunk))
     with jax.named_scope("near1"):
         kv_near(1)
         attention(1, 1, 0)
@@ -932,17 +941,26 @@
     with jax.named_scope("attn_grad1"):
         attention_back(1, lambda: None, lambda: rs_forward(1))
 
+        @pl.when(rank != group - 1)
+        def _():
+            rs_forward(1)
+
+
+    def forward_at(z):
+        @pl.when(zlo == z)
+        def _():
+            rs_forward(0)
+
+    def late_x(l):
+        @pl.when(zlo == 1)
+        def _():
+            grad_x(l, 0)
+
     def early(l, z):
         @pl.when(zlo == z)
         def _():
             early_grads(l)
             grad_core(l, 0)
-
-    with jax.named_scope("forward1"):
-
-        @pl.when(zlo == 0)
-        def _():
-            rs_forward(1)
 
     with jax.named_scope("early1"):
         early(1, 0)
@@ -950,19 +968,21 @@
         qkv_back(1)
     with jax.named_scope("early1b"):
         early(1, 1)
+    with jax.named_scope("norm_grad1"):
+        norm_grads(1)
+    with jax.named_scope("forward"):
+        forward_at(1)
+    with jax.named_scope("gx10"):
+        late_x(1)
     with jax.named_scope("late1"):
         late_grads(1)
         grad_core(1, 1)
     with jax.named_scope("forward"):
-        rs_forward(0)
-    with jax.named_scope("norm_grad1"):
-        norm_grads(1)
-    with jax.named_scope("gx10"):
-        grad_x(1, 0)
+        forward_at(0)
+    with jax.named_scope("gx11"):
+        grad_x(1, 1)
     with jax.named_scope("stream_reduce1"):
         stream_reduce(1)
-    with jax.named_scope("gx11"):
-        grad_x(1, 1)
 
     def next_gradient(at, dx):
         gradient = v.g[at, :] + dx
@@ -976,10 +996,9 @@
 
     with jax.named_scope("gather2"):
         ag_forward(0)
+        branch_reduce(1)
         ag_pairs(0, 0, ny, next_gradient, next_back)
         ag_sent(0)
-    with jax.named_scope("reduce1"):
-        branch_reduce(1)
     with jax.named_scope("attn_grad0"):
         attention_back(0, lambda: ag_forward(1), lambda: None)
     with jax.named_scope("forward1b"):
@@ -988,9 +1007,6 @@
         def _():
             ag_forward(1)
 
-    with jax.named_scope("gz1"):
-        grad_z(1, 0)
-        grad_z(1, 1)
     with jax.named_scope("early0"):
         early(0, 0)
     with jax.named_scope("qkv_grad0"):
@@ -1000,15 +1016,22 @@
     with jax.named_scope("norm_grad0"):
         norm_grads(0)
         small_start()
+    with jax.named_scope("gx00"):
+        late_x(0)
+    with jax.named_scope("forward"):
+        forward_at(1)
+    with jax.named_scope("small_second"):
+        small_second()
     with jax.named_scope("late0"):
         late_grads(0)
         grad_core(0, 1)
-    with jax.named_scope("small_second"):
-        small_second()
-    with jax.named_scope("gx00"):
-        grad_x(0, 0)
     with jax.named_scope("forward"):
-        rs_forward(0)
+        forward_at(0)
+    with jax.named_scope("gx01"):
+        grad_x(0, 1)
+    with jax.named_scope("gz1"):
+        grad_z(1, 0)
+        grad_z(1, 1)
 
     def last_stream(at, z):
         v.x[at, :] = v.x[at, :] + (z + (v.bout[1:2, :] + v.bdown[1:2, :]))
@@ -1017,8 +1040,6 @@
     store_g = pltpu.make_async_copy(v.g, v.og, v.lsem.at[1])
     with jax.named_scope("stream_reduce0"):
         stream_reduce(0)
-    with jax.named_scope("gx01"):
-        grad_x(0, 1)
     with jax.named_scope("forward0c"):
         ag_forward(0)
     with jax.named_scope("small_third"):
@@ -1035,16 +1056,16 @@
         v.g[at, :] = v.g[at, :] + dx
 
     with jax.named_scope("gather3"):
-        ag_pairs(0, 0, ny // 2, last_gradient, nothing)
+        ag_pairs(0, 0, ny - 1, last_gradient, nothing)
     with jax.named_scope("small_fourth"):
         small_fourth()
-    with jax.named_scope("gather3b"):
-        ag_pairs(0, ny // 2, ny, last_gradient, nothing)
-        store_g.start()
-        ag_sent(0)
     with jax.named_scope("gz0"):
         grad_z(0, 0)
         grad_z(0, 1)
+    with jax.named_scope("gather3b"):
+        ag_pairs(0, ny - 1, ny, last_gradient, nothing)
+        store_g.start()
+        ag_sent(0)
     with jax.named_scope("small_end"):
         small_end()
     with jax.named_scope("gend0"):
@@ -1063,7 +1084,8 @@
 
             @pl.when(here)
             def _():
-                dkv_copy(l, step).wait_send()
+                for i in range(rows // KT):
+                    dkv_copy(l, step, i).wait_send()
 
 
 def store_kernel(count, *refs):
@@ -1173,15 +1195,15 @@
         vm((8, ff), F32),
         vm((nt_dev - 1, 8, LANES), F32),
         vm((half - 1, 8, ff), F32),
-        vm((8, depth), F32),
-        vm((half - 1, 8, depth), F32),
+        vm((8, LANES), F32),
+        vm((half - 1, 8, LANES), F32),
         vm((nt_dev, 8, LANES), F32),
         vm((5, 8, depth), F32),
         dma((16 + TP,)),
         dma((two, 3)),
         dma((two, 3)),
-        dma((two, 3)),
-        dma((two, 3)),
+        dma((two, 3, rows // KT)),
+        dma((two, 3, rows // KT)),
         dma((2, 7 * (nt_dev // 2) - 3)),
         dma((2, 7 * (nt_dev // 2) - 3)),
         dma((two, 2)),

time: 152 us -> 145 us (0.954)
  the two profiles are of different devices: /device:TPU:2 before, /device:TPU:1 now
where the time goes in v5:
time: 145 us
  Pallas kernels  144 us (99%)
    pallas_call x1, Pallas kernels, on_device(): pl.pallas_call(functools.partial(step_kernel, nt_dev, nd), out_shape=[jax...  140 us
    pallas_call x1, Pallas kernels, on_device(): pl.pallas_call(functools.partial(store_kernel, len(shapes)), out_shape=[j...  4.63 us

profile of v5, /device:TPU:1, one launch (start us, length us, event | category | flops | bytes accessed | tf_op | source)
XLA Modules:
  0.0 145.1 jit_solution(3261644722793634369)
XLA Ops:
  0.6 139.6 %shard_map.229 = (f32[512,1024]{1,0:T(8,128)}, f32[512,1024]{1,0:T(8,128)}, f32[2,2,1024]{2,1,0:T(2,128)}, f32[2,2,1024]{2,1,0:T(2,128)}, f32[3,2,128]{2,1,0:T(2...) custom-call(bf16[512,1024]{1,0:T(8,128)(2,1)} %refs_0_.1, ...), custom_call_target="tpu_custom_call" | custom-call | tf_op jit(solution)/shard_map/pallas_call | solution.py:1240
  140.3 4.6 %shard_map.230 = (f32[512,1024]{1,0:T(8,128)}, f32[512,1024]{1,0:T(8,128)}, f32[2,2,1024]{2,1,0:T(2,128)}, f32[2,2,1024]{2,1,0:T(2,128)}, f32[3,2,128]{2,1,0:T(2...) custom-call(f32[512,1024]{1,0:T(8,128)} %get-tuple-element.36.refs_0, ...), custom_call_target="tpu_custom_call" | custom-call | tf_op jit(solution)/shard_map/pallas_call | solution.py:1265

commit v6 on v5

--- a/solution.py
+++ b/solution.py
@@ -1018,20 +1018,19 @@
         small_start()
     with jax.named_scope("gx00"):
         late_x(0)
+    with jax.named_scope("small_second"):
+        small_second()
     with jax.named_scope("forward"):
         forward_at(1)
-    with jax.named_scope("small_second"):
-        small_second()
     with jax.named_scope("late0"):
         late_grads(0)
         grad_core(0, 1)
     with jax.named_scope("forward"):
         forward_at(0)
+    with jax.named_scope("small_third"):
+        small_third()
     with jax.named_scope("gx01"):
         grad_x(0, 1)
-    with jax.named_scope("gz1"):
-        grad_z(1, 0)
-        grad_z(1, 1)
 
     def last_stream(at, z):
         v.x[at, :] = v.x[at, :] + (z + (v.bout[1:2, :] + v.bdown[1:2, :]))
@@ -1042,30 +1041,34 @@
         stream_reduce(0)
     with jax.named_scope("forward0c"):
         ag_forward(0)
-    with jax.named_scope("small_third"):
-        small_third()
+    with jax.named_scope("gz1"):
+        grad_z(1, 0)
+        grad_z(1, 1)
     with jax.named_scope("gather1"):
         ag_pairs(1, 0, ny, last_stream, nothing)
         ag_sent(1)
         store_x.start()
-    with jax.named_scope("gend1"):
-        grad_end(1, 0)
-        grad_end(1, 1)
 
     def last_gradient(at, dx):
         v.g[at, :] = v.g[at, :] + dx
 
     with jax.named_scope("gather3"):
-        ag_pairs(0, 0, ny - 1, last_gradient, nothing)
+        ag_pairs(0, 0, ny // 2, last_gradient, nothing)
     with jax.named_scope("small_fourth"):
         small_fourth()
-    with jax.named_scope("gz0"):
+    with jax.named_scope("gz00"):
         grad_z(0, 0)
+    with jax.named_scope("gather3a"):
+        ag_pairs(0, ny // 2, ny - 1, last_gradient, nothing)
+    with jax.named_scope("gz01"):
         grad_z(0, 1)
     with jax.named_scope("gather3b"):
         ag_pairs(0, ny - 1, ny, last_gradient, nothing)
         store_g.start()
         ag_sent(0)
+    with jax.named_scope("gend1"):
+        grad_end(1, 0)
+        grad_end(1, 1)
     with jax.named_scope("small_end"):
         small_end()
     with jax.named_scope("gend0"):

time: 145 us -> 144 us (level)
  Pallas kernels: 144 us -> 142 us
    pallas_call x1, Pallas kernels: 140 us -> 137 us  [on_device(): pl.pallas_call(functools.partial(step_kernel, nt_dev, nd), out_shape=[jax...]
where the time goes in v6:
time: 144 us; the launch traced here: 143 us
  Pallas kernels  142 us (99%)
    pallas_call x1, Pallas kernels, on_device(): pl.pallas_call(functools.partial(step_kernel, nt_dev, nd), out_shape=[jax...  137 us
    pallas_call x1, Pallas kernels, on_device(): pl.pallas_call(functools.partial(store_kernel, len(shapes)), out_shape=[j...  4.63 us

profile of v6, /device:TPU:1, one launch (start us, length us, event | category | flops | bytes accessed | tf_op | source)
XLA Modules:
  0.0 142.7 jit_solution(3097599592624792087)
XLA Ops:
  0.6 137.3 %shard_map.229 = (f32[512,1024]{1,0:T(8,128)}, f32[512,1024]{1,0:T(8,128)}, f32[2,2,1024]{2,1,0:T(2,128)}, f32[2,2,1024]{2,1,0:T(2,128)}, f32[3,2,128]{2,1,0:T(2...) custom-call(bf16[512,1024]{1,0:T(8,128)(2,1)} %refs_0_.1, ...), custom_call_target="tpu_custom_call" | custom-call | tf_op jit(solution)/shard_map/pallas_call | solution.py:1243
  137.9 4.6 %shard_map.230 = (f32[512,1024]{1,0:T(8,128)}, f32[512,1024]{1,0:T(8,128)}, f32[2,2,1024]{2,1,0:T(2,128)}, f32[2,2,1024]{2,1,0:T(2,128)}, f32[3,2,128]{2,1,0:T(2...) custom-call(f32[512,1024]{1,0:T(8,128)} %get-tuple-element.36.refs_0, ...), custom_call_target="tpu_custom_call" | custom-call | tf_op jit(solution)/shard_map/pallas_call | solution.py:1268

commit v7 on v6

--- a/solution.py
+++ b/solution.py
@@ -22,7 +22,7 @@
 MT = 256
 ST = 32
 TP = 4
-PARTS = 4
+PARTS = 2
 
 
 def nn(a, b):
@@ -989,18 +989,30 @@
         v.g[at, :] = gradient
         v.dz[at, :] = gradient.astype(BF16)
 
-    def next_back(at):
+    def next_do(at):
         do_rows(0, at)
+
+    def next_slope(at):
         dact_rows(0, at)
         back_rows(0, at, 2 * chunk)
 
+    def next_back(at):
+        next_do(at)
+        next_slope(at)
+
     with jax.named_scope("gather2"):
         ag_forward(0)
+        ag_pairs(0, 0, ny // 2, next_gradient, next_back)
+    with jax.named_scope("reduce1"):
         branch_reduce(1)
-        ag_pairs(0, 0, ny, next_gradient, next_back)
+    with jax.named_scope("gather2b"):
+        ag_pairs(0, ny // 2, ny - 1, next_gradient, next_back)
+        ag_pairs(0, ny - 1, ny, next_gradient, next_do)
         ag_sent(0)
     with jax.named_scope("attn_grad0"):
         attention_back(0, lambda: ag_forward(1), lambda: None)
+    with jax.named_scope("slope0"):
+        next_slope(rows_at(at_y(place(ny - 1)), 2 * chunk))
     with jax.named_scope("forward1b"):
 
         @pl.when(zlo == 0)
@@ -1092,28 +1104,14 @@
 
 
 def store_kernel(count, *refs):
-    given, kept, held = refs[:count], refs[count : 2 * count], refs[2 * count : 3 * count]
-    sems = refs[3 * count]
-    parts = []
-    for i in range(count):
-        pieces = PARTS if i < 2 else 1
-        rows = held[i].shape[0] // pieces
-        parts += [(i, slice(j * rows, (j + 1) * rows)) for j in range(pieces)]
-    loads = [
-        pltpu.make_async_copy(given[i].at[at], held[i].at[at], sems.at[0, n])
-        for n, (i, at) in enumerate(parts)
-    ]
-    stores = [
-        pltpu.make_async_copy(held[i].at[at], kept[i].at[at], sems.at[1, n])
-        for n, (i, at) in enumerate(parts)
-    ]
-    for copy in loads:
-        copy.start()
-    for load, store in zip(loads, stores):
-        load.wait()
-        store.start()
-    for copy in stores:
-        copy.wait()
+    given, kept = refs[:count], refs[count:]
+    for i in range(2):
+        kept[i][...] = given[i][...]
+
+    @pl.when(pl.program_id(0) == 0)
+    def _():
+        for i in range(2, count):
+            kept[i][...] = given[i][...]
 
 
 def on_device(nt_dev, nd, *args):
@@ -1268,9 +1266,11 @@
     out = pl.pallas_call(
         functools.partial(store_kernel, len(shapes)),
         out_shape=[jax.ShapeDtypeStruct(s, F32) for s in shapes],
-        in_specs=[away] * len(shapes),
-        out_specs=[away] * len(shapes),
-        scratch_shapes=[vm(s, F32) for s in shapes] + [dma((2, 2 * PARTS + len(shapes)))],
+        grid=(PARTS,),
+        in_specs=[pl.BlockSpec((rows // PARTS, depth), lambda i: (i, 0))] * 2
+        + [here] * (len(shapes) - 2),
+        out_specs=[pl.BlockSpec((rows // PARTS, depth), lambda i: (i, 0))] * 2
+        + [here] * (len(shapes) - 2),
     )(*out)
     x, g, gain, bias, bqkv, bout, b_in_g, bdown, wq, wo, wi, wd = out
     return (

time: 144 us -> 143 us (level)
  no operation moved by 1% of the time
where the time goes in v7:
time: 143 us; the launch traced here: 142 us
  Pallas kernels  142 us (99%)
    pallas_call x1, Pallas kernels, on_device(): pl.pallas_call(functools.partial(step_kernel, nt_dev, nd), out_shape=[jax...  137 us
    pallas_call x1, Pallas kernels, on_device(): pl.pallas_call(functools.partial(store_kernel, len(shapes)), out_shape=[j...  4.34 us

profile of v7, /device:TPU:1, one launch (start us, length us, event | category | flops | bytes accessed | tf_op | source)
XLA Modules:
  0.0 142.3 jit_solution(15317929732724320249)
XLA Ops:
  0.6 137.2 %shard_map.229 = (f32[512,1024]{1,0:T(8,128)}, f32[512,1024]{1,0:T(8,128)}, f32[2,2,1024]{2,1,0:T(2,128)}, f32[2,2,1024]{2,1,0:T(2,128)}, f32[3,2,128]{2,1,0:T(2...) custom-call(bf16[512,1024]{1,0:T(8,128)(2,1)} %refs_0_.1, ...), custom_call_target="tpu_custom_call" | custom-call | tf_op jit(solution)/shard_map/pallas_call | solution.py:1241
  137.8 4.3 %shard_map.230 = (f32[512,1024]{1,0:T(8,128)}, f32[512,1024]{1,0:T(8,128)}, f32[2,2,1024]{2,1,0:T(2,128)}, f32[2,2,1024]{2,1,0:T(2,128)}, f32[3,2,128]{2,1,0:T(2...) custom-call(f32[512,1024]{1,0:T(8,128)} %get-tuple-element.36.refs_0, ...), custom_call_target="tpu_custom_call" | custom-call | tf_op jit(solution)/shard_map/pallas_call | solution.py:1266

commit v8 on v7

--- a/solution.py
+++ b/solution.py
@@ -924,12 +924,13 @@
         for c in load_qkv[1]:
             c.wait()
         ag_forward(0)
-        ag_pairs(0, 0, ny - 1, next_stream, next_both)
-        ag_pairs(0, ny - 1, ny, next_stream, next_qkv)
+        ag_pairs(0, 0, ny // 2, next_stream, next_both)
+        ag_pairs(0, ny // 2, ny, next_stream, next_qkv)
         kv_send(1)
         ag_sent(0)
     with jax.named_scope("ffn1"):
-        next_ffn(rows_at(at_y(place(ny - 1)), 2 * chunk))
+        for k in range(ny // 2, ny):
+            next_ffn(rows_at(at_y(place(k)), 2 * chunk))
     with jax.named_scope("near1"):
         kv_near(1)
         attention(1, 1, 0)
@@ -1006,13 +1007,13 @@
     with jax.named_scope("reduce1"):
         branch_reduce(1)
     with jax.named_scope("gather2b"):
-        ag_pairs(0, ny // 2, ny - 1, next_gradient, next_back)
-        ag_pairs(0, ny - 1, ny, next_gradient, next_do)
+        ag_pairs(0, ny // 2, ny, next_gradient, next_do)
         ag_sent(0)
     with jax.named_scope("attn_grad0"):
         attention_back(0, lambda: ag_forward(1), lambda: None)
     with jax.named_scope("slope0"):
-        next_slope(rows_at(at_y(place(ny - 1)), 2 * chunk))
+        for k in range(ny // 2, ny):
+            next_slope(rows_at(at_y(place(k)), 2 * chunk))
     with jax.named_scope("forward1b"):
 
         @pl.when(zlo == 0)

time: 143 us -> 143 us (level)
  no operation moved by 1% of the time
where the time goes in v8:
time: 143 us; the launch traced here: 142 us
  Pallas kernels  142 us (99%)
    pallas_call x1, Pallas kernels, on_device(): pl.pallas_call(functools.partial(step_kernel, nt_dev, nd), out_shape=[jax...  137 us
    pallas_call x1, Pallas kernels, on_device(): pl.pallas_call(functools.partial(store_kernel, len(shapes)), out_shape=[j...  4.34 us

profile of v8, /device:TPU:1, one launch (start us, length us, event | category | flops | bytes accessed | tf_op | source)
XLA Modules:
  0.0 142.5 jit_solution(8213350471433006122)
XLA Ops:
  0.6 137.3 %shard_map.229 = (f32[512,1024]{1,0:T(8,128)}, f32[512,1024]{1,0:T(8,128)}, f32[2,2,1024]{2,1,0:T(2,128)}, f32[2,2,1024]{2,1,0:T(2,128)}, f32[3,2,128]{2,1,0:T(2...) custom-call(bf16[512,1024]{1,0:T(8,128)(2,1)} %refs_0_.1, ...), custom_call_target="tpu_custom_call" | custom-call | tf_op jit(solution)/shard_map/pallas_call | solution.py:1242
  138.0 4.3 %shard_map.230 = (f32[512,1024]{1,0:T(8,128)}, f32[512,1024]{1,0:T(8,128)}, f32[2,2,1024]{2,1,0:T(2,128)}, f32[2,2,1024]{2,1,0:T(2,128)}, f32[3,2,128]{2,1,0:T(2...) custom-call(f32[512,1024]{1,0:T(8,128)} %get-tuple-element.36.refs_0, ...), custom_call_target="tpu_custom_call" | custom-call | tf_op jit(solution)/shard_map/pallas_call | solution.py:1267
